TPU v7x, 128 devices: a whole 4x4x4 slice. The times are simulated.
128 devices in a mesh: dp: 4 (over z_hi, core), blk: 4 (over y), ulys: 8 (over x, z_lo).
Axes of the slice: x: 4, y: 4, z: 4 (z_hi: 2, z_lo: 2; z = z_hi * 2 + z_lo), core: 2. Of those that a mesh axis runs over, the one named last changes fastest.
Arguments:
- tokens: bfloat16 [16384, 1536], P(('dp', 'blk', 'ulys')), may hold values from -6 to 6
- cotangent: bfloat16 [16384, 1536], P(('dp', 'blk', 'ulys')), may hold values from -6 to 6
- routes: int32 [16384, 8], P(('dp', 'blk', 'ulys')), may hold values from 0 to 39, all different within a row; in each aligned block of 128 rows (0 to 127, 128 to 255, ...) at most 48 rows name the same one
- project_in: float32 [1536, 2560], P(('dp', 'blk', 'ulys')), may hold values from -0.5 to 0.5
- project_out: float32 [1536, 1536], P(None, ('dp', 'blk', 'ulys')), may hold values from -1.5 to 1.5
- router_weight: float32 [1536, 40], P(('dp', 'blk', 'ulys')), may hold values from -0.078125 to 0.078125
- norm_gains: float32 [2, 1536], P(None, ('dp', 'blk', 'ulys')), may hold values from 0.5 to 1.5
- expert_up: float32 [40, 1536, 1024], P('ulys', ('dp', 'blk')), may hold values from -0.15625 to 0.15625
- expert_down: float32 [40, 512, 1536], P('ulys', None, ('dp', 'blk')), may hold values from -6 to 6
- project_in_first: float32 [1536, 2560], P(('dp', 'blk', 'ulys'))
- project_in_second: float32 [1536, 2560], P(('dp', 'blk', 'ulys')), as said below
- project_out_first: float32 [1536, 1536], P(None, ('dp', 'blk', 'ulys'))
- project_out_second: float32 [1536, 1536], P(None, ('dp', 'blk', 'ulys')), as said below
- router_weight_first: float32 [1536, 40], P(('dp', 'blk', 'ulys'))
- router_weight_second: float32 [1536, 40], P(('dp', 'blk', 'ulys')), as said below
- norm_gains_first: float32 [2, 1536], P(None, ('dp', 'blk', 'ulys'))
- norm_gains_second: float32 [2, 1536], P(None, ('dp', 'blk', 'ulys')), as said below
- expert_up_first: float32 [40, 1536, 1024], P('ulys', ('dp', 'blk'))
- expert_up_second: float32 [40, 1536, 1024], P('ulys', ('dp', 'blk')), as said below
- expert_down_first: float32 [40, 512, 1536], P('ulys', None, ('dp', 'blk'))
- expert_down_second: float32 [40, 512, 1536], P('ulys', None, ('dp', 'blk')), as said below
Outputs:
- layer_out: float32 [16384, 1536], P(('dp', 'blk', 'ulys'))
- tokens_grad: float32 [16384, 1536], P(('dp', 'blk', 'ulys'))
- project_in_new: float32 [1536, 2560], P(('dp', 'blk', 'ulys'))
- project_in_first_new: float32 [1536, 2560], P(('dp', 'blk', 'ulys'))
- project_in_second_new: float32 [1536, 2560], P(('dp', 'blk', 'ulys'))
- project_out_new: float32 [1536, 1536], P(None, ('dp', 'blk', 'ulys'))
- project_out_first_new: float32 [1536, 1536], P(None, ('dp', 'blk', 'ulys'))
- project_out_second_new: float32 [1536, 1536], P(None, ('dp', 'blk', 'ulys'))
- router_weight_new: float32 [1536, 40], P(('dp', 'blk', 'ulys'))
- router_weight_first_new: float32 [1536, 40], P(('dp', 'blk', 'ulys'))
- router_weight_second_new: float32 [1536, 40], P(('dp', 'blk', 'ulys'))
- norm_gains_new: float32 [2, 1536], P(None, ('dp', 'blk', 'ulys'))
- norm_gains_first_new: float32 [2, 1536], P(None, ('dp', 'blk', 'ulys'))
- norm_gains_second_new: float32 [2, 1536], P(None, ('dp', 'blk', 'ulys'))
- expert_up_new: float32 [40, 1536, 1024], P('ulys', ('dp', 'blk'))
- expert_up_first_new: float32 [40, 1536, 1024], P('ulys', ('dp', 'blk'))
- expert_up_second_new: float32 [40, 1536, 1024], P('ulys', ('dp', 'blk'))
- expert_down_new: float32 [40, 512, 1536], P('ulys', None, ('dp', 'blk'))
- expert_down_first_new: float32 [40, 512, 1536], P('ulys', None, ('dp', 'blk'))
- expert_down_second_new: float32 [40, 512, 1536], P('ulys', None, ('dp', 'blk'))
Inputs may be any that keep to these rules, and one draw needn't show every extreme that they name: `routes`: each row names 8 different experts. In each aligned block of 128 rows (the rows of one device) no expert is named more than 48 times, a bound that some block reaches. `project_in_second`: Positive. `project_out_second`: Positive. `router_weight_second`: Positive. `norm_gains_second`: Positive. `expert_up_second`: Positive. `expert_down_second`: Positive.
All inputs are finite; a program needn't handle non-finite values.
Results may differ from a plain program's by a relative error of at most 0.024.
Values may be sent and summed in bfloat16 or wider, within the bound.
No kernel may reach another device: no remote copies, remote signals or barrier semaphores. Data moves between devices by JAX's collectives and lax.ppermute only.
A program may use at most 256 MiB of HBM per device.

v0:
```python
import jax
import jax.numpy as jnp
from jax import lax
from jax.sharding import PartitionSpec as P

HQ = 24
HK = 8
HD = 64
F = 512
EXPERTS = 40
TOPK = 8
ADAM_STEP = 10
CAP = 48


highest = lax.Precision.HIGHEST
attention_scale = 0.015625
residual_scale = 0.22
norm_epsilon = 1e-06
rope_base = 10000.0
beta_first = 0.9
beta_second = 0.95
adam_epsilon = 1e-08
weight_decay = 0.1
rate_project_in = 0.2
rate_project_out = 2.0
rate_router = 0.03
rate_gains = 0.5
rate_expert_up = 0.05
rate_expert_down = 2.0


def rope_tables(positions, head_dim):
    half_dim = head_dim // 2
    frequency = rope_base ** (-jnp.arange(half_dim, dtype=jnp.float32) * 2.0 / head_dim)
    angles = positions.astype(jnp.float32)[:, None] * frequency[None, :]
    angles = jnp.concatenate([angles, angles], axis=1)
    return (jnp.cos(angles), jnp.sin(angles))


def rotate(values, cosine_table, sine_table):
    half_dim = values.shape[-1] // 2
    turned = jnp.concatenate([-values[..., half_dim:], values[..., :half_dim]], axis=-1)
    return values * cosine_table + turned * sine_table


def unrotate(values, cosine_table, sine_table):
    half_dim = values.shape[-1] // 2
    scaled = values * sine_table
    turned = jnp.concatenate([scaled[..., half_dim:], -scaled[..., :half_dim]], axis=-1)
    return values * cosine_table + turned


def rms_scale(rows_in):
    return lax.rsqrt(jnp.mean(rows_in * rows_in, axis=1, keepdims=True) + norm_epsilon)


def norm_back(rows_in, scale_in, gain_in, grad_in):
    weighted = grad_in * gain_in
    inner_sum = jnp.mean(weighted * rows_in, axis=1, keepdims=True)
    return scale_in * weighted - rows_in * (scale_in * scale_in * scale_in) * inner_sum


def slot_table(route_rows, expert_count, capacity):
    flat_routes = route_rows.reshape(-1)
    onehot = (flat_routes[:, None] == jnp.arange(expert_count, dtype=jnp.int32)[None, :]).astype(
        jnp.int32
    )
    before = jnp.cumsum(onehot, axis=0) - onehot
    ranks = jnp.sum(before * onehot, axis=1)
    return flat_routes * capacity + ranks


def adam_update(weight, first_moment, second, gradient, step_rate):
    first_new = beta_first * first_moment + (1.0 - beta_first) * gradient
    second_new = beta_second * second + (1.0 - beta_second) * gradient * gradient
    first_hat = first_new / (1.0 - beta_first**ADAM_STEP)
    second_hat = second_new / (1.0 - beta_second**ADAM_STEP)
    weight_new = weight - step_rate * (
        first_hat / (jnp.sqrt(second_hat) + adam_epsilon) + weight_decay * weight
    )
    return (weight_new, first_new, second_new)


def dispatch(buffer):
    return lax.all_to_all(buffer, "ulys", split_axis=0, concat_axis=1, tiled=True)


def combine(buffer):
    return lax.all_to_all(buffer, "ulys", split_axis=1, concat_axis=0, tiled=True)


def shards(
    tokens,
    cotangent,
    routes,
    project_in,
    project_out,
    router_weight,
    norm_gains,
    expert_up,
    expert_down,
    project_in_first,
    project_in_second,
    project_out_first,
    project_out_second,
    router_weight_first,
    router_weight_second,
    norm_gains_first,
    norm_gains_second,
    expert_up_first,
    expert_up_second,
    expert_down_first,
    expert_down_second,
):
    token_rows = tokens.shape[0]
    model_width = tokens.shape[1]
    ulys_count = lax.axis_size("ulys")
    blk_count = lax.axis_size("blk")
    group_size = HQ // HK
    local_heads = HQ // ulys_count
    local_kv = HK // ulys_count
    query_width = HQ * HD
    kv_width = HK * HD
    local_span = token_rows * ulys_count
    key_span = local_span * blk_count
    in_full, out_full, router_full, gains_full = (
        lax.all_gather(project_in.astype(jnp.bfloat16), ("dp", "blk", "ulys"), axis=0, tiled=True),
        lax.all_gather(project_out.astype(jnp.bfloat16), ("dp", "blk", "ulys"), axis=1, tiled=True),
        lax.all_gather(
            router_weight.astype(jnp.bfloat16), ("dp", "blk", "ulys"), axis=0, tiled=True
        ),
        lax.all_gather(norm_gains.astype(jnp.bfloat16), ("dp", "blk", "ulys"), axis=1, tiled=True),
    )
    gain_attn = gains_full[0].astype(jnp.float32)
    gain_ffn = gains_full[1].astype(jnp.float32)
    xfloat = tokens.astype(jnp.float32)
    scale_attn = rms_scale(xfloat)
    normed = (xfloat * scale_attn * gain_attn).astype(jnp.bfloat16)
    mixed_rows = jnp.dot(normed, in_full, preferred_element_type=jnp.float32)
    position = (
        lax.axis_index("blk") * ulys_count + lax.axis_index("ulys")
    ) * token_rows + jnp.arange(token_rows, dtype=jnp.int32)
    cosine_table, sine_table = rope_tables(position, HD)
    cosine_table = cosine_table[:, None, :]
    sine_table = sine_table[:, None, :]
    queries = rotate(
        mixed_rows[:, :query_width].reshape(token_rows, HQ, HD), cosine_table, sine_table
    )
    queries = queries.reshape(token_rows, query_width).astype(jnp.bfloat16)
    key_rows = rotate(
        mixed_rows[:, query_width : query_width + kv_width].reshape(token_rows, HK, HD),
        cosine_table,
        sine_table,
    )
    key_rows = key_rows.reshape(token_rows, kv_width).astype(jnp.bfloat16)
    values = mixed_rows[:, query_width + kv_width :].astype(jnp.bfloat16)
    head_queries, head_keys, head_values = (
        lax.all_to_all(queries, "ulys", split_axis=1, concat_axis=0, tiled=True),
        lax.all_to_all(key_rows, "ulys", split_axis=1, concat_axis=0, tiled=True),
        lax.all_to_all(values, "ulys", split_axis=1, concat_axis=0, tiled=True),
    )
    keys_all, values_all = (
        lax.all_gather(head_keys, "blk", axis=0, tiled=True),
        lax.all_gather(head_values, "blk", axis=0, tiled=True),
    )
    block_rows = min(512, local_span)
    block_count = local_span // block_rows
    query_base = lax.axis_index("blk") * local_span
    key_positions = jnp.arange(key_span, dtype=jnp.int32)
    keys_grid = keys_all.reshape(key_span, local_kv, HD)
    values_grid = values_all.reshape(key_span, local_kv, HD)
    query_grid = head_queries.reshape(block_count, block_rows, local_kv, group_size, HD)
    offsets = jnp.arange(block_count, dtype=jnp.int32) * block_rows

    def scores_of(query_block, offset):
        scores = (
            jnp.einsum("qhgd,khd->hgqk", query_block, keys_grid, preferred_element_type=jnp.float32)
            * attention_scale
        )
        query_positions = query_base + offset + jnp.arange(block_rows, dtype=jnp.int32)
        allowed = key_positions[None, :] <= query_positions[:, None]
        return jnp.where(allowed, scores, -jnp.inf)

    def attend(pair_in):
        query_block, offset = pair_in
        scores = scores_of(query_block, offset)
        row_peak = jnp.max(scores, axis=-1, keepdims=True)
        exponent = jnp.exp(scores - row_peak)
        row_total = jnp.sum(exponent, axis=-1, keepdims=True)
        weights = (exponent / row_total).astype(jnp.bfloat16)
        result = jnp.einsum(
            "hgqk,khd->qhgd", weights, values_grid, preferred_element_type=jnp.float32
        )
        return (result.astype(jnp.bfloat16), (row_peak + jnp.log(row_total))[..., 0])

    head_out, log_totals = lax.map(attend, (query_grid, offsets))
    attended = lax.all_to_all(
        head_out.reshape(local_span, local_heads * HD),
        "ulys",
        split_axis=0,
        concat_axis=1,
        tiled=True,
    )
    branch = jnp.dot(attended, out_full, preferred_element_type=jnp.float32)
    hidden = xfloat + residual_scale * branch
    scale_ffn = rms_scale(hidden)
    normed_ffn = (hidden * scale_ffn * gain_ffn).astype(jnp.bfloat16)
    logits = jnp.dot(normed_ffn, router_full, preferred_element_type=jnp.float32)
    chosen = jnp.take_along_axis(logits, routes, axis=1)
    gate_weights = jax.nn.softmax(chosen, axis=1)
    slot_of = slot_table(routes, EXPERTS, CAP)
    token_of = jnp.arange(token_rows * TOPK, dtype=jnp.int32) // TOPK
    source = jnp.zeros((EXPERTS * CAP,), jnp.int32).at[slot_of].set(token_of)
    filled = jnp.zeros((EXPERTS * CAP,), jnp.bool_).at[slot_of].set(True)
    outgoing = jnp.where(filled[:, None], normed_ffn[source], jnp.zeros((), jnp.bfloat16))
    arriving = dispatch(outgoing.reshape(EXPERTS, CAP, model_width))
    up_full, down_full = (
        lax.all_gather(expert_up.astype(jnp.bfloat16), ("dp", "blk"), axis=1, tiled=True),
        lax.all_gather(expert_down.astype(jnp.bfloat16), ("dp", "blk"), axis=2, tiled=True),
    )
    both_parts = jnp.einsum("erd,edf->erf", arriving, up_full, preferred_element_type=jnp.float32)
    gate_part = both_parts[..., :F]
    up_part = both_parts[..., F:]
    silu_gate = jax.nn.silu(gate_part)
    activated = (silu_gate * up_part).astype(jnp.bfloat16)
    produced = jnp.einsum(
        "erf,efd->erd", activated, down_full, preferred_element_type=jnp.float32
    ).astype(jnp.bfloat16)
    returned = combine(produced).reshape(EXPERTS * CAP, model_width)
    picked = returned[slot_of].reshape(token_rows, TOPK, model_width).astype(jnp.float32)
    mixture = jnp.sum(gate_weights[:, :, None] * picked, axis=1)
    layer_out = hidden + residual_scale * mixture
    upstream = cotangent.astype(jnp.float32)
    moe_grad = residual_scale * upstream
    gate_grad = jnp.sum(picked * moe_grad[:, None, :], axis=2)
    chosen_grad = gate_weights * (
        gate_grad - jnp.sum(gate_weights * gate_grad, axis=1, keepdims=True)
    )
    route_hits = (routes[:, :, None] == jnp.arange(EXPERTS, dtype=jnp.int32)[None, None, :]).astype(
        jnp.float32
    )
    logit_grad = jnp.sum(route_hits * chosen_grad[:, :, None], axis=1)
    slot_grad = (
        (gate_weights[:, :, None] * moe_grad[:, None, :])
        .astype(jnp.bfloat16)
        .reshape(token_rows * TOPK, model_width)
    )
    sending = jnp.zeros((EXPERTS * CAP, model_width), jnp.bfloat16).at[slot_of].set(slot_grad)
    produced_grad = dispatch(sending.reshape(EXPERTS, CAP, model_width))
    up_back, down_back = (
        lax.all_gather(expert_up.astype(jnp.bfloat16), ("dp", "blk"), axis=1, tiled=True),
        lax.all_gather(expert_down.astype(jnp.bfloat16), ("dp", "blk"), axis=2, tiled=True),
    )
    activated_grad = jnp.einsum(
        "erd,efd->erf", produced_grad, down_back, preferred_element_type=jnp.float32
    )
    sigmoid_gate = jax.nn.sigmoid(gate_part)
    gate_slope = sigmoid_gate * (1.0 + gate_part * (1.0 - sigmoid_gate))
    both_grad = jnp.concatenate(
        [activated_grad * up_part * gate_slope, activated_grad * silu_gate], axis=-1
    ).astype(jnp.bfloat16)
    arriving_grad = jnp.einsum(
        "erf,edf->erd", both_grad, up_back, preferred_element_type=jnp.float32
    ).astype(jnp.bfloat16)
    returned_grad = combine(arriving_grad).reshape(EXPERTS * CAP, model_width)
    router_float = router_full.astype(jnp.float32)
    ffn_grad = jnp.sum(
        returned_grad[slot_of].reshape(token_rows, TOPK, model_width).astype(jnp.float32), axis=1
    )
    ffn_grad = ffn_grad + jnp.dot(logit_grad, router_float.T, precision=highest)
    router_grad = jnp.dot(normed_ffn.astype(jnp.float32).T, logit_grad, precision=highest)
    gain_ffn_grad = jnp.sum(ffn_grad * hidden * scale_ffn, axis=0)
    hidden_grad = upstream + norm_back(hidden, scale_ffn, gain_ffn, ffn_grad)
    branch_grad = (residual_scale * hidden_grad).astype(jnp.bfloat16)
    out_grad = jnp.einsum("tq,td->qd", attended, branch_grad, preferred_element_type=jnp.float32)
    attended_grad = jnp.einsum(
        "td,qd->tq", branch_grad, out_full, preferred_element_type=jnp.float32
    ).astype(jnp.bfloat16)
    head_grad = lax.all_to_all(attended_grad, "ulys", split_axis=1, concat_axis=0, tiled=True)
    grad_grid = head_grad.reshape(block_count, block_rows, local_kv, group_size, HD)

    def attend_back(carried, quad):
        keys_acc, values_acc = carried
        query_block, grad_block, offset, log_total = quad
        scores = scores_of(query_block, offset)
        probs = jnp.exp(scores - log_total[..., None])
        weights = probs.astype(jnp.bfloat16)
        prob_grad = jnp.einsum(
            "qhgd,khd->hgqk", grad_block, values_grid, preferred_element_type=jnp.float32
        )
        inner_sum = jnp.sum(probs * prob_grad, axis=-1, keepdims=True)
        score_grad = (probs * (prob_grad - inner_sum)).astype(jnp.bfloat16)
        query_grad = (
            jnp.einsum("hgqk,khd->qhgd", score_grad, keys_grid, preferred_element_type=jnp.float32)
            * attention_scale
        )
        keys_acc = (
            keys_acc
            + jnp.einsum(
                "hgqk,qhgd->khd", score_grad, query_block, preferred_element_type=jnp.float32
            )
            * attention_scale
        )
        values_acc = values_acc + jnp.einsum(
            "hgqk,qhgd->khd", weights, grad_block, preferred_element_type=jnp.float32
        )
        return ((keys_acc, values_acc), query_grad.astype(jnp.bfloat16))

    zero_keys = jnp.zeros((key_span, local_kv, HD), jnp.float32)
    (keys_acc, values_acc), query_grads = lax.scan(
        attend_back, (zero_keys, zero_keys), (query_grid, grad_grid, offsets, log_totals)
    )
    key_sum, value_sum = (
        lax.psum_scatter(
            keys_acc.reshape(key_span, local_kv * HD).astype(jnp.bfloat16),
            "blk",
            scatter_dimension=0,
            tiled=True,
        ).astype(jnp.float32),
        lax.psum_scatter(
            values_acc.reshape(key_span, local_kv * HD).astype(jnp.bfloat16),
            "blk",
            scatter_dimension=0,
            tiled=True,
        ).astype(jnp.float32),
    )
    query_tok, key_tok, value_tok = (
        lax.all_to_all(
            query_grads.reshape(local_span, local_heads * HD),
            "ulys",
            split_axis=0,
            concat_axis=1,
            tiled=True,
        ),
        lax.all_to_all(
            key_sum.astype(jnp.bfloat16), "ulys", split_axis=0, concat_axis=1, tiled=True
        ),
        lax.all_to_all(
            value_sum.astype(jnp.bfloat16), "ulys", split_axis=0, concat_axis=1, tiled=True
        ),
    )
    query_pre = unrotate(
        query_tok.astype(jnp.float32).reshape(token_rows, HQ, HD), cosine_table, sine_table
    )
    key_pre = unrotate(
        key_tok.astype(jnp.float32).reshape(token_rows, HK, HD), cosine_table, sine_table
    )
    mixed_grad = jnp.concatenate(
        [
            query_pre.reshape(token_rows, query_width),
            key_pre.reshape(token_rows, kv_width),
            value_tok.astype(jnp.float32),
        ],
        axis=1,
    ).astype(jnp.bfloat16)
    in_grad = jnp.einsum("td,tc->dc", normed, mixed_grad, preferred_element_type=jnp.float32)
    normed_grad = jnp.einsum("tc,dc->td", mixed_grad, in_full, preferred_element_type=jnp.float32)
    gain_attn_grad = jnp.sum(normed_grad * xfloat * scale_attn, axis=0)
    tokens_grad = hidden_grad + norm_back(xfloat, scale_attn, gain_attn, normed_grad)
    gains_grad = jnp.stack([gain_attn_grad, gain_ffn_grad])
    in_sum, out_sum, router_sum, gains_sum = (
        lax.psum_scatter(in_grad, ("dp", "blk", "ulys"), scatter_dimension=0, tiled=True),
        lax.psum_scatter(out_grad, ("dp", "blk", "ulys"), scatter_dimension=1, tiled=True),
        lax.psum_scatter(router_grad, ("dp", "blk", "ulys"), scatter_dimension=0, tiled=True),
        lax.psum_scatter(gains_grad, ("dp", "blk", "ulys"), scatter_dimension=1, tiled=True),
    )
    up_grad = jnp.einsum("erd,erf->edf", arriving, both_grad, preferred_element_type=jnp.float32)
    down_grad = jnp.einsum(
        "erf,erd->efd", activated, produced_grad, preferred_element_type=jnp.float32
    )
    up_sum, down_sum = (
        lax.psum_scatter(
            up_grad.astype(jnp.bfloat16), ("dp", "blk"), scatter_dimension=1, tiled=True
        ).astype(jnp.float32),
        lax.psum_scatter(
            down_grad.astype(jnp.bfloat16), ("dp", "blk"), scatter_dimension=2, tiled=True
        ).astype(jnp.float32),
    )
    in_new, in_first, in_second = adam_update(
        project_in, project_in_first, project_in_second, in_sum, rate_project_in
    )
    out_new, out_first, out_second = adam_update(
        project_out, project_out_first, project_out_second, out_sum, rate_project_out
    )
    router_new, router_first, router_second = adam_update(
        router_weight, router_weight_first, router_weight_second, router_sum, rate_router
    )
    gains_new, gains_first, gains_second = adam_update(
        norm_gains, norm_gains_first, norm_gains_second, gains_sum, rate_gains
    )
    up_new, up_first, up_second = adam_update(
        expert_up, expert_up_first, expert_up_second, up_sum, rate_expert_up
    )
    down_new, down_first, down_second = adam_update(
        expert_down, expert_down_first, expert_down_second, down_sum, rate_expert_down
    )
    return (
        layer_out,
        tokens_grad,
        in_new,
        in_first,
        in_second,
        out_new,
        out_first,
        out_second,
        router_new,
        router_first,
        router_second,
        gains_new,
        gains_first,
        gains_second,
        up_new,
        up_first,
        up_second,
        down_new,
        down_first,
        down_second,
    )


def solution(mesh):
    in_specs = (
        P(("dp", "blk", "ulys"), None),
        P(("dp", "blk", "ulys"), None),
        P(("dp", "blk", "ulys"), None),
        P(("dp", "blk", "ulys"), None),
        P(None, ("dp", "blk", "ulys")),
        P(("dp", "blk", "ulys"), None),
        P(None, ("dp", "blk", "ulys")),
        P("ulys", ("dp", "blk"), None),
        P("ulys", None, ("dp", "blk")),
        P(("dp", "blk", "ulys"), None),
        P(("dp", "blk", "ulys"), None),
        P(None, ("dp", "blk", "ulys")),
        P(None, ("dp", "blk", "ulys")),
        P(("dp", "blk", "ulys"), None),
        P(("dp", "blk", "ulys"), None),
        P(None, ("dp", "blk", "ulys")),
        P(None, ("dp", "blk", "ulys")),
        P("ulys", ("dp", "blk"), None),
        P("ulys", ("dp", "blk"), None),
        P("ulys", None, ("dp", "blk")),
        P("ulys", None, ("dp", "blk")),
    )
    out_specs = (
        P(("dp", "blk", "ulys"), None),
        P(("dp", "blk", "ulys"), None),
        P(("dp", "blk", "ulys"), None),
        P(("dp", "blk", "ulys"), None),
        P(("dp", "blk", "ulys"), None),
        P(None, ("dp", "blk", "ulys")),
        P(None, ("dp", "blk", "ulys")),
        P(None, ("dp", "blk", "ulys")),
        P(("dp", "blk", "ulys"), None),
        P(("dp", "blk", "ulys"), None),
        P(("dp", "blk", "ulys"), None),
        P(None, ("dp", "blk", "ulys")),
        P(None, ("dp", "blk", "ulys")),
        P(None, ("dp", "blk", "ulys")),
        P("ulys", ("dp", "blk"), None),
        P("ulys", ("dp", "blk"), None),
        P("ulys", ("dp", "blk"), None),
        P("ulys", None, ("dp", "blk")),
        P("ulys", None, ("dp", "blk")),
        P("ulys", None, ("dp", "blk")),
    )
    return jax.shard_map(shards, mesh=mesh, in_specs=in_specs, out_specs=out_specs, check_vma=False)
```

profile of v0, /device:TPU:0, one launch (start us, length us, event | category | flops | bytes accessed | tf_op | source)
XLA Modules:
  0.0 3028.6 jit_solution(15935652092493261328)
XLA Ops:
  19.4 316.5 %all-gather = bf16[128,12,2]{1,2,0:T(2,128)(2,1)S(1)} all-gather(bf16[1,12,2]{1,2,0:T(2,128)(2,1)S(1)} %convert_bitcast_fusion.5), channel_id=1, replica_groups=mesh['dp'=4,'blk'=4,'ulys'=8] {'dp','blk','ulys'}, dimensions={0}, use_global_device_ids=true | all-gather | bytes 6192 | tf_op jit(solution)/shard_map/all_gather | solution.py:133
  349.3 312.8 %all-gather.3 = bf16[128,12,40]{2,1,0:T(8,128)(2,1)S(1)} all-gather(bf16[1,12,40]{2,1,0:T(8,128)(2,1)S(1)} %convert_bitcast_fusion.4), channel_id=1, replica_groups=mesh['dp'=4,'blk'=4,'ulys'=8] {'dp','blk','ulys'}, dimensions={0}, use_global_device_ids=true | all-gather | bytes 123840 | tf_op jit(solution)/shard_map/all_gather | solution.py:130
  665.2 12.9 reshape.549
  709.8 13.8 all_gather.28
  723.6 12.9 all_gather.29
  737.1 76.8 %while.28 = (s32[]{:T(128)}, bf16[2,512,1,3,64]{1,4,3,2,0:T(8,128)(2,1)S(1)}, f32[2,1,3,512]{3,2,1,0:T(4,128)S(1)}, s32[2]{0:T(128)S(1)}, s32[]{:T(128)}, /*inde...) while((s32[]{:T(128)}, ...), condition=%wide.region_4.5_spmd.clone, body=%wide.region_1.4_spmd.clone.sunk | while | flops 1688304640 | bytes 85391504 | solution.py:197
  751.2 12.2 fusion.197
  763.4 12.4 fusion.198
  880.8 43.9 %all-to-all-done.6 = bf16[40,48,1536]{2,1,0:T(8,128)(2,1)} async-done(((bf16[40,48,1536]{2,1,0:T(8,128)(2,1)}), bf16[40,48,1536]{2,1,0:T(8,128)(2,1)}, u32[]{:S(2)}, u32[]{:S(2)}) %all-to-all-start.6) | async-done | bytes 5898272 | tf_op jit(solution)/shard_map/all_to_all | solution.py:86
  935.7 38.2 %all-to-all-done.4 = bf16[40,48,1536]{2,1,0:T(8,128)(2,1)} async-done(((bf16[40,48,1536]{2,1,0:T(8,128)(2,1)}), bf16[40,48,1536]{2,1,0:T(8,128)(2,1)}, u32[]{:S(2)}, u32[]{:S(2)}) %all-to-all-start.4) | async-done | bytes 5898272 | tf_op jit(solution)/shard_map/all_to_all | solution.py:86
  979.5 13.4 fusion.145
  992.9 14.1 multiply_convert_fusion.1
  1007.0 12.8 convolution_convert_fusion.2
  1054.4 89.8 %all-to-all-done.7 = bf16[5,384,1536]{2,0,1:T(8,128)(2,1)} async-done(((bf16[5,384,1536]{2,0,1:T(8,128)(2,1)}), bf16[5,384,1536]{2,0,1:T(8,128)(2,1)}, u32[]{:S(2)}, u32[]{:S(2)}) %all-to-all-start.7) | async-done | bytes 5898272 | tf_op jit(solution)/shard_map/all_to_all | solution.py:90
  1173.9 46.8 %all-to-all-done.5 = bf16[5,384,1536]{2,0,1:T(8,128)(2,1)} async-done(((bf16[5,384,1536]{2,0,1:T(8,128)(2,1)}), bf16[5,384,1536]{2,0,1:T(8,128)(2,1)}, u32[]{:S(2)}, u32[]{:S(2)}) %all-to-all-start.5) | async-done | bytes 5898272 | tf_op jit(solution)/shard_map/all_to_all | solution.py:90
  1265.1 139.1 %while.29 = (s32[]{:T(128)}, f32[4096,1,64]{0,2,1:T(8,128)}, f32[4096,1,64]{0,2,1:T(8,128)}, bf16[2,512,1,3,64]{1,4,3,2,0:T(8,128)(2,1)}, bf16[2,512,1,3,64]{1,4...) while((s32[]{:T(128)}, f32[4096,1,64]{0,2,1:T(8,128)}, ...), condition=%wide.region_22.23_spmd.clone, body=%wide.region_20.22_spmd.clone.sunk | while | flops 4124507136 | bytes 217039184 | solution.py:311
  1279.8 12.7 fusion.211
  1292.5 16.9 fusion.208
  1309.4 17.5 fusion.209
  1348.9 13.0 fusion.211
  1362.0 16.9 fusion.208
  1378.9 17.5 fusion.209
  1420.9 14.6 convolution_convert_fusion
  1479.2 831.4 %fusion.133 = (f32[16,2560]{1,0:T(8,128)S(1)}, f32[1536,16]{0,1:T(8,128)S(1)}, f32[16,40]{1,0:T(8,128)S(1)}) fusion(f32[1536,2560]{1,0:T(8,128)} %fusion.95, f32[1536,1536]{0,1:T(8,128)} %fusion.106, f32[1536,40]{1,0:T(8,128)S(1)} %fusion.146), kind=kCustom, calls=%all-reduce-scatter.3 | all-reduce-scatter fusion | flops 8470529 | bytes 25676288
  2330.0 14.3 collective-permute-start.93
  2576.6 19.1 collective-permute-start.59
  2595.8 16.6 collective-permute-start.58
  2633.2 12.3 collective-permute-start.52
  2773.2 62.6 %all-reduce.3 = f32[2,1536]{1,0:T(2,128)S(1)} all-reduce(f32[2,1536]{1,0:T(2,128)S(1)} %pad_maximum_fusion.8), channel_id=7, replica_groups=mesh['dp'=4,'blk'=4,'ulys'=8] {'dp','blk','ulys'}, use_global_device_ids=true, to_apply=%region_31.32.clone | all-reduce | flops 3072 | bytes 24576
  2856.5 21.2 concatenate.46
  2899.5 31.7 %concatenate.45 = f32[1536,524]{0,1:T(8,128)S(1)} concatenate(f32[1536,12]{0,1:T(8,128)} %copy-done.71, f32[1536,16]{0,1:T(8,128)} %copy-done.68, f32[1536,16]{0,1:T(8,128)} %copy-done.69, f32[1536,16]{0,1:T(8,128)} %copy-done.70, f32[1536,16]{0,1:T(8,128)} %copy-done.72, f32[1536,16]{0,1:T(8,128)} %copy-done.73, f32[1536,16]{0,1:T(8,128)} %copy-done.74, f32[1536,16]{0,1:T(8,128)} %copy-done.75, ...), dimensions={1} | concatenate | bytes 6438912
  2952.1 57.3 %concatenate.44 = f32[524,2560]{1,0:T(8,128)} concatenate(f32[12,2560]{1,0:T(8,128)} %copy-done.41, f32[16,2560]{1,0:T(8,128)} %copy-done.40, f32[16,2560]{1,0:T(8,128)} %copy-done.42, f32[16,2560]{1,0:T(8,128)} %copy-done.43, f32[16,2560]{1,0:T(8,128)} %copy-done.44, f32[16,2560]{1,0:T(8,128)} %copy-done.45, f32[16,2560]{1,0:T(8,128)} %copy-done.46, f32[16,2560]{1,0:T(8,128)} %copy-done.47, ...), dimensions={0} | concatenate | bytes 10731520
  (686 shorter events, 879.3 us)
Async XLA Ops:
  7.2 657.9 %all-gather.13.cloned.1.call-start = ((), (), s32[]{:S(2)}) async-start(), calls=%async_computation.22 | async-start | bytes 10567680 | tf_op jit(solution)/shard_map/all_gather | solution.py:128
  8.9 812.3 %all-gather.15.cloned.1.call-start = ((), (), s32[]{:S(2)}) async-start(), calls=%async_computation.23 | async-start | bytes 6340608 | tf_op jit(solution)/shard_map/all_gather | solution.py:129
  10.5 969.0 %all-gather.9.cloned.1.call-start = ((), (), s32[]{:S(2)}) async-start(), calls=%async_computation.16 | async-start | bytes 16711680 | tf_op jit(solution)/shard_map/all_gather | solution.py:219
  13.3 979.7 %all-gather.11.cloned.1.call-start = ((), (), s32[]{:S(2)}) async-start(), calls=%async_computation.17 | async-start | bytes 8355840 | tf_op jit(solution)/shard_map/all_gather | solution.py:220
  852.4 72.3 %all-to-all-start.6 = ((bf16[40,48,1536]{2,1,0:T(8,128)(2,1)}), bf16[40,48,1536]{2,1,0:T(8,128)(2,1)}, u32[]{:S(2)}, u32[]{:S(2)}) async-start(bf16[40,48,1536]{2,1,0:T(8,128)(2,1)} %bitcast.406), calls=%async_computation.6 | async-start | bytes 11796480 | tf_op jit(solution)/shard_map/all_to_all | solution.py:86
  924.7 49.2 %all-to-all-start.4 = ((bf16[40,48,1536]{2,1,0:T(8,128)(2,1)}), bf16[40,48,1536]{2,1,0:T(8,128)(2,1)}, u32[]{:S(2)}, u32[]{:S(2)}) async-start(bf16[40,48,1536]{2,1,0:T(8,128)(2,1)} %broadcast_select_fusion), calls=%async_computation.4 | async-start | bytes 11796480 | tf_op jit(solution)/shard_map/all_to_all | solution.py:86
  1029.8 114.4 %all-to-all-start.7 = ((bf16[5,384,1536]{2,0,1:T(8,128)(2,1)}), bf16[5,384,1536]{2,0,1:T(8,128)(2,1)}, u32[]{:S(2)}, u32[]{:S(2)}) async-start(bf16[5,384,1536]{2,0,1:T(8,128)(2,1)} %copy.288), calls=%async_computation.7 | async-start | bytes 18874368 | tf_op jit(solution)/shard_map/all_to_all | solution.py:90
  1144.2 76.5 %all-to-all-start.5 = ((bf16[5,384,1536]{2,0,1:T(8,128)(2,1)}), bf16[5,384,1536]{2,0,1:T(8,128)(2,1)}, u32[]{:S(2)}, u32[]{:S(2)}) async-start(bf16[5,384,1536]{2,0,1:T(8,128)(2,1)} %copy.284), calls=%async_computation.5 | async-start | bytes 18874368 | tf_op jit(solution)/shard_map/all_to_all | solution.py:90
  1255.7 193.6 %reduce-scatter.12.cloned.1.call-start = ((), (), s32[]{:S(2)}) async-start(), calls=%async_computation.18 | async-start | bytes 655360 | tf_op jit(solution)/shard_map/reduce_scatter | solution.py:315
  1406.4 48.7 %reduce-scatter.14.cloned.1.call-start = ((), (), s32[]{:S(2)}) async-start(), calls=%async_computation.19 | async-start | bytes 655360 | tf_op jit(solution)/shard_map/reduce_scatter | solution.py:321
  1408.5 1603.0 %reduce-scatter.18.cloned.1.call-start = ((), (), s32[]{:S(2)}) async-start(), calls=%async_computation.21 | async-start | bytes 8355840 | tf_op jit(solution)/shard_map/reduce_scatter | solution.py:376
  1419.4 1595.9 %reduce-scatter.16.cloned.1.call-start = ((), (), s32[]{:S(2)}) async-start(), calls=%async_computation.20 | async-start | bytes 16711680 | tf_op jit(solution)/shard_map/reduce_scatter | solution.py:373
  2310.6 301.7 %collective-permute-start.62 = (f32[1536,16]{0,1:T(8,128)S(1)}, f32[1536,16]{0,1:T(8,128)S(1)}, u32[]{:S(2)}, u32[]{:S(2)}) collective-permute-start(f32[1536,16]{0,1:T(8,128)S(1)} %get-tuple-element.357), channel_id=1, source_target_pairs={{0,31},{1,32},{2,33},{3,34},{4,35},{5,36},{6,37},{7,38},{8,39},{9,... | collective-permute-start | bytes 294920
  2313.9 305.2 %collective-permute-start.61 = (f32[1536,16]{0,1:T(8,128)S(1)}, f32[1536,16]{0,1:T(8,128)S(1)}, u32[]{:S(2)}, u32[]{:S(2)}) collective-permute-start(f32[1536,16]{0,1:T(8,128)S(1)} %get-tuple-element.357), channel_id=1, source_target_pairs={{0,30},{1,31},{2,32},{3,33},{4,34},{5,35},{6,36},{7,37},{8,38},{9,... | collective-permute-start | bytes 294920
  2315.2 309.5 %collective-permute-start.60 = (f32[1536,16]{0,1:T(8,128)S(1)}, f32[1536,16]{0,1:T(8,128)S(1)}, u32[]{:S(2)}, u32[]{:S(2)}) collective-permute-start(f32[1536,16]{0,1:T(8,128)S(1)} %get-tuple-element.357), channel_id=1, source_target_pairs={{0,29},{1,30},{2,31},{3,32},{4,33},{5,34},{6,35},{7,36},{8,37},{9,... | collective-permute-start | bytes 294920
  2354.5 241.2 %collective-permute-start.63 = (f32[1536,12]{0,1:T(8,128)S(1)}, f32[1536,12]{0,1:T(8,128)S(1)}, u32[]{:S(2)}, u32[]{:S(2)}) collective-permute-start(f32[1536,12]{0,1:T(8,128)S(1)} %slice.95), channel_id=1, source_target_pairs={{0,32},{1,33},{2,34},{3,35},{4,36},{5,37},{6,38},{7,39},{8,40},{9,... | collective-permute-start | bytes 221192
  2576.6 49.4 %collective-permute-start.59 = (f32[1536,16]{0,1:T(8,128)S(1)}, f32[1536,16]{0,1:T(8,128)S(1)}, u32[]{:S(2)}, u32[]{:S(2)}) collective-permute-start(f32[1536,16]{0,1:T(8,128)S(1)} %get-tuple-element.357), channel_id=1, source_target_pairs={{0,28},{1,29},{2,30},{3,31},{4,32},{5,33},{6,34},{7,35},{8,36},{9,... | collective-permute-start | bytes 294920
  2748.7 87.1 %collective-permute-start.19 = (f32[16,2560]{1,0:T(8,128)S(1)}, f32[16,2560]{1,0:T(8,128)S(1)}, u32[]{:S(2)}, u32[]{:S(2)}) collective-permute-start(f32[16,2560]{1,0:T(8,128)S(1)} %get-tuple-element.356), channel_id=1, source_target_pairs={{0,20},{1,21},{2,22},{3,23},{4,24},{5,25},{6,26},{7,27},{8,28},{9,... | collective-permute-start | bytes 491528
  2750.1 88.2 %collective-permute-start.18 = (f32[16,2560]{1,0:T(8,128)S(1)}, f32[16,2560]{1,0:T(8,128)S(1)}, u32[]{:S(2)}, u32[]{:S(2)}) collective-permute-start(f32[16,2560]{1,0:T(8,128)S(1)} %get-tuple-element.356), channel_id=1, source_target_pairs={{0,19},{1,20},{2,21},{3,22},{4,23},{5,24},{6,25},{7,26},{8,27},{9,... | collective-permute-start | bytes 491528
  2752.2 90.9 %collective-permute-start.17 = (f32[16,2560]{1,0:T(8,128)S(1)}, f32[16,2560]{1,0:T(8,128)S(1)}, u32[]{:S(2)}, u32[]{:S(2)}) collective-permute-start(f32[16,2560]{1,0:T(8,128)S(1)} %get-tuple-element.356), channel_id=1, source_target_pairs={{0,18},{1,19},{2,20},{3,21},{4,22},{5,23},{6,24},{7,25},{8,26},{9,... | collective-permute-start | bytes 491528
  2757.2 89.5 %collective-permute-start.16 = (f32[16,2560]{1,0:T(8,128)S(1)}, f32[16,2560]{1,0:T(8,128)S(1)}, u32[]{:S(2)}, u32[]{:S(2)}) collective-permute-start(f32[16,2560]{1,0:T(8,128)S(1)} %get-tuple-element.356), channel_id=1, source_target_pairs={{0,17},{1,18},{2,19},{3,20},{4,21},{5,22},{6,23},{7,24},{8,25},{9,... | collective-permute-start | bytes 491528
  2768.0 83.5 %collective-permute-start.15 = (f32[16,2560]{1,0:T(8,128)S(1)}, f32[16,2560]{1,0:T(8,128)S(1)}, u32[]{:S(2)}, u32[]{:S(2)}) collective-permute-start(f32[16,2560]{1,0:T(8,128)S(1)} %get-tuple-element.356), channel_id=1, source_target_pairs={{0,16},{1,17},{2,18},{3,19},{4,20},{5,21},{6,22},{7,23},{8,24},{9,... | collective-permute-start | bytes 491528
  2835.8 41.8 %collective-permute-start.14 = (f32[16,2560]{1,0:T(8,128)S(1)}, f32[16,2560]{1,0:T(8,128)S(1)}, u32[]{:S(2)}, u32[]{:S(2)}) collective-permute-start(f32[16,2560]{1,0:T(8,128)S(1)} %get-tuple-element.356), channel_id=1, source_target_pairs={{0,15},{1,16},{2,17},{3,18},{4,19},{5,20},{6,21},{7,22},{8,23},{9,... | collective-permute-start | bytes 491528
  2838.3 43.3 %collective-permute-start.13 = (f32[16,2560]{1,0:T(8,128)S(1)}, f32[16,2560]{1,0:T(8,128)S(1)}, u32[]{:S(2)}, u32[]{:S(2)}) collective-permute-start(f32[16,2560]{1,0:T(8,128)S(1)} %get-tuple-element.356), channel_id=1, source_target_pairs={{0,14},{1,15},{2,16},{3,17},{4,18},{5,19},{6,20},{7,21},{8,22},{9,... | collective-permute-start | bytes 491528
  2843.1 43.9 %collective-permute-start.12 = (f32[16,2560]{1,0:T(8,128)S(1)}, f32[16,2560]{1,0:T(8,128)S(1)}, u32[]{:S(2)}, u32[]{:S(2)}) collective-permute-start(f32[16,2560]{1,0:T(8,128)S(1)} %get-tuple-element.356), channel_id=1, source_target_pairs={{0,13},{1,14},{2,15},{3,16},{4,17},{5,18},{6,19},{7,20},{8,21},{9,... | collective-permute-start | bytes 491528
  2846.7 42.8 %collective-permute-start.11 = (f32[16,2560]{1,0:T(8,128)S(1)}, f32[16,2560]{1,0:T(8,128)S(1)}, u32[]{:S(2)}, u32[]{:S(2)}) collective-permute-start(f32[16,2560]{1,0:T(8,128)S(1)} %get-tuple-element.356), channel_id=1, source_target_pairs={{0,12},{1,13},{2,14},{3,15},{4,16},{5,17},{6,18},{7,19},{8,20},{9,... | collective-permute-start | bytes 491528
  2851.4 44.2 %collective-permute-start.10 = (f32[16,2560]{1,0:T(8,128)S(1)}, f32[16,2560]{1,0:T(8,128)S(1)}, u32[]{:S(2)}, u32[]{:S(2)}) collective-permute-start(f32[16,2560]{1,0:T(8,128)S(1)} %get-tuple-element.356), channel_id=1, source_target_pairs={{0,11},{1,12},{2,13},{3,14},{4,15},{5,16},{6,17},{7,18},{8,19},{9,... | collective-permute-start | bytes 491528
  2877.7 53.5 %collective-permute-start.9 = (f32[16,2560]{1,0:T(8,128)S(1)}, f32[16,2560]{1,0:T(8,128)}, u32[]{:S(2)}, u32[]{:S(2)}) collective-permute-start(f32[16,2560]{1,0:T(8,128)S(1)} %get-tuple-element.356), channel_id=1, source_target_pairs={{0,10},{1,11},{2,12},{3,13},{4,14},{5,15},{6,16},{7,17},{8,18},{9,... | collective-permute-start | bytes 491528
  2881.6 54.9 %collective-permute-start.8 = (f32[16,2560]{1,0:T(8,128)S(1)}, f32[16,2560]{1,0:T(8,128)}, u32[]{:S(2)}, u32[]{:S(2)}) collective-permute-start(f32[16,2560]{1,0:T(8,128)S(1)} %get-tuple-element.356), channel_id=1, source_target_pairs={{0,9},{1,10},{2,11},{3,12},{4,13},{5,14},{6,15},{7,16},{8,17},{9,1... | collective-permute-start | bytes 491528
  2886.9 52.1 %collective-permute-start.7 = (f32[16,2560]{1,0:T(8,128)S(1)}, f32[16,2560]{1,0:T(8,128)}, u32[]{:S(2)}, u32[]{:S(2)}) collective-permute-start(f32[16,2560]{1,0:T(8,128)S(1)} %get-tuple-element.356), channel_id=1, source_target_pairs={{0,8},{1,9},{2,10},{3,11},{4,12},{5,13},{6,14},{7,15},{8,16},{9,17... | collective-permute-start | bytes 491528
  2889.6 51.0 %collective-permute-start.6 = (f32[16,2560]{1,0:T(8,128)S(1)}, f32[16,2560]{1,0:T(8,128)}, u32[]{:S(2)}, u32[]{:S(2)}) collective-permute-start(f32[16,2560]{1,0:T(8,128)S(1)} %get-tuple-element.356), channel_id=1, source_target_pairs={{0,7},{1,8},{2,9},{3,10},{4,11},{5,12},{6,13},{7,14},{8,15},{9,16}... | collective-permute-start | bytes 491528
  2895.7 48.9 %collective-permute-start.5 = (f32[16,2560]{1,0:T(8,128)S(1)}, f32[16,2560]{1,0:T(8,128)}, u32[]{:S(2)}, u32[]{:S(2)}) collective-permute-start(f32[16,2560]{1,0:T(8,128)S(1)} %get-tuple-element.356), channel_id=1, source_target_pairs={{0,6},{1,7},{2,8},{3,9},{4,10},{5,11},{6,12},{7,13},{8,14},{9,15},... | collective-permute-start | bytes 491528
  (222 other events, 13842.3 us)
Sparse Core Ops, SparseCore 0:
  10.3 320.4 all-gather.12
  333.1 310.2 all-gather.14
  646.5 111.8 all-gather.8
  761.2 85.4 all-gather.10
  1406.5 16.7 reduce-scatter.11
  1426.1 21.1 reduce-scatter.13
  1451.5 160.8 reduce-scatter.17
  1616.8 254.1 reduce-scatter.15
where the time goes:
time: 3040 us; the launch traced here: 3030 us
  blocking collectives  1550 us (51%)
  starting transfers between devices  523 us (17%)
  waiting for transfers between devices  288 us (9%)
  local copies, waits for them, and re-layouts  256 us (8%)
  matrix products  249 us (8%)
  other arithmetic  141 us (5%)
    unnamed x2, blocking collectives  894 us
    unnamed x96, starting transfers between devices  467 us
    all_gather x1, blocking collectives, shards(): lax.all_gather(norm_gains.astype(jnp.bfloat16), ('dp', 'blk', 'ulys'), ax...  317 us
    all_gather x1, blocking collectives, shards(): lax.all_gather(router_weight.astype(jnp.bfloat16), ('dp', 'blk', 'ulys'),...  313 us
    unnamed x269, local copies, waits for them, and re-layouts  138 us
    all_to_all x2, waiting for transfers between devices, combine(): lax.all_to_all(buffer, 'ulys', split_axis=1, concat_axis=0, tiled=True)  137 us
    all_to_all x2, waiting for transfers between devices, dispatch(): lax.all_to_all(buffer, 'ulys', split_axis=0, concat_axis=1, tiled=True)  82.1 us
  transfers between devices with their start and end apart: 116, of which 40 were waited for; matrix products, arithmetic and copies ran while one was open for 41% of the time, Pallas kernels for 0%

commit v1 on v0

v1 whole, which is shorter than its diff:
```python
import functools

import jax
import jax.numpy as jnp
from jax import lax
from jax.experimental import pallas as pl
from jax.experimental.pallas import tpu as pltpu
from jax.sharding import Mesh
from jax.sharding import PartitionSpec as P

D = 1536
HQ = 24
HK = 8
HD = 64
F = 512
EXPERTS = 40
TOPK = 8
ADAM_STEP = 10
CAP = 48
TOK = 128
GROUP = 8
LOCAL_E = 5
SPAN = 1024
CHUNK = 512
QW = 192
SLOTS = GROUP * CAP
HALF = HD // 2
EXTRA = 128

bf16 = jnp.bfloat16
f32 = jnp.float32
attention_scale = 0.015625
residual_scale = 0.22
norm_epsilon = 1e-06
rope_base = 10000.0
beta_first = 0.9
beta_second = 0.95
adam_epsilon = 1e-08
weight_decay = 0.1
rate_project_in = 0.2
rate_project_out = 2.0
rate_router = 0.03
rate_gains = 0.5
rate_expert_up = 0.05
rate_expert_down = 2.0
log2_e = 1.4426950408889634

ULYS = ("x", "zl")
ALL = ("zh", "co", "blk", "x", "zl")
DPBLK = ("zh", "co", "blk")


def dot(a, b, dims):
    return lax.dot_general(a, b, ((dims[0], dims[1]), ((), ())), preferred_element_type=f32)


def rms_scale(rows_in):
    return lax.rsqrt(jnp.mean(rows_in * rows_in, axis=1, keepdims=True) + norm_epsilon)


def norm_back(rows_in, scale_in, gain_in, grad_in):
    weighted = grad_in * gain_in
    inner_sum = jnp.mean(weighted * rows_in, axis=1, keepdims=True)
    return scale_in * weighted - rows_in * (scale_in * scale_in * scale_in) * inner_sum


def adam_update(weight, first_moment, second, gradient, step_rate):
    first_new = beta_first * first_moment + (1.0 - beta_first) * gradient
    second_new = beta_second * second + (1.0 - beta_second) * gradient * gradient
    first_hat = first_new / (1.0 - beta_first**ADAM_STEP)
    second_hat = second_new / (1.0 - beta_second**ADAM_STEP)
    weight_new = weight - step_rate * (
        first_hat / (jnp.sqrt(second_hat) + adam_epsilon) + weight_decay * weight
    )
    return (weight_new, first_new, second_new)


def a2a(value, axes):
    return lax.all_to_all(value, axes, split_axis=0, concat_axis=0, tiled=True)


def swap(value, axis):
    return lax.ppermute(value, axis, [(0, 1), (1, 0)])


def zigzag(value):
    pairs = []
    for blk in range(4):
        for x in range(4):
            other = 3 - blk if x >= 2 else blk
            pairs.append((blk * 4 + x, other * 4 + x))
    return lax.ppermute(value, ("blk", "x"), pairs)


def gather_group(value):
    pair = jnp.stack([value, swap(value, "zl")])
    return a2a(jnp.broadcast_to(pair[None], (4,) + pair.shape), "x")


def scatter_group(partial):
    arrived = jnp.sum(a2a(partial, "x").astype(f32), axis=0)
    return arrived[0] + swap(arrived[1].astype(bf16), "zl").astype(f32)


def gather_rows(value):
    mine = a2a(jnp.broadcast_to(value[None], (8,) + value.shape), ("zh", "blk"))
    other = swap(mine, "co")
    first = lax.axis_index("co") == 0
    low = jnp.where(first, mine, other).reshape(2, 1, 4, *value.shape)
    high = jnp.where(first, other, mine).reshape(2, 1, 4, *value.shape)
    return jnp.concatenate([low, high], axis=1).reshape(D, value.shape[1])


def scatter_rows(partial):
    columns = partial.shape[1]
    cut = partial.reshape(2, 2, 4, 96, columns)
    first = lax.axis_index("co") == 0
    keep = jnp.where(first, cut[:, 0], cut[:, 1])
    give = jnp.where(first, cut[:, 1], cut[:, 0])
    both = keep.astype(f32) + swap(give, "co").astype(f32)
    arrived = a2a(both.astype(bf16).reshape(8, 96, columns), ("zh", "blk"))
    return jnp.sum(arrived.astype(f32), axis=0)


def attend_kernel(block_ref, pos_row, pos_col, q_ref, k_ref, v_ref, out_ref, log_ref, acc, peak, total):
    base = 2 * block_ref[0]

    def part(half, at, masked):
        cols = slice(half * CHUNK, (half + 1) * CHUNK)
        keys = k_ref[at]
        vals = v_ref[at]
        for head in range(3):
            scores = dot(keys, q_ref[head, :, cols], ((1,), (0,))) * (attention_scale * log2_e)
            if masked:
                scores = jnp.where(pos_col[...] <= pos_row[...], scores, -jnp.inf)
            before = peak[head]
            now = jnp.maximum(before, jnp.max(scores, axis=0, keepdims=True))
            weights = jnp.exp2(scores - now)
            fade = jnp.exp2(before - now)
            total[head] = total[head] * fade + jnp.sum(weights, axis=0, keepdims=True)
            acc[head] = acc[head] * fade + dot(vals, weights.astype(bf16), ((1,), (0,)))
            peak[head] = now

    for half in range(2):
        cols = slice(half * CHUNK, (half + 1) * CHUNK)
        last = base if half == 0 else 7 - base
        acc[...] = jnp.zeros_like(acc)
        total[...] = jnp.zeros_like(total)
        peak[...] = jnp.full_like(peak, -1e30)
        part(half, last, True)

        def step(at, carry):
            part(half, at, False)
            return carry

        lax.fori_loop(0, last, step, 0)
        for head in range(3):
            out_ref[head, :, cols] = acc[head] / total[head]
            log_ref[head, :, cols] = peak[head] + jnp.log2(total[head])


def attend(block, pos, q_t, keys, vals_t):
    vmem = pl.BlockSpec(memory_space=pltpu.VMEM)
    return pl.pallas_call(
        attend_kernel,
        out_shape=(
            jax.ShapeDtypeStruct((3, HD, SPAN), f32),
            jax.ShapeDtypeStruct((3, 1, SPAN), f32),
        ),
        in_specs=[pl.BlockSpec(memory_space=pltpu.SMEM)] + [vmem] * 5,
        out_specs=(vmem, vmem),
        scratch_shapes=[
            pltpu.VMEM((3, HD, CHUNK), f32),
            pltpu.VMEM((3, 1, CHUNK), f32),
            pltpu.VMEM((3, 1, CHUNK), f32),
        ],
        compiler_params=pltpu.CompilerParams(vmem_limit_bytes=48 << 20),
        cost_estimate=pl.CostEstimate(flops=4 * 9 * 3 * 512 * 512 * 256, bytes_accessed=4 << 20, transcendentals=7 << 20),
        name="attend",
    )(block, pos[None, :], pos[:, None], q_t, keys, vals_t)


def attend_back_kernel(
    block_ref, pos_row, pos_col, qt_ref, q_ref, k_ref, kt_ref, v_ref, dot_ref, do_ref, out_ref, log_ref,
    dq_ref, dk_ref, dv_ref, dq_acc, dk_acc, dv_acc, inner
):
    base = 2 * block_ref[0]
    dk_acc[...] = jnp.zeros_like(dk_acc)
    dv_acc[...] = jnp.zeros_like(dv_acc)
    for head in range(3):
        inner[head] = jnp.sum(dot_ref[head].astype(f32) * out_ref[head], axis=0, keepdims=True)

    def part(half, at, masked):
        cols = slice(half * CHUNK, (half + 1) * CHUNK)
        keys = k_ref[at]
        keys_t = kt_ref[at]
        vals = v_ref[at]
        for head in range(3):
            scores = dot(keys, qt_ref[head, :, cols], ((1,), (0,))) * (attention_scale * log2_e)
            probs = jnp.exp2(scores - log_ref[head, :, cols])
            if masked:
                probs = jnp.where(pos_col[...] <= pos_row[...], probs, 0.0)
            prob_grad = dot(vals, dot_ref[head, :, cols], ((1,), (0,)))
            score_grad = (probs * (prob_grad - inner[head, :, cols])).astype(bf16)
            dv_acc[at] += dot(probs.astype(bf16), do_ref[head, cols], ((1,), (0,)))
            dk_acc[at] += dot(score_grad, q_ref[head, cols], ((1,), (0,)))
            dq_acc[head] += dot(keys_t, score_grad, ((1,), (0,)))

    for half in range(2):
        cols = slice(half * CHUNK, (half + 1) * CHUNK)
        last = base if half == 0 else 7 - base
        dq_acc[...] = jnp.zeros_like(dq_acc)
        part(half, last, True)

        def step(at, carry):
            part(half, at, False)
            return carry

        lax.fori_loop(0, last, step, 0)
        dq_ref[:, :, cols] = (dq_acc[...] * attention_scale).astype(bf16)
    dk_ref[...] = (dk_acc[...] * attention_scale).astype(bf16)
    dv_ref[...] = dv_acc[...].astype(bf16)


def attend_back(block, pos, q_t, q_n, keys, keys_t, vals, grad_t, grad_n, out_t, logs):
    vmem = pl.BlockSpec(memory_space=pltpu.VMEM)
    return pl.pallas_call(
        attend_back_kernel,
        out_shape=(
            jax.ShapeDtypeStruct((3, HD, SPAN), bf16),
            jax.ShapeDtypeStruct((8, CHUNK, HD), bf16),
            jax.ShapeDtypeStruct((8, CHUNK, HD), bf16),
        ),
        in_specs=[pl.BlockSpec(memory_space=pltpu.SMEM)] + [vmem] * 11,
        out_specs=(vmem, vmem, vmem),
        scratch_shapes=[
            pltpu.VMEM((3, HD, CHUNK), f32),
            pltpu.VMEM((8, CHUNK, HD), f32),
            pltpu.VMEM((8, CHUNK, HD), f32),
            pltpu.VMEM((3, 1, SPAN), f32),
        ],
        compiler_params=pltpu.CompilerParams(vmem_limit_bytes=48 << 20),
        cost_estimate=pl.CostEstimate(flops=10 * 9 * 3 * 512 * 512 * 256, bytes_accessed=8 << 20, transcendentals=7 << 20),
        name="attend_back",
    )(block, pos[None, :], pos[:, None], q_t, q_n, keys, keys_t, vals, grad_t, grad_n, out_t, logs)


def pick_rows(rank_ref, at):
    return rank_ref[0, at : at + 1, :] == lax.broadcasted_iota(jnp.int32, (CAP, TOK), 0)


def expert_kernel(
    first_ref, rank_ref, gate_ref, x_ref, c_ref, w_ref,
    sum_ref, rows_ref, slot_ref, act_ref, both_ref, scale_ref, acc
):
    number = pl.program_id(0)
    weights = w_ref.at[:, 0]

    @pl.when(number == 0)
    def _():
        acc[...] = jnp.zeros_like(acc)

    cots = []
    for at in range(GROUP):
        rows = slice(at * CAP, (at + 1) * CAP)
        hits = pick_rows(rank_ref, at)
        onehot = hits.astype(f32).astype(bf16)
        rows_ref[0, rows] = dot(onehot, x_ref[at], ((1,), (0,))).astype(bf16)
        scale = jnp.sum(jnp.where(hits, gate_ref[0, at : at + 1, :], 0.0), axis=1, keepdims=True)
        scale_ref[0, rows] = jnp.broadcast_to(scale, (CAP, 128))
        cot = dot(onehot, c_ref[at, :, :D], ((1,), (0,))) * residual_scale
        slot_ref[0, rows] = (cot * scale).astype(bf16)
    up = weights[:, :, : 2 * F].reshape(D, 2 * F)
    down = weights[:, :, 2 * F :].reshape(D, F)
    both = dot(rows_ref[0], up, ((1,), (0,)))
    gate = both[:, :F]
    linear = both[:, F:]
    sigmoid = 1.0 / (1.0 + jnp.exp(-gate))
    silu = gate * sigmoid
    activated = (silu * linear).astype(bf16)
    act_ref[0] = activated
    slope = sigmoid * (1.0 + gate * (1.0 - sigmoid))
    act_grad = dot(slot_ref[0], down, ((1,), (0,)))
    weighted = jnp.sum(activated.astype(f32) * act_grad, axis=1, keepdims=True)
    both_ref[0, :, :F] = (act_grad * linear * slope).astype(bf16)
    both_ref[0, :, F:] = (act_grad * silu).astype(bf16)
    back = dot(both_ref[0], up, ((1,), (1,))).astype(bf16)
    high = weighted.astype(bf16).astype(f32)
    low = weighted - high
    lane = lax.broadcasted_iota(jnp.int32, (SLOTS, EXTRA), 1)
    mine = first_ref[0] + number
    tail = (jnp.where(lane == mine, high, 0.0) + jnp.where(lane == mine + EXPERTS, low, 0.0)).astype(bf16)
    for at in range(GROUP):
        rows = slice(at * CAP, (at + 1) * CAP)
        onehot = pick_rows(rank_ref, at).astype(f32).astype(bf16)
        acc[at, :, :D] += dot(onehot, back[rows], ((0,), (0,)))
        acc[at, :, D:] += dot(onehot, tail[rows], ((0,), (0,)))

    @pl.when(number == LOCAL_E - 1)
    def _():
        sum_ref[...] = acc[...].astype(bf16)


def expert_pass(first, ranks, gates, rows, cots, weights):
    whole = lambda *shape: pl.BlockSpec(shape, lambda e: (0,) * len(shape), pipeline_mode=pl.Buffered(1))
    return pl.pallas_call(
        expert_kernel,
        grid=(LOCAL_E,),
        out_shape=(
            jax.ShapeDtypeStruct((GROUP, TOK, D + EXTRA), bf16),
            jax.ShapeDtypeStruct((LOCAL_E, SLOTS, D), bf16),
            jax.ShapeDtypeStruct((LOCAL_E, SLOTS, D), bf16),
            jax.ShapeDtypeStruct((LOCAL_E, SLOTS, F), bf16),
            jax.ShapeDtypeStruct((LOCAL_E, SLOTS, 2 * F), bf16),
            jax.ShapeDtypeStruct((LOCAL_E, SLOTS, 128), f32),
        ),
        in_specs=[
            pl.BlockSpec(memory_space=pltpu.SMEM),
            pl.BlockSpec((1, GROUP, TOK), lambda e: (e, 0, 0)),
            pl.BlockSpec((1, GROUP, TOK), lambda e: (e, 0, 0)),
            whole(GROUP, TOK, D),
            whole(GROUP, TOK, D + EXTRA),
            pl.BlockSpec((16, 1, 96, 3 * F), lambda e: (0, e, 0, 0)),
        ],
        out_specs=(
            whole(GROUP, TOK, D + EXTRA),
            pl.BlockSpec((1, SLOTS, D), lambda e: (e, 0, 0)),
            pl.BlockSpec((1, SLOTS, D), lambda e: (e, 0, 0)),
            pl.BlockSpec((1, SLOTS, F), lambda e: (e, 0, 0)),
            pl.BlockSpec((1, SLOTS, 2 * F), lambda e: (e, 0, 0)),
            pl.BlockSpec((1, SLOTS, 128), lambda e: (e, 0, 0)),
        ),
        scratch_shapes=[pltpu.VMEM((GROUP, TOK, D + EXTRA), f32)],
        compiler_params=pltpu.CompilerParams(vmem_limit_bytes=58 << 20),
        cost_estimate=pl.CostEstimate(flops=5 * 3 * 10**9, bytes_accessed=60 << 20, transcendentals=1 << 20),
        name="experts",
    )(first, ranks, gates, rows, cots, weights)


def grad_kernel(rows_ref, slot_ref, act_ref, both_ref, out_ref):
    for at in range(4):
        cols = slice(at * 384, (at + 1) * 384)
        up = dot(rows_ref[0, :, cols], both_ref[0], ((0,), (0,)))
        out_ref[at * 4 : at * 4 + 4, 0, :, : 2 * F] = up.astype(bf16).reshape(4, 96, 2 * F)
        down = dot(slot_ref[0, :, cols], act_ref[0], ((0,), (0,)))
        out_ref[at * 4 : at * 4 + 4, 0, :, 2 * F :] = down.astype(bf16).reshape(4, 96, F)


def expert_grads(rows, slots, activated, both):
    block = lambda width: pl.BlockSpec((1, SLOTS, width), lambda e: (e, 0, 0))
    return pl.pallas_call(
        grad_kernel,
        grid=(LOCAL_E,),
        out_shape=jax.ShapeDtypeStruct((16, LOCAL_E, 96, 3 * F), bf16),
        in_specs=[block(D), block(D), block(F), block(2 * F)],
        out_specs=pl.BlockSpec((16, 1, 96, 3 * F), lambda e: (0, e, 0, 0)),
        compiler_params=pltpu.CompilerParams(vmem_limit_bytes=48 << 20),
        cost_estimate=pl.CostEstimate(flops=9 * 10**9, bytes_accessed=45 << 20, transcendentals=0),
        name="expert_grads",
    )(rows, slots, activated, both)


def mixture_kernel(rank_ref, act_ref, scale_ref, w_ref, sum_ref, acc):
    number = pl.program_id(0)

    @pl.when(number == 0)
    def _():
        acc[...] = jnp.zeros_like(acc)

    down = w_ref[:, 0].reshape(D, F)
    produced = dot(act_ref[0], down, ((1,), (1,))).astype(bf16).astype(f32)
    produced = (produced * scale_ref[0, :, 0:1]).astype(bf16)
    for at in range(GROUP):
        rows = slice(at * CAP, (at + 1) * CAP)
        onehot = pick_rows(rank_ref, at).astype(f32).astype(bf16)
        acc[at] += dot(onehot, produced[rows], ((0,), (0,)))

    @pl.when(number == LOCAL_E - 1)
    def _():
        sum_ref[...] = acc[...].astype(bf16)


def expert_mixture(ranks, activated, scales, weights):
    return pl.pallas_call(
        mixture_kernel,
        grid=(LOCAL_E,),
        out_shape=jax.ShapeDtypeStruct((GROUP, TOK, D), bf16),
        in_specs=[
            pl.BlockSpec((1, GROUP, TOK), lambda e: (e, 0, 0)),
            pl.BlockSpec((1, SLOTS, F), lambda e: (e, 0, 0)),
            pl.BlockSpec((1, SLOTS, 128), lambda e: (e, 0, 0)),
            pl.BlockSpec((16, 1, 96, F), lambda e: (0, e, 0, 2)),
        ],
        out_specs=pl.BlockSpec((GROUP, TOK, D), lambda e: (0, 0, 0)),
        scratch_shapes=[pltpu.VMEM((GROUP, TOK, D), f32)],
        compiler_params=pltpu.CompilerParams(vmem_limit_bytes=48 << 20),
        cost_estimate=pl.CostEstimate(flops=4 * 10**9, bytes_accessed=20 << 20, transcendentals=0),
        name="mixture",
    )(ranks, activated, scales, weights)


def shards(
    tokens, cotangent, routes, project_in, project_out, router_weight, norm_gains, expert_up, expert_down,
    project_in_first, project_in_second, project_out_first, project_out_second,
    router_weight_first, router_weight_second, norm_gains_first, norm_gains_second,
    expert_up_first, expert_up_second, expert_down_first, expert_down_second,
):
    block = lax.axis_index("blk")
    z_low = lax.axis_index("zl")
    ulys = lax.axis_index("x") * 2 + z_low

    experts_own = jnp.concatenate(
        [expert_up.astype(bf16), jnp.swapaxes(expert_down.astype(bf16), 1, 2)], axis=2
    )
    experts_full = lax.all_gather(
        experts_own.reshape(LOCAL_E * 96, 3 * F), DPBLK, axis=0, tiled=True
    ).reshape(16, LOCAL_E, 96, 3 * F)

    tokens = zigzag(tokens)
    tokens_all = gather_group(tokens).reshape(SPAN, D)

    in_own = project_in.astype(bf16)
    small = jnp.concatenate([router_weight.astype(bf16), norm_gains.astype(bf16).T], axis=1)
    small = jnp.pad(small, ((0, 0), (0, 22)))
    out_own = project_out.astype(bf16).T
    cut = lambda v: jnp.swapaxes(v.reshape(12, GROUP, -1), 0, 1)
    payload = jnp.concatenate(
        [
            cut(in_own[:, :1536]),
            cut(in_own[:, 1536:2048]),
            cut(in_own[:, 2048:]),
            jnp.broadcast_to(small[None], (GROUP, 12, 64)),
            jnp.broadcast_to(out_own[None], (GROUP, 12, D)),
        ],
        axis=2,
    )
    arrived = a2a(payload, ULYS).reshape(96, 384 + D)
    near = gather_rows(arrived[:, :384])
    out_t = gather_rows(arrived[:, 384:])
    in_cols = near[:, :320]
    router_full = near[:, 320:360]
    gains = near[:, 360:362].astype(f32).T
    gain_attn = gains[0]
    gain_ffn = gains[1]

    cotangent = zigzag(cotangent)
    route_cols = zigzag(routes).astype(bf16)
    carried = jnp.concatenate([cotangent, jnp.pad(route_cols, ((0, 0), (0, EXTRA - TOPK)))], axis=1)
    carried_all = gather_group(carried).reshape(GROUP, TOK, D + EXTRA)

    x_all = tokens_all.astype(f32)
    scale_all = rms_scale(x_all)
    normed_all = (x_all * scale_all * gain_attn).astype(bf16)
    mixed_t = dot(in_cols, normed_all, ((0,), (1,)))
    x_of = jnp.arange(SPAN, dtype=jnp.int32) // 256
    turn = jnp.arange(SPAN, dtype=jnp.int32) // 128 % 2
    within = ((x_of % 2) * 2 + (turn ^ z_low)) * 128 + jnp.arange(SPAN, dtype=jnp.int32) % 128
    chunk_of = jnp.where(x_of < 2, 2 * block, 7 - 2 * block)
    position = (chunk_of * CHUNK + within).astype(f32)
    frequency = rope_base ** (-jnp.arange(HALF, dtype=f32) * 2.0 / HD)
    angles = frequency[:, None] * position[None, :]
    cosine = jnp.cos(angles)
    sine = jnp.sin(angles)
    turned = mixed_t[:256].reshape(4, 2, HALF, SPAN)
    lower = turned[:, 0] * cosine - turned[:, 1] * sine
    upper = turned[:, 1] * cosine + turned[:, 0] * sine
    turned = jnp.stack([lower, upper], axis=1).astype(bf16).reshape(4, HD, SPAN)
    q_t = turned[:3]
    kv_t = jnp.concatenate([turned[3], mixed_t[256:].astype(bf16)], axis=0)
    kv_all = a2a(jnp.broadcast_to(kv_t[None], (4, 128, SPAN)), "blk")
    chunks = []
    for at in range(8):
        source, half = (at // 2, 0) if at % 2 == 0 else ((7 - at) // 2, 1)
        chunks.append(kv_all[source, :, half * CHUNK : (half + 1) * CHUNK])
    kv_chunks = jnp.stack(chunks)
    keys_t = kv_chunks[:, :HD]
    vals_t = kv_chunks[:, HD:]
    keys_n = jnp.swapaxes(keys_t, 1, 2)
    vals_n = jnp.swapaxes(vals_t, 1, 2)
    block_one = block.reshape(1).astype(jnp.int32)
    mask_pos = within[:CHUNK]
    heads_t, logs = attend(block_one, mask_pos, q_t, keys_n, vals_t)
    heads_low = heads_t.astype(bf16).reshape(QW, GROUP, TOK)
    absolute = lambda v: jnp.where(z_low == 0, v, v[:, ::-1])
    sent = absolute(jnp.swapaxes(heads_low, 0, 1).reshape(4, 2, QW, TOK)).reshape(GROUP, QW, TOK)
    attended_t = a2a(sent, ULYS).reshape(D, TOK)

    branch = dot(attended_t, out_t, ((0,), (1,)))
    x_own = tokens.astype(f32)
    hidden = x_own + residual_scale * branch
    scale_ffn = rms_scale(hidden)
    normed_ffn = (hidden * scale_ffn * gain_ffn).astype(bf16)
    ffn_all = gather_group(normed_ffn).reshape(GROUP, TOK, D)

    def gates_of(logits, hits):
        masked = jnp.where(hits, logits, -jnp.inf)
        raised = jnp.exp(masked - jnp.max(masked, axis=-1, keepdims=True))
        return raised / jnp.sum(raised, axis=-1, keepdims=True)

    expert_ids = jnp.arange(EXPERTS, dtype=jnp.int32)
    route_all = carried_all[:, :, D : D + TOPK].astype(jnp.int32)
    hits_all = jnp.any(route_all[..., None] == expert_ids, axis=2)
    hits_own = jnp.any(route_cols.astype(jnp.int32)[..., None] == expert_ids, axis=1)
    first = (ulys * LOCAL_E).astype(jnp.int32)
    hits_local = lax.dynamic_slice_in_dim(hits_all, first, LOCAL_E, axis=2)
    earlier = jnp.tril(jnp.ones((TOK, TOK), bf16), -1)
    ranks = jnp.einsum("rt,stj->jsr", earlier, hits_local.astype(bf16), preferred_element_type=f32)
    ranks = jnp.where(jnp.transpose(hits_local, (2, 0, 1)), ranks.astype(jnp.int32), -1)
    logits_all = dot(ffn_all.reshape(SPAN, D), router_full, ((1,), (0,)))
    gates_all = gates_of(logits_all.reshape(GROUP, TOK, EXPERTS), hits_all)
    gates_local = jnp.transpose(lax.dynamic_slice_in_dim(gates_all, first, LOCAL_E, axis=2), (2, 0, 1))
    gates_own = gates_of(dot(normed_ffn, router_full, ((1,), (0,))), hits_own)

    ffn_sums, slot_rows, slot_grads, activated, both_grad, slot_gates = expert_pass(
        first.reshape(1), ranks, gates_local, ffn_all, carried_all, experts_full
    )
    expert_grad = expert_grads(slot_rows, slot_grads, activated, both_grad)
    expert_sum = lax.psum_scatter(
        expert_grad.reshape(16 * LOCAL_E * 96, 3 * F), DPBLK, scatter_dimension=0, tiled=True
    ).reshape(LOCAL_E, 96, 3 * F)
    returned = scatter_group(ffn_sums.reshape(4, 2, TOK, D + EXTRA))

    upstream = cotangent.astype(f32)
    weighted = returned[:, D : D + EXPERTS] + returned[:, D + EXPERTS : D + 2 * EXPERTS]
    logit_grad = weighted - gates_own * jnp.sum(weighted, axis=1, keepdims=True)
    ffn_grad = returned[:, :D] + jnp.dot(
        logit_grad, router_full.astype(f32).T, precision=lax.Precision.HIGHEST
    )
    router_grad = dot(normed_ffn, logit_grad.astype(bf16), ((0,), (0,)))
    gain_ffn_grad = jnp.sum(ffn_grad * hidden * scale_ffn, axis=0)
    hidden_grad = upstream + norm_back(hidden, scale_ffn, gain_ffn, ffn_grad)
    branch_grad = (residual_scale * hidden_grad).astype(bf16)

    attended_grad_t = dot(out_t, branch_grad, ((0,), (1,))).astype(bf16)
    grad_all = a2a(attended_grad_t.reshape(GROUP, QW, TOK), ULYS)
    grad_all = absolute(grad_all.reshape(4, 2, QW, TOK)).reshape(GROUP, QW, TOK)
    grad_t = jnp.swapaxes(grad_all, 0, 1).reshape(3, HD, SPAN)
    dq_t, dk, dv = attend_back(
        block_one, mask_pos, q_t, jnp.swapaxes(q_t, 1, 2), keys_n, keys_t, vals_n,
        grad_t, jnp.swapaxes(grad_t, 1, 2), heads_t, logs,
    )
    kv_grad = jnp.concatenate([dk, dv], axis=2)
    kv_parts = jnp.stack([jnp.concatenate([kv_grad[2 * g], kv_grad[7 - 2 * g]], axis=0) for g in range(4)])
    kv_sum_t = jnp.sum(a2a(kv_parts, "blk").astype(f32), axis=0).T.astype(bf16)

    branch_grad_all = gather_group(branch_grad).reshape(SPAN, D)
    out_grad_t = dot(branch_grad_all, heads_low.reshape(QW, SPAN), ((0,), (1,)))

    mixture_sums = expert_mixture(ranks, activated, slot_gates, experts_full)
    layer_out = hidden + residual_scale * scatter_group(mixture_sums.reshape(4, 2, TOK, D))

    back = jnp.concatenate([dq_t.reshape(QW, SPAN), kv_sum_t[:HD]], axis=0).astype(f32)
    back = back.reshape(4, 2, HALF, SPAN)
    lower = back[:, 0] * cosine + back[:, 1] * sine
    upper = back[:, 1] * cosine - back[:, 0] * sine
    back = jnp.stack([lower, upper], axis=1).astype(bf16).reshape(256, SPAN)
    mixed_grad_t = jnp.concatenate([back, kv_sum_t[HD:]], axis=0)
    in_grad = dot(normed_all, mixed_grad_t, ((0,), (1,)))
    normed_part = dot(mixed_grad_t, in_cols, ((0,), (1,)))
    gain_attn_grad = jnp.sum(normed_part * x_all * scale_all, axis=0)
    normed_grad = scatter_group(normed_part.astype(bf16).reshape(4, 2, TOK, D))
    tokens_grad = hidden_grad + norm_back(x_own, rms_scale(x_own), gain_attn, normed_grad)

    rest = jnp.stack([gain_attn_grad, gain_ffn_grad], axis=1)
    grads = jnp.concatenate(
        [in_grad.astype(bf16), out_grad_t.astype(bf16), router_grad.astype(bf16), rest.astype(bf16)], axis=1
    )
    grads = jnp.pad(grads, ((0, 0), (0, 640 - 554)))
    owned = a2a(scatter_rows(grads).astype(bf16).reshape(GROUP, 12, 640), ULYS).astype(f32)
    lay = lambda v: jnp.swapaxes(v, 0, 1).reshape(12, -1)
    in_sum = jnp.concatenate([lay(owned[:, :, :192]), lay(owned[:, :, 192:256]), lay(owned[:, :, 256:320])], axis=1)
    out_sum = lay(owned[:, :, 320:512]).T
    shared_sum = jnp.sum(owned[:, :, 512:554], axis=0)
    router_sum = shared_sum[:, :EXPERTS]
    gains_sum = shared_sum[:, EXPERTS:].T
    up_sum = expert_sum[:, :, : 2 * F].astype(f32)
    down_sum = jnp.swapaxes(expert_sum[:, :, 2 * F :], 1, 2).astype(f32)

    layer_out = zigzag(layer_out)
    tokens_grad = zigzag(tokens_grad)
    return (
        layer_out,
        tokens_grad,
        *adam_update(project_in, project_in_first, project_in_second, in_sum, rate_project_in),
        *adam_update(project_out, project_out_first, project_out_second, out_sum, rate_project_out),
        *adam_update(router_weight, router_weight_first, router_weight_second, router_sum, rate_router),
        *adam_update(norm_gains, norm_gains_first, norm_gains_second, gains_sum, rate_gains),
        *adam_update(expert_up, expert_up_first, expert_up_second, up_sum, rate_expert_up),
        *adam_update(expert_down, expert_down_first, expert_down_second, down_sum, rate_expert_down),
    )


def solution(mesh):
    fine = Mesh(mesh.devices.reshape(2, 2, 4, 4, 2), ALL)
    rows = P(ALL, None)
    cols = P(None, ALL)
    up = P(ULYS, DPBLK, None)
    down = P(ULYS, None, DPBLK)
    in_specs = (rows,) * 4 + (cols, rows, cols, up, down)
    in_specs += (rows,) * 2 + (cols,) * 2 + (rows,) * 2 + (cols,) * 2 + (up,) * 2 + (down,) * 2
    out_specs = (rows,) * 5 + (cols,) * 3 + (rows,) * 3 + (cols,) * 3 + (up,) * 3 + (down,) * 3
    return jax.shard_map(shards, mesh=fine, in_specs=in_specs, out_specs=out_specs, check_vma=False)
```

time: 3040 us -> 726 us (0.24)
  blocking collectives: 1550 us -> 38.2 us
  starting transfers between devices: 523 us -> 109 us
  matrix products: 249 us -> 24.9 us
  local copies, waits for them, and re-layouts: 256 us -> 60.4 us
  Pallas kernels: 0 us -> 101 us
  other arithmetic: 141 us -> 58 us
    unnamed x2 -> x0, blocking collectives: 894 us -> none
    all_gather x4 -> x0, blocking collectives: 656 us -> none  [the longest x1 317 us: shards(): lax.all_gather(norm_gains.astype(jnp.bfloat16), ('dp', 'blk', 'ulys'), ax...]
    unnamed x96 -> x0, starting transfers between devices: 467 us -> none
    dot_general x29 -> x11, matrix products: 249 us -> 24.9 us  [the longest x9 21.5 us: dot(): lax.dot_general(a, b, ((dims[0], dims[1]), ((), ())), preferred_element_t...]
    unnamed x269 -> x175, local copies, waits for them, and re-layouts: 138 us -> 22.2 us
    pallas_call x0 -> x5, Pallas kernels: none -> 101 us  [the longest x1 34.2 us: expert_pass(): pl.pallas_call(expert_kernel, grid=(LOCAL_E,), out_shape=(jax.ShapeDtypeS...]
    ppermute x0 -> x15, waiting for transfers between devices: none -> 58.2 us  [the longest x10 58.2 us: swap(): return lax.ppermute(value, axis, [(0, 1), (1, 0)])]
    another operation x8 -> x16, other arithmetic: 47.3 us -> 4.04 us  [the longest x6 2.47 us: gather_group(): pair = jnp.stack([value, swap(value, 'zl')])]
  transfers between devices with their start and end apart: 116 -> 32, of which waited for: 40 -> 20; matrix products, arithmetic and copies ran while one was open for 41% -> 16% of each run, Pallas kernels for 0% -> 7%
where the time goes in v1:
time: 726 us; the launch traced here: 715 us
  waiting for transfers between devices  307 us (42%)
  starting transfers between devices  109 us (15%)
  Pallas kernels  101 us (14%)
  local copies, waits for them, and re-layouts  60.4 us (8%)
  other arithmetic  58 us (8%)
  blocking collectives  38.2 us (5%)
  matrix products  24.9 us (3%)
  between operations  16 us (2%)
    all_to_all x15, waiting for transfers between devices, a2a(): return lax.all_to_all(value, axes, split_axis=0, concat_axis=0, tiled=True)  249 us
    all_to_all x15, starting transfers between devices, a2a(): return lax.all_to_all(value, axes, split_axis=0, concat_axis=0, tiled=True)  89.9 us
    ppermute x10, waiting for transfers between devices, swap(): return lax.ppermute(value, axis, [(0, 1), (1, 0)])  58.2 us
    all_to_all x1, blocking collectives, a2a(): return lax.all_to_all(value, axes, split_axis=0, concat_axis=0, tiled=True)  38.2 us
    pallas_call x1, Pallas kernels, expert_pass(): pl.pallas_call(expert_kernel, grid=(LOCAL_E,), out_shape=(jax.ShapeDtypeS...  34.2 us
    pallas_call x1, Pallas kernels, attend_back(): pl.pallas_call(attend_back_kernel, out_shape=(jax.ShapeDtypeStruct((3, HD...  22.5 us
    unnamed x175, local copies, waits for them, and re-layouts  22.2 us
    dot_general x9, matrix products, dot(): lax.dot_general(a, b, ((dims[0], dims[1]), ((), ())), preferred_element_t...  21.5 us
  transfers between devices with their start and end apart: 32, of which 20 were waited for; matrix products, arithmetic and copies ran while one was open for 16% of the time, Pallas kernels for 7%

profile of v1, /device:TPU:0, one launch (start us, length us, event | category | flops | bytes accessed | tf_op | source)
XLA Modules:
  0.0 714.6 jit_solution(17893609808588776348)
XLA Ops:
  13.8 10.0 %all-to-all-start = ((bf16[8,12,1920]{2,1,0:T(8,128)(2,1)}), bf16[8,12,1920]{2,1,0:T(8,128)(2,1)S(1)}, u32[]{:S(2)}, u32[]{:S(2)}) async-start(bf16[8,12,1920]{2,1,0:T(8,128)(2,1)} %concatenate.50), calls=%async_computation | async-start | bytes 983040 | tf_op jit(solution)/shard_map/all_to_all | solution.py:79
  25.8 7.7 %all-to-all-done = bf16[8,12,1920]{2,1,0:T(8,128)(2,1)S(1)} async-done(((bf16[8,12,1920]{2,1,0:T(8,128)(2,1)}), bf16[8,12,1920]{2,1,0:T(8,128)(2,1)S(1)}, u32[]{:S(2)}, u32[]{:S(2)}) %all-to-all-start) | async-done | bytes 368672 | tf_op jit(solution)/shard_map/all_to_all | solution.py:79
  34.6 5.4 all-to-all-start.1
  40.0 14.2 %collective-permute-done.2 = bf16[128,1536]{1,0:T(8,128)(2,1)S(1)} collective-permute-done((bf16[128,1536]{1,0:T(8,128)(2,1)S(1)}, bf16[128,1536]{1,0:T(8,128)(2,1)S(1)}, u32[]{:S(2)}, u32[]{:S(2)}) %collective-permute-start.2) | collective-permute-done | bytes 393248 | tf_op jit(solution)/shard_map/ppermute | solution.py:83
  72.3 30.9 %all-to-all-done.2 = bf16[4,2,128,1536]{3,2,1,0:T(8,128)(2,1)S(1)} async-done(((bf16[4,2,128,1536]{3,2,1,0:T(8,128)(2,1)}), bf16[4,2,128,1536]{3,2,1,0:T(8,128)(2,1)S(1)}, u32[]{:S(2)}, u32[]{:S(2)}) %all-to-all-start.2) | async-done | bytes 3145760 | tf_op jit(solution)/shard_map/all_to_all | solution.py:79
  115.5 31.1 %all-to-all-done.5 = bf16[8,96,1536]{2,1,0:T(8,128)(2,1)} async-done(((bf16[8,96,1536]{2,1,0:T(8,128)(2,1)}), bf16[8,96,1536]{2,1,0:T(8,128)(2,1)}, u32[]{:S(2)}, u32[]{:S(2)}) %all-to-all-start.5) | async-done | bytes 2359328 | tf_op jit(solution)/shard_map/all_to_all | solution.py:79
  154.6 15.2 %all-to-all-done.3 = bf16[4,128,1024]{1,2,0:T(8,128)(2,1)S(1)} async-done(((bf16[4,128,1024]{1,2,0:T(8,128)(2,1)}), bf16[4,128,1024]{1,2,0:T(8,128)(2,1)S(1)}, u32[]{:S(2)}, u32[]{:S(2)}) %all-to-all-start.3) | async-done | bytes 1048608 | tf_op jit(solution)/shard_map/all_to_all | solution.py:79
  174.4 14.8 %attend.1 = (f32[3,64,1024]{2,1,0:T(8,128)S(1)}, f32[3,1,1024]{2,1,0:T(1,128)S(1)}) custom-call(s32[1]{0:T(128)} %bitcast.block_ref, s32[1,512]{1,0:T(1,128)S(1)} %bitcast.224, s32[512,1]{1,0:T(8,128)S(1)} %copy.225.pos_col, bf16[3,64,1024]{2,1,0:T(8,128)(2,1)S(1)} %bitcast.217, bf16[8,512,64]{2,1,0:T(8,128)(2,1)S(1)} %get-tuple-element.191.k_ref, ...), custom_call_target="tpu_custom_call" | custom-call | flops 7247757312 | bytes 4194304 | tf_op jit(solution)/shard_map/attend/pallas_call | solution.py:164
  191.2 14.0 %all-to-all-start.4 = ((bf16[8,192,128]{2,1,0:T(8,128)(2,1)}), bf16[8,192,128]{2,1,0:T(8,128)(2,1)S(1)}, u32[]{:S(2)}, u32[]{:S(2)}) async-start(bf16[8,192,128]{2,1,0:T(8,128)(2,1)} %bitcast.23), calls=%async_computation.4 | async-start | bytes 786432 | tf_op jit(solution)/shard_map/all_to_all | solution.py:79
  206.3 7.6 %all-to-all-done.4 = bf16[8,192,128]{2,1,0:T(8,128)(2,1)S(1)} async-done(((bf16[8,192,128]{2,1,0:T(8,128)(2,1)}), bf16[8,192,128]{2,1,0:T(8,128)(2,1)S(1)}, u32[]{:S(2)}, u32[]{:S(2)}) %all-to-all-start.4) | async-done | bytes 393248 | tf_op jit(solution)/shard_map/all_to_all | solution.py:79
  228.5 8.8 %collective-permute-done.7 = bf16[128,1536]{1,0:T(8,128)(2,1)S(1)} collective-permute-done((bf16[128,1536]{1,0:T(8,128)(2,1)S(1)}, bf16[128,1536]{1,0:T(8,128)(2,1)S(1)}, u32[]{:S(2)}, u32[]{:S(2)}) %collective-permute-start.7) | collective-permute-done | bytes 393248 | tf_op jit(solution)/shard_map/ppermute | solution.py:83
  237.4 23.6 %all-to-all-done.6 = bf16[4,2,128,1664]{3,2,1,0:T(8,128)(2,1)} async-done(((bf16[4,2,128,1664]{3,2,1,0:T(8,128)(2,1)}), bf16[4,2,128,1664]{3,2,1,0:T(8,128)(2,1)}, u32[]{:S(2)}, u32[]{:S(2)}) %all-to-all-start.6) | async-done | bytes 3407904 | tf_op jit(solution)/shard_map/all_to_all | solution.py:79
  274.2 28.8 %all-to-all-done.7 = bf16[4,2,128,1536]{3,2,1,0:T(8,128)(2,1)S(1)} async-done(((bf16[4,2,128,1536]{3,2,1,0:T(8,128)(2,1)}), bf16[4,2,128,1536]{3,2,1,0:T(8,128)(2,1)S(1)}, u32[]{:S(2)}, u32[]{:S(2)}) %all-to-all-start.7) | async-done | bytes 3145760 | tf_op jit(solution)/shard_map/all_to_all | solution.py:79
  306.2 34.2 %experts.1 = (bf16[8,128,1664]{2,1,0:T(8,128)(2,1)}, bf16[5,384,1536]{2,1,0:T(8,128)(2,1)}, bf16[5,384,1536]{2,1,0:T(8,128)(2,1)}, bf16[5,384,512]{2,1,0:T(8,128...) custom-call(s32[1]{0:T(128)} %bitcast.34.first_ref, s32[5,8,128]{2,1,0:T(8,128)} %fusion.11.rank_ref, ...), custom_call_target="tpu_custom_call" | custom-call | flops 15000000512 | bytes 62914560 | tf_op jit(solution)/shard_map/experts/pallas_call | solution.py:306
  344.1 18.4 %expert_grads.1 = bf16[16,5,96,1536]{3,2,1,0:T(8,128)(2,1)} custom-call(bf16[5,384,1536]{2,1,0:T(8,128)(2,1)} %get-tuple-element.39.rows_ref, bf16[5,384,1536]{2,1,0:T(8,128)(2,1)} %get-tuple-element.40.slot_ref, bf16[5,384,512]{2,1,0:T(8,128)(2,1)S(1)} %copy-done, bf16[5,384,1024]{2,1,0:T(8,128)(2,1)S(1)} %copy-done.2), custom_call_target="tpu_custom_call" | custom-call | flops 8999999488 | bytes 47185920 | tf_op jit(solution)/shard_map/expert_grads/pallas_call | solution.py:351
  364.3 10.6 %mixture.1 = bf16[8,128,1536]{2,1,0:T(8,128)(2,1)S(1)} custom-call(s32[5,8,128]{2,1,0:T(8,128)S(1)} %copy-done.11, bf16[5,384,512]{2,1,0:T(8,128)(2,1)S(1)} %copy-done.1, f32[5,384,128]{2,1,0:T(8,128)S(1)} %copy-done.4, bf16[16,5,96,1536]{3,2,1,0:T(8,128)(2,1)} %bitcast.228), custom_call_target="tpu_custom_call" | custom-call | flops 4000000000 | bytes 20971520 | tf_op jit(solution)/shard_map/mixture/pallas_call | solution.py:384
  375.0 38.2 %all_to_all.80 = bf16[4,2,128,1536]{3,2,1,0:T(8,128)(2,1)S(1)} all-to-all(bf16[4,2,128,1536]{3,2,1,0:T(8,128)(2,1)S(1)} %bitcast.216), channel_id=1, replica_groups=mesh['zh'=2,'co'=2,'blk'=4,'x'=4,'zl'=2] {'x'}, dimensions={0} | all-to-all | bytes 6291456 | tf_op jit(solution)/shard_map/all_to_all | solution.py:79
  423.4 32.4 %all-to-all-done.9 = bf16[4,2,128,1664]{3,2,1,0:T(8,128)(2,1)} async-done(((bf16[4,2,128,1664]{3,2,1,0:T(8,128)(2,1)}), bf16[4,2,128,1664]{3,2,1,0:T(8,128)(2,1)}, u32[]{:S(2)}, u32[]{:S(2)}) %all-to-all-start.9) | async-done | bytes 3407904 | tf_op jit(solution)/shard_map/all_to_all | solution.py:79
  461.0 19.6 %collective-permute-done.10 = bf16[128,1664]{1,0:T(8,128)(2,1)S(1)} collective-permute-done((bf16[128,1664]{1,0:T(8,128)(2,1)S(1)}, bf16[128,1664]{1,0:T(8,128)(2,1)S(1)}, u32[]{:S(2)}, u32[]{:S(2)}) %collective-permute-start.10) | collective-permute-done | bytes 426016 | tf_op jit(solution)/shard_map/ppermute | solution.py:83
  482.8 7.8 %collective-permute-done.8 = bf16[128,1536]{1,0:T(8,128)(2,1)S(1)} collective-permute-done((bf16[128,1536]{1,0:T(8,128)(2,1)S(1)}, bf16[128,1536]{1,0:T(8,128)(2,1)S(1)}, u32[]{:S(2)}, u32[]{:S(2)}) %collective-permute-start.8) | collective-permute-done | bytes 393248 | tf_op jit(solution)/shard_map/ppermute | solution.py:83
  499.4 5.9 all-to-all-done.10
  510.4 22.5 %attend_back.1 = (bf16[3,64,1024]{2,1,0:T(8,128)(2,1)S(1)}, bf16[8,512,64]{2,1,0:T(8,128)(2,1)S(1)}, bf16[8,512,64]{2,1,0:T(8,128)(2,1)}) custom-call(s32[1]{0:T(128)} %bitcast.block_ref, s32[1,512]{1,0:T(1,128)S(1)} %bitcast.225, s32[512,1]{1,0:T(8,128)S(1)} %copy-done.10, bf16[3,64,1024]{2,1,0:T(8,128)(2,1)S(1)} %bitcast.219, ...), custom_call_target="tpu_custom_call" | custom-call | flops 18119393280 | bytes 8388608 | tf_op jit(solution)/shard_map/attend_back/pallas_call | solution.py:227
  540.9 7.8 %collective-permute-done.13 = bf16[128,1536]{1,0:T(8,128)(2,1)S(1)} collective-permute-done((bf16[128,1536]{1,0:T(8,128)(2,1)S(1)}, bf16[128,1536]{1,0:T(8,128)(2,1)S(1)}, u32[]{:S(2)}, u32[]{:S(2)}) %collective-permute-start.13) | collective-permute-done | bytes 393248 | tf_op jit(solution)/shard_map/ppermute | solution.py:83
  548.8 11.6 %all-to-all-done.11 = bf16[4,1024,128]{2,1,0:T(8,128)(2,1)S(1)} async-done(((bf16[4,1024,128]{2,1,0:T(8,128)(2,1)}), bf16[4,1024,128]{2,1,0:T(8,128)(2,1)S(1)}, u32[]{:S(2)}, u32[]{:S(2)}) %all-to-all-start.11) | async-done | bytes 1048608 | tf_op jit(solution)/shard_map/all_to_all | solution.py:79
  574.2 22.7 %all-to-all-done.13 = bf16[4,2,128,1536]{3,2,1,0:T(8,128)(2,1)} async-done(((bf16[4,2,128,1536]{3,2,1,0:T(8,128)(2,1)}), bf16[4,2,128,1536]{3,2,1,0:T(8,128)(2,1)}, u32[]{:S(2)}, u32[]{:S(2)}) %all-to-all-start.13) | async-done | bytes 3145760 | tf_op jit(solution)/shard_map/all_to_all | solution.py:79
  615.9 12.5 %all-to-all-done.12 = bf16[4,2,128,1536]{3,2,1,0:T(8,128)(2,1)} async-done(((bf16[4,2,128,1536]{3,2,1,0:T(8,128)(2,1)}), bf16[4,2,128,1536]{3,2,1,0:T(8,128)(2,1)}, u32[]{:S(2)}, u32[]{:S(2)}) %all-to-all-start.12) | async-done | bytes 3145760 | tf_op jit(solution)/shard_map/all_to_all | solution.py:79
  632.0 7.4 %collective-permute-start.9 = (f32[128,1536]{1,0:T(8,128)}, f32[128,1536]{1,0:T(8,128)}, u32[]{:S(2)}, u32[]{:S(2)}) collective-permute-start(f32[128,1536]{1,0:T(8,128)} %get-tuple-element.194), channel_id=1, source_target_pairs={{0,0},{2,2},{4,28},{6,30},{8,8},{10,10},{12,20},{14,22},{16,16},{1... | collective-permute-start | bytes 2359304 | tf_op jit(solution)/shard_map/ppermute | solution.py:92
  641.9 9.0 %all-to-all-start.14 = ((bf16[8,96,640]{2,1,0:T(8,128)(2,1)}), bf16[8,96,640]{2,1,0:T(8,128)(2,1)S(1)}, u32[]{:S(2)}, u32[]{:S(2)}) async-start(bf16[8,96,640]{2,1,0:T(8,128)(2,1)} %bitcast.242), calls=%async_computation.14 | async-start | bytes 1966080 | tf_op jit(solution)/shard_map/all_to_all | solution.py:79
  656.3 7.3 %all-to-all-done.14 = bf16[8,96,640]{2,1,0:T(8,128)(2,1)S(1)} async-done(((bf16[8,96,640]{2,1,0:T(8,128)(2,1)}), bf16[8,96,640]{2,1,0:T(8,128)(2,1)S(1)}, u32[]{:S(2)}, u32[]{:S(2)}) %all-to-all-start.14) | async-done | bytes 983072 | tf_op jit(solution)/shard_map/all_to_all | solution.py:79
  664.5 9.4 %all-to-all-start.15 = ((bf16[8,12,640]{2,1,0:T(8,128)(2,1)}), bf16[8,12,640]{2,1,0:T(8,128)(2,1)S(1)}, u32[]{:S(2)}, u32[]{:S(2)}) async-start(bf16[8,12,640]{2,1,0:T(8,128)(2,1)} %reshape.406), calls=%async_computation.15 | async-start | bytes 327680 | tf_op jit(solution)/shard_map/all_to_all | solution.py:79
  673.9 6.5 all-to-all-done.15
  694.9 6.3 multiply_subtract_fusion
  (365 shorter events, 196.2 us)
Async XLA Ops:
  7.2 299.0 %all-gather.2.cloned.1.call-start = ((), (), s32[]{:S(2)}) async-start(), calls=%async_computation.17 | async-start | bytes 25067520 | tf_op jit(solution)/shard_map/all_gather | solution.py:415
  11.5 12.2 %collective-permute-start = (bf16[128,1536]{1,0:T(8,128)(2,1)S(1)}, bf16[128,1536]{1,0:T(8,128)(2,1)S(1)}, u32[]{:S(2)}, u32[]{:S(2)}) collective-permute-start(bf16[128,1536]{1,0:T(8,128)(2,1)S(1)} %copy-done.75), channel_id=1, source_target_pairs={{0,0},{2,2},{4,28},{6,30},{8,8},{10,10},{12,20},{14,22},{16,16},{1... | collective-permute-start | bytes 1179656 | tf_op jit(solution)/shard_map/ppermute | solution.py:92
  13.8 19.8 %all-to-all-start = ((bf16[8,12,1920]{2,1,0:T(8,128)(2,1)}), bf16[8,12,1920]{2,1,0:T(8,128)(2,1)S(1)}, u32[]{:S(2)}, u32[]{:S(2)}) async-start(bf16[8,12,1920]{2,1,0:T(8,128)(2,1)} %concatenate.50), calls=%async_computation | async-start | bytes 983040 | tf_op jit(solution)/shard_map/all_to_all | solution.py:79
  23.7 30.5 %collective-permute-start.2 = (bf16[128,1536]{1,0:T(8,128)(2,1)S(1)}, bf16[128,1536]{1,0:T(8,128)(2,1)S(1)}, u32[]{:S(2)}, u32[]{:S(2)}) collective-permute-start(bf16[128,1536]{1,0:T(8,128)(2,1)S(1)} %collective-permute-done), channel_id=1, source_target_pairs={{0,1},{1,0},{2,3},{3,2},{4,5},{5,4},{6,7},{7,6},{8,9},{9,8},{10,11... | collective-permute-start | bytes 1179656 | tf_op jit(solution)/shard_map/ppermute | solution.py:83
  34.6 24.5 %all-to-all-start.1 = ((bf16[8,96,384]{2,1,0:T(8,128)(2,1)}), bf16[8,96,384]{2,1,0:T(8,128)(2,1)S(1)}, u32[]{:S(2)}, u32[]{:S(2)}) async-start(bf16[8,96,384]{2,1,0:T(8,128)(2,1)} %broadcast_in_dim.48), calls=%async_computation.1 | async-start | bytes 1179648 | tf_op jit(solution)/shard_map/all_to_all | solution.py:79
  61.2 42.0 %all-to-all-start.2 = ((bf16[4,2,128,1536]{3,2,1,0:T(8,128)(2,1)}), bf16[4,2,128,1536]{3,2,1,0:T(8,128)(2,1)S(1)}, u32[]{:S(2)}, u32[]{:S(2)}) async-start(bf16[4,2,128,1536]{3,2,1,0:T(8,128)(2,1)} %broadcast_in_dim.49), calls=%async_computation.2 | async-start | bytes 6291456 | tf_op jit(solution)/shard_map/all_to_all | solution.py:79
  65.5 3.6 collective-permute-start.1
  106.0 40.5 %all-to-all-start.5 = ((bf16[8,96,1536]{2,1,0:T(8,128)(2,1)}), bf16[8,96,1536]{2,1,0:T(8,128)(2,1)}, u32[]{:S(2)}, u32[]{:S(2)}) async-start(bf16[8,96,1536]{2,1,0:T(8,128)(2,1)} %broadcast_in_dim.55), calls=%async_computation.5 | async-start | bytes 4718592 | tf_op jit(solution)/shard_map/all_to_all | solution.py:79
  147.6 22.1 %all-to-all-start.3 = ((bf16[4,128,1024]{1,2,0:T(8,128)(2,1)}), bf16[4,128,1024]{1,2,0:T(8,128)(2,1)S(1)}, u32[]{:S(2)}, u32[]{:S(2)}) async-start(bf16[4,128,1024]{1,2,0:T(8,128)(2,1)} %broadcast_in_dim.53), calls=%async_computation.3 | async-start | bytes 2097152 | tf_op jit(solution)/shard_map/all_to_all | solution.py:79
  151.2 2.3 collective-permute-start.4
  151.9 0.9 collective-permute-start.5
  154.5 50.6 %collective-permute-start.6 = (bf16[128,1664]{1,0:T(8,128)(2,1)}, bf16[128,1664]{1,0:T(8,128)(2,1)}, u32[]{:S(2)}, u32[]{:S(2)}) collective-permute-start(bf16[128,1664]{1,0:T(8,128)(2,1)} %get-tuple-element.196), channel_id=1, source_target_pairs={{0,1},{1,0},{2,3},{3,2},{4,5},{5,4},{6,7},{7,6},{8,9},{9,8},{10,11... | collective-permute-start | bytes 1277960 | tf_op jit(solution)/shard_map/ppermute | solution.py:83
  154.6 66.1 %collective-permute-start.3 = (bf16[8,96,1536]{2,1,0:T(8,128)(2,1)}, bf16[8,96,1536]{2,1,0:T(8,128)(2,1)}, u32[]{:S(2)}, u32[]{:S(2)}) collective-permute-start(bf16[8,96,1536]{2,1,0:T(8,128)(2,1)} %all-to-all-done.5), channel_id=1, source_target_pairs={{0,32},{32,0},{1,33},{33,1},{2,34},{34,2},{3,35},{35,3},{4,36},{36... | collective-permute-start | bytes 7077896 | tf_op jit(solution)/shard_map/ppermute | solution.py:83
  191.2 22.7 %all-to-all-start.4 = ((bf16[8,192,128]{2,1,0:T(8,128)(2,1)}), bf16[8,192,128]{2,1,0:T(8,128)(2,1)S(1)}, u32[]{:S(2)}, u32[]{:S(2)}) async-start(bf16[8,192,128]{2,1,0:T(8,128)(2,1)} %bitcast.23), calls=%async_computation.4 | async-start | bytes 786432 | tf_op jit(solution)/shard_map/all_to_all | solution.py:79
  216.0 45.0 %all-to-all-start.6 = ((bf16[4,2,128,1664]{3,2,1,0:T(8,128)(2,1)}), bf16[4,2,128,1664]{3,2,1,0:T(8,128)(2,1)}, u32[]{:S(2)}, u32[]{:S(2)}) async-start(bf16[4,2,128,1664]{3,2,1,0:T(8,128)(2,1)} %broadcast_in_dim.57), calls=%async_computation.6 | async-start | bytes 6815744 | tf_op jit(solution)/shard_map/all_to_all | solution.py:79
  226.8 10.5 %collective-permute-start.7 = (bf16[128,1536]{1,0:T(8,128)(2,1)S(1)}, bf16[128,1536]{1,0:T(8,128)(2,1)S(1)}, u32[]{:S(2)}, u32[]{:S(2)}) collective-permute-start(bf16[128,1536]{1,0:T(8,128)(2,1)S(1)} %multiply_convert_fusion.1), channel_id=1, source_target_pairs={{0,1},{1,0},{2,3},{3,2},{4,5},{5,4},{6,7},{7,6},{8,9},{9,8},{10,11... | collective-permute-start | bytes 1179656 | tf_op jit(solution)/shard_map/ppermute | solution.py:83
  262.9 40.2 %all-to-all-start.7 = ((bf16[4,2,128,1536]{3,2,1,0:T(8,128)(2,1)}), bf16[4,2,128,1536]{3,2,1,0:T(8,128)(2,1)S(1)}, u32[]{:S(2)}, u32[]{:S(2)}) async-start(bf16[4,2,128,1536]{3,2,1,0:T(8,128)(2,1)} %broadcast_in_dim.62), calls=%async_computation.7 | async-start | bytes 6291456 | tf_op jit(solution)/shard_map/all_to_all | solution.py:79
  266.6 428.2 %reduce-scatter.2.cloned.1.call-start = ((), (), s32[]{:S(2)}) async-start(), calls=%async_computation.18 | async-start | bytes 25067520 | tf_op jit(solution)/shard_map/reduce_scatter | solution.py:518
  413.2 42.6 %all-to-all-start.9 = ((bf16[4,2,128,1664]{3,2,1,0:T(8,128)(2,1)}), bf16[4,2,128,1664]{3,2,1,0:T(8,128)(2,1)}, u32[]{:S(2)}, u32[]{:S(2)}) async-start(bf16[4,2,128,1664]{3,2,1,0:T(8,128)(2,1)} %bitcast.245), calls=%async_computation.9 | async-start | bytes 6815744 | tf_op jit(solution)/shard_map/all_to_all | solution.py:79
  458.7 21.9 %collective-permute-start.10 = (bf16[128,1664]{1,0:T(8,128)(2,1)S(1)}, bf16[128,1664]{1,0:T(8,128)(2,1)S(1)}, u32[]{:S(2)}, u32[]{:S(2)}) collective-permute-start(bf16[128,1664]{1,0:T(8,128)(2,1)S(1)} %fusion.33), channel_id=1, source_target_pairs={{0,1},{1,0},{2,3},{3,2},{4,5},{5,4},{6,7},{7,6},{8,9},{9,8},{10,11... | collective-permute-start | bytes 1277960 | tf_op jit(solution)/shard_map/ppermute | solution.py:83
  459.7 30.9 %collective-permute-start.8 = (bf16[128,1536]{1,0:T(8,128)(2,1)S(1)}, bf16[128,1536]{1,0:T(8,128)(2,1)S(1)}, u32[]{:S(2)}, u32[]{:S(2)}) collective-permute-start(bf16[128,1536]{1,0:T(8,128)(2,1)S(1)} %fusion.35), channel_id=1, source_target_pairs={{0,1},{1,0},{2,3},{3,2},{4,5},{5,4},{6,7},{7,6},{8,9},{9,8},{10,11... | collective-permute-start | bytes 1179656 | tf_op jit(solution)/shard_map/ppermute | solution.py:83
  494.3 11.0 %all-to-all-start.10 = ((bf16[8,192,128]{2,1,0:T(8,128)(2,1)}), bf16[8,192,128]{2,1,0:T(8,128)(2,1)S(1)}, u32[]{:S(2)}, u32[]{:S(2)}) async-start(bf16[8,192,128]{2,1,0:T(8,128)(2,1)} %bitcast.51), calls=%async_computation.10 | async-start | bytes 786432 | tf_op jit(solution)/shard_map/all_to_all | solution.py:79
  535.9 24.5 %all-to-all-start.11 = ((bf16[4,1024,128]{2,1,0:T(8,128)(2,1)}), bf16[4,1024,128]{2,1,0:T(8,128)(2,1)S(1)}, u32[]{:S(2)}, u32[]{:S(2)}) async-start(bf16[4,1024,128]{2,1,0:T(8,128)(2,1)} %pad_maximum_fusion.3), calls=%async_computation.11 | async-start | bytes 2097152 | tf_op jit(solution)/shard_map/all_to_all | solution.py:79
  539.5 9.2 %collective-permute-start.13 = (bf16[128,1536]{1,0:T(8,128)(2,1)S(1)}, bf16[128,1536]{1,0:T(8,128)(2,1)S(1)}, u32[]{:S(2)}, u32[]{:S(2)}) collective-permute-start(bf16[128,1536]{1,0:T(8,128)(2,1)S(1)} %get-tuple-element.166), channel_id=1, source_target_pairs={{0,1},{1,0},{2,3},{3,2},{4,5},{5,4},{6,7},{7,6},{8,9},{9,8},{10,11... | collective-permute-start | bytes 1179656 | tf_op jit(solution)/shard_map/ppermute | solution.py:83
  562.3 34.6 %all-to-all-start.13 = ((bf16[4,2,128,1536]{3,2,1,0:T(8,128)(2,1)}), bf16[4,2,128,1536]{3,2,1,0:T(8,128)(2,1)}, u32[]{:S(2)}, u32[]{:S(2)}) async-start(bf16[4,2,128,1536]{3,2,1,0:T(8,128)(2,1)} %broadcast_in_dim.65), calls=%async_computation.13 | async-start | bytes 6291456 | tf_op jit(solution)/shard_map/all_to_all | solution.py:79
  596.9 31.4 %all-to-all-start.12 = ((bf16[4,2,128,1536]{3,2,1,0:T(8,128)(2,1)}), bf16[4,2,128,1536]{3,2,1,0:T(8,128)(2,1)}, u32[]{:S(2)}, u32[]{:S(2)}) async-start(bf16[4,2,128,1536]{3,2,1,0:T(8,128)(2,1)} %bitcast.73), calls=%async_computation.12 | async-start | bytes 6291456 | tf_op jit(solution)/shard_map/all_to_all | solution.py:79
  615.6 23.8 %collective-permute-start.14 = (bf16[2,4,96,640]{3,2,1,0:T(8,128)(2,1)}, bf16[2,4,96,640]{3,2,1,0:T(8,128)(2,1)}, u32[]{:S(2)}, u32[]{:S(2)}) collective-permute-start(bf16[2,4,96,640]{3,2,1,0:T(8,128)(2,1)} %fusion.17), channel_id=1, source_target_pairs={{0,32},{32,0},{1,33},{33,1},{2,34},{34,2},{3,35},{35,3},{4,36},{36... | collective-permute-start | bytes 2949128 | tf_op jit(solution)/shard_map/ppermute | solution.py:83
  631.7 19.2 %collective-permute-start.11 = (bf16[128,1536]{1,0:T(8,128)(2,1)}, bf16[128,1536]{1,0:T(8,128)(2,1)}, u32[]{:S(2)}, u32[]{:S(2)}) collective-permute-start(bf16[128,1536]{1,0:T(8,128)(2,1)} %fusion.36), channel_id=1, source_target_pairs={{0,1},{1,0},{2,3},{3,2},{4,5},{5,4},{6,7},{7,6},{8,9},{9,8},{10,11... | collective-permute-start | bytes 1179656 | tf_op jit(solution)/shard_map/ppermute | solution.py:83
  632.0 41.9 %collective-permute-start.9 = (f32[128,1536]{1,0:T(8,128)}, f32[128,1536]{1,0:T(8,128)}, u32[]{:S(2)}, u32[]{:S(2)}) collective-permute-start(f32[128,1536]{1,0:T(8,128)} %get-tuple-element.194), channel_id=1, source_target_pairs={{0,0},{2,2},{4,28},{6,30},{8,8},{10,10},{12,20},{14,22},{16,16},{1... | collective-permute-start | bytes 2359304 | tf_op jit(solution)/shard_map/ppermute | solution.py:92
  641.9 21.8 %all-to-all-start.14 = ((bf16[8,96,640]{2,1,0:T(8,128)(2,1)}), bf16[8,96,640]{2,1,0:T(8,128)(2,1)S(1)}, u32[]{:S(2)}, u32[]{:S(2)}) async-start(bf16[8,96,640]{2,1,0:T(8,128)(2,1)} %bitcast.242), calls=%async_computation.14 | async-start | bytes 1966080 | tf_op jit(solution)/shard_map/all_to_all | solution.py:79
  654.5 19.4 %collective-permute-start.12 = (f32[128,1536]{1,0:T(8,128)}, f32[128,1536]{1,0:T(8,128)S(1)}, u32[]{:S(2)}, u32[]{:S(2)}) collective-permute-start(f32[128,1536]{1,0:T(8,128)} %fusion.25), channel_id=1, source_target_pairs={{0,0},{2,2},{4,28},{6,30},{8,8},{10,10},{12,20},{14,22},{16,16},{1... | collective-permute-start | bytes 2359304 | tf_op jit(solution)/shard_map/ppermute | solution.py:92
  664.5 15.9 %all-to-all-start.15 = ((bf16[8,12,640]{2,1,0:T(8,128)(2,1)}), bf16[8,12,640]{2,1,0:T(8,128)(2,1)S(1)}, u32[]{:S(2)}, u32[]{:S(2)}) async-start(bf16[8,12,640]{2,1,0:T(8,128)(2,1)} %reshape.406), calls=%async_computation.15 | async-start | bytes 327680 | tf_op jit(solution)/shard_map/all_to_all | solution.py:79
  (80 other events, 1150.2 us)
Sparse Core Ops, SparseCore 0:
  11.6 195.7 all-gather.1
  362.7 202.0 reduce-scatter.1

commit v2 on v1

v2 whole, which is shorter than its diff:
```python
import functools

import jax
import jax.numpy as jnp
from jax import lax
from jax.experimental import pallas as pl
from jax.experimental.pallas import tpu as pltpu
from jax.sharding import Mesh
from jax.sharding import PartitionSpec as P

D = 1536
HQ = 24
HK = 8
HD = 64
F = 512
EXPERTS = 40
TOPK = 8
ADAM_STEP = 10
CAP = 48
TOK = 128
GROUP = 8
LOCAL_E = 5
SPAN = 1024
ROWS = 80
CHUNK = 512
QW = 192
SLOTS = GROUP * CAP
HALF = HD // 2
EXTRA = 128
VMEM_LIMIT = 60 << 20
WIDE = 640
ROUTER_AT = 64
GAIN_AT = 104

bf16 = jnp.bfloat16
f32 = jnp.float32
attention_scale = 0.015625
residual_scale = 0.22
norm_epsilon = 1e-06
rope_base = 10000.0
beta_first = 0.9
beta_second = 0.95
adam_epsilon = 1e-08
weight_decay = 0.1
rate_project_in = 0.2
rate_project_out = 2.0
rate_router = 0.03
rate_gains = 0.5
rate_expert_up = 0.05
rate_expert_down = 2.0
log2_e = 1.4426950408889634

ULYS = ("x", "zl")
ALL = ("zh", "co", "blk", "x", "zl")
DPBLK = ("zh", "co", "blk")


def dot(a, b, dims):
    return lax.dot_general(a, b, ((dims[0], dims[1]), ((), ())), preferred_element_type=f32)


def rms_scale(rows_in):
    return lax.rsqrt(jnp.mean(rows_in * rows_in, axis=1, keepdims=True) + norm_epsilon)


def norm_back(rows_in, scale_in, gain_in, grad_in):
    weighted = grad_in * gain_in
    inner_sum = jnp.mean(weighted * rows_in, axis=1, keepdims=True)
    return scale_in * weighted - rows_in * (scale_in * scale_in * scale_in) * inner_sum


def adam_update(weight, first_moment, second, gradient, step_rate):
    first_new = beta_first * first_moment + (1.0 - beta_first) * gradient
    second_new = beta_second * second + (1.0 - beta_second) * gradient * gradient
    first_hat = first_new / (1.0 - beta_first**ADAM_STEP)
    second_hat = second_new / (1.0 - beta_second**ADAM_STEP)
    weight_new = weight - step_rate * (
        first_hat / (jnp.sqrt(second_hat) + adam_epsilon) + weight_decay * weight
    )
    return (weight_new, first_new, second_new)


def a2a(value, axes):
    return lax.all_to_all(value, axes, split_axis=0, concat_axis=0, tiled=True)


def trade(value, axis, mask):
    return lax.ppermute(value, axis, [(i, i ^ mask) for i in range(2 if axis in ("zl", "co", "zh") else 4)])


def after(value, *others):
    return lax.optimization_barrier((value,) + others)[0]


def spread(near, partner):
    a0 = trade(near, "x", 1)
    b0 = trade(near, "x", 3)
    far0 = trade(near, "x", 2)
    b1 = trade(partner, "x", 3)
    a1 = trade(partner, "x", 1)
    far1 = trade(partner, "x", 2)
    return [near, partner, a0, a1, far0, far1, b0, b1]


def collect(blocks, gate=None, last=None):
    to3 = trade(blocks[5], "x", 3)
    to1 = trade(blocks[4], "x", 1)
    got3_1 = trade(blocks[7], "x", 3)
    got1_0 = trade(blocks[2], "x", 1)
    if gate is not None:
        to3, to1, _ = lax.optimization_barrier((to3, to1, gate))
    send1 = (blocks[3].astype(f32) + to3.astype(f32)).astype(bf16)
    send3 = (blocks[6].astype(f32) + to1.astype(f32)).astype(bf16)
    got1_1 = trade(send1, "x", 1)
    got3_0 = trade(send3, "x", 3)
    if last is not None:
        got1_1 = after(got1_1, last)
    other = (blocks[1].astype(f32) + got1_1.astype(f32) + got3_1.astype(f32)).astype(bf16)
    other = trade(other, "zl", 1)
    return (blocks[0], got1_0, got3_0, other)


def total_of(parts):
    return sum(part.astype(f32) for part in parts)


def vmem_specs(count):
    return [pl.BlockSpec(memory_space=pltpu.VMEM)] * count


NO_COST = pl.CostEstimate(flops=0, bytes_accessed=0, transcendentals=0)
SCALARS = pl.BlockSpec(memory_space=pltpu.SMEM)


def project_kernel(info_ref, mine_ref, other_ref, cos_ref, sin_ref, *refs):
    xs = refs[:4]
    near_ref, tail_ref, normed_ref, q_ref, kv_ref, mixed = refs[4:]
    for zh in range(2):
        for blk in range(4):
            own = (zh * 2 + info_ref[3]) * 4 + blk
            far = (zh * 2 + 1 - info_ref[3]) * 4 + blk
            near_ref[own] = mine_ref[zh * 4 + blk]
            near_ref[far] = other_ref[zh * 4 + blk]
    near = near_ref[...].reshape(D, WIDE)
    tail_ref[...] = near[:, 512:].astype(f32).T
    gain = tail_ref[GAIN_AT : GAIN_AT + 1, :]
    weights = near[:, : QW + 2 * HD]
    for at in range(GROUP):
        span = slice(at * TOK, (at + 1) * TOK)
        rows = xs[at // 2][at % 2].astype(f32)
        normed = (rows * rms_scale(rows) * gain).astype(bf16)
        normed_ref[span] = normed
        mixed[:, span] = dot(normed, weights, ((1,), (0,))).T
    cosine = cos_ref[...]
    sine = sin_ref[...]
    for head in range(4):
        low = mixed[head * HD : head * HD + HALF]
        high = mixed[head * HD + HALF : (head + 1) * HD]
        low_out = (low * cosine - high * sine).astype(bf16)
        high_out = (high * cosine + low * sine).astype(bf16)
        if head < 3:
            q_ref[head, :HALF] = low_out
            q_ref[head, HALF:] = high_out
        else:
            kv_ref[:HALF] = low_out
            kv_ref[HALF:HD] = high_out
    kv_ref[HD:] = mixed[4 * HD :].astype(bf16)


def project(info, mine, other, cosine, sine, token_pairs):
    return pl.pallas_call(
        project_kernel,
        out_shape=(
            jax.ShapeDtypeStruct((16, 96, WIDE), bf16),
            jax.ShapeDtypeStruct((128, D), f32),
            jax.ShapeDtypeStruct((SPAN, D), bf16),
            jax.ShapeDtypeStruct((3, HD, SPAN), bf16),
            jax.ShapeDtypeStruct((2 * HD, SPAN), bf16),
        ),
        in_specs=[SCALARS] + vmem_specs(8),
        out_specs=tuple(vmem_specs(5)),
        scratch_shapes=[pltpu.VMEM((QW + 2 * HD, SPAN), f32)],
        compiler_params=pltpu.CompilerParams(vmem_limit_bytes=VMEM_LIMIT),
        cost_estimate=NO_COST,
        name="project",
    )(info, mine, other, cosine, sine, *token_pairs)


def chunk_place(info_ref, chunk):
    source = jnp.bitwise_xor(chunk // 2, info_ref[0])
    return source * 2 + jnp.bitwise_xor(chunk % 2, info_ref[1])


def causal_parts(info_ref, part):
    for half in range(2):
        last = 2 * info_ref[0] + jnp.bitwise_xor(half, info_ref[1])
        part(half, half, True)

        def step(chunk, carry):
            part(half, chunk_place(info_ref, chunk), False)
            return carry

        lax.fori_loop(0, last, step, 0)


def attend_kernel(
    info_ref, pos_row, pos_col, q_ref, near_ref, kv0, kv1, kv2, kv3, out_ref, low_ref, log_ref, *refs
):
    branches = refs[:GROUP]
    keys, vals, acc, peak = refs[GROUP:]
    for source, kv in enumerate((kv0, kv1, kv2, kv3)):
        for half in range(2):
            cols = slice(half * CHUNK, (half + 1) * CHUNK)
            keys[source * 2 + half] = kv[:HD, cols].T
            vals[source * 2 + half, :HD] = kv[HD:, cols]
            vals[source * 2 + half, HD:] = jnp.ones((ROWS - HD, CHUNK), bf16)

    def run(follow):
        def part(half, at, masked):
            cols = slice(half * CHUNK, (half + 1) * CHUNK)
            key = keys[at]
            val = vals[at]
            for head in range(3):
                scores = dot(key, q_ref[head, :, cols], ((1,), (0,))) * (attention_scale * log2_e)
                if masked:
                    scores = jnp.where(pos_col[...] <= pos_row[...], scores, -jnp.inf)
                    now = jnp.max(scores, axis=0, keepdims=True)
                elif follow:
                    now = jnp.maximum(peak[head, :, cols], jnp.max(scores, axis=0, keepdims=True))
                else:
                    now = peak[head, :, cols]
                grown = dot(val, jnp.exp2(scores - now).astype(bf16), ((1,), (0,)))
                if masked:
                    acc[head, :, cols] = grown
                elif follow:
                    acc[head, :, cols] = acc[head, :, cols] * jnp.exp2(peak[head, :, cols] - now) + grown
                else:
                    acc[head, :, cols] += grown
                if masked or follow:
                    peak[head, :, cols] = now

        causal_parts(info_ref, part)

    run(False)
    odd = jnp.where(jnp.abs(acc[...]) < 1e37, 0.0, 1.0)

    @pl.when(jnp.sum(odd) > 0.0)
    def _():
        run(True)

    for head in range(3):
        total = acc[head, HD : HD + 1]
        result = acc[head, :HD] / total
        out_ref[head] = result
        log_ref[head] = peak[head] + jnp.log2(total)
        low_ref[head * HD : (head + 1) * HD] = result.astype(bf16)
    out_cols = near_ref[:, :, 384 : 384 + QW].reshape(D, QW)
    for at in range(GROUP):
        heads = low_ref[:, at * TOK : (at + 1) * TOK]
        branches[at][...] = dot(heads, out_cols, ((0,), (1,))).astype(bf16)


def attend(info, pos, q_t, near, kvs):
    return pl.pallas_call(
        attend_kernel,
        out_shape=(
            jax.ShapeDtypeStruct((3, HD, SPAN), f32),
            jax.ShapeDtypeStruct((QW, SPAN), bf16),
            jax.ShapeDtypeStruct((3, 1, SPAN), f32),
        )
        + (jax.ShapeDtypeStruct((TOK, D), bf16),) * GROUP,
        in_specs=[SCALARS] + vmem_specs(8),
        out_specs=tuple(vmem_specs(3 + GROUP)),
        scratch_shapes=[
            pltpu.VMEM((8, CHUNK, HD), bf16),
            pltpu.VMEM((8, ROWS, CHUNK), bf16),
            pltpu.VMEM((3, ROWS, SPAN), f32),
            pltpu.VMEM((3, 1, SPAN), f32),
        ],
        compiler_params=pltpu.CompilerParams(vmem_limit_bytes=VMEM_LIMIT),
        cost_estimate=NO_COST,
        name="attend",
    )(info, pos[None, :], pos[:, None], q_t, near, *kvs)


def attend_back_kernel(
    info_ref, pos_row, pos_col, qt_ref, near_ref, kv0, kv1, kv2, kv3, out_ref, log_ref, *refs
):
    grads = refs[:GROUP]
    dq_ref, dkv0, dkv1, dkv2, dkv3, qn, kn, kt, vn, gt, gn, dq_acc, dk_acc, dv_acc, inner = refs[GROUP:]
    for source, kv in enumerate((kv0, kv1, kv2, kv3)):
        for half in range(2):
            cols = slice(half * CHUNK, (half + 1) * CHUNK)
            kt[source * 2 + half] = kv[:HD, cols]
            kn[source * 2 + half] = kv[:HD, cols].T
            vn[source * 2 + half] = kv[HD:, cols].T
    out_cols = near_ref[:, :, 384 : 384 + QW].reshape(D, QW)
    for at in range(GROUP):
        span = slice(at * TOK, (at + 1) * TOK)
        grad = dot(grads[at][...], out_cols, ((1,), (0,)))
        grad_t = grad.T
        for head in range(3):
            gn[head, span] = grad[:, head * HD : (head + 1) * HD].astype(bf16)
            gt[head, :, span] = grad_t[head * HD : (head + 1) * HD].astype(bf16)
    dk_acc[...] = jnp.zeros_like(dk_acc)
    dv_acc[...] = jnp.zeros_like(dv_acc)
    for head in range(3):
        inner[head] = jnp.sum(gt[head].astype(f32) * out_ref[head], axis=0, keepdims=True)
        qn[head] = qt_ref[head].T

    dq_acc[...] = jnp.zeros_like(dq_acc)

    def part(half, at, masked):
        cols = slice(half * CHUNK, (half + 1) * CHUNK)
        keys = kn[at]
        keys_t = kt[at]
        vals = vn[at]
        for head in range(3):
            scores = dot(keys, qt_ref[head, :, cols], ((1,), (0,))) * (attention_scale * log2_e)
            probs = jnp.exp2(scores - log_ref[head, :, cols])
            if masked:
                probs = jnp.where(pos_col[...] <= pos_row[...], probs, 0.0)
            prob_grad = dot(vals, gt[head, :, cols], ((1,), (0,)))
            score_grad = (probs * (prob_grad - inner[head, :, cols])).astype(bf16)
            dv_acc[at] += dot(probs.astype(bf16), gn[head, cols], ((1,), (0,)))
            dk_acc[at] += dot(score_grad, qn[head, cols], ((1,), (0,)))
            dq_acc[head, :, cols] += dot(keys_t, score_grad, ((1,), (0,)))

    causal_parts(info_ref, part)
    dq_ref[...] = (dq_acc[...] * attention_scale).astype(bf16)
    for source, dkv in enumerate((dkv0, dkv1, dkv2, dkv3)):
        for half in range(2):
            rows = slice(half * CHUNK, (half + 1) * CHUNK)
            at = source * 2 + half
            both = jnp.concatenate([dk_acc[at] * attention_scale, dv_acc[at]], axis=1)
            dkv[rows] = both.astype(bf16)


def attend_back(info, pos, q_t, near, kvs, out_t, logs, branch_blocks):
    return pl.pallas_call(
        attend_back_kernel,
        out_shape=(jax.ShapeDtypeStruct((3, HD, SPAN), bf16),)
        + (jax.ShapeDtypeStruct((SPAN, 2 * HD), bf16),) * 4,
        in_specs=[SCALARS] + vmem_specs(10 + GROUP),
        out_specs=tuple(vmem_specs(5)),
        scratch_shapes=[
            pltpu.VMEM((3, SPAN, HD), bf16),
            pltpu.VMEM((8, CHUNK, HD), bf16),
            pltpu.VMEM((8, HD, CHUNK), bf16),
            pltpu.VMEM((8, CHUNK, HD), bf16),
            pltpu.VMEM((3, HD, SPAN), bf16),
            pltpu.VMEM((3, SPAN, HD), bf16),
            pltpu.VMEM((3, HD, SPAN), f32),
            pltpu.VMEM((8, CHUNK, HD), f32),
            pltpu.VMEM((8, CHUNK, HD), f32),
            pltpu.VMEM((3, 1, SPAN), f32),
        ],
        compiler_params=pltpu.CompilerParams(vmem_limit_bytes=VMEM_LIMIT),
        cost_estimate=NO_COST,
        name="attend_back",
    )(info, pos[None, :], pos[:, None], q_t, near, *kvs, out_t, logs, *branch_blocks)


def turn_back_kernel(near_ref, tail_ref, cos_ref, sin_ref, dq_ref, kv0, kv1, kv2, kv3, *refs):
    xs = refs[:4]
    outs = refs[4 : 4 + GROUP]
    mixed_ref, gain_ref, back = refs[4 + GROUP :]
    kv_sum = kv0[...].astype(f32) + kv1[...].astype(f32) + kv2[...].astype(f32) + kv3[...].astype(f32)
    kv_sum = kv_sum.astype(bf16).astype(f32).T
    cosine = cos_ref[...]
    sine = sin_ref[...]
    for head in range(4):
        part = dq_ref[head].astype(f32) if head < 3 else kv_sum[:HD]
        low = part[:HALF]
        high = part[HALF:]
        back[head * HD : head * HD + HALF] = low * cosine + high * sine
        back[head * HD + HALF : (head + 1) * HD] = high * cosine - low * sine
    back[4 * HD :] = kv_sum[HD:]
    mixed_ref[...] = back[...].T.astype(bf16)
    weights = near_ref[:, :, : QW + 2 * HD].reshape(D, QW + 2 * HD)
    gain = jnp.zeros((1, D), f32)
    for at in range(GROUP):
        span = slice(at * TOK, (at + 1) * TOK)
        normed_grad = dot(mixed_ref[span], weights, ((1,), (1,)))
        outs[at][...] = normed_grad.astype(bf16)
        rows = xs[at // 2][at % 2].astype(f32)
        gain = gain + jnp.sum(normed_grad * (rows * rms_scale(rows)), axis=0, keepdims=True)
    gain_ref[...] = gain


def turn_back(near, tail, cosine, sine, dq_t, kv_parts, token_pairs):
    return pl.pallas_call(
        turn_back_kernel,
        out_shape=(jax.ShapeDtypeStruct((TOK, D), bf16),) * GROUP
        + (jax.ShapeDtypeStruct((SPAN, QW + 2 * HD), bf16), jax.ShapeDtypeStruct((1, D), f32)),
        in_specs=vmem_specs(13),
        out_specs=tuple(vmem_specs(GROUP + 2)),
        scratch_shapes=[pltpu.VMEM((QW + 2 * HD, SPAN), f32)],
        compiler_params=pltpu.CompilerParams(vmem_limit_bytes=VMEM_LIMIT),
        cost_estimate=NO_COST,
        name="turn_back",
    )(near, tail, cosine, sine, dq_t, *kv_parts, *token_pairs)


def weight_grad_kernel(info_ref, normed_ref, mixed_ref, heads_ref, rest_ref, gain_ref, *refs):
    branches = refs[:GROUP]
    out_ref = refs[GROUP]
    in_grad = dot(normed_ref[...], mixed_ref[...], ((0,), (0,)))
    out_grad = jnp.zeros((384, QW), f32)
    for at in range(GROUP):
        heads = heads_ref[:, at * TOK : (at + 1) * TOK]
        out_grad = out_grad + dot(branches[at][...], heads, ((0,), (1,)))
    lane = lax.broadcasted_iota(jnp.int32, (384, 128), 1)
    column = jnp.broadcast_to(gain_ref[...], (128, 384)).T
    rest = jnp.where(lane == GAIN_AT, column, rest_ref[...])
    out_ref[0, 0, :, :, :320] = in_grad.astype(bf16).reshape(4, 96, 320)
    out_ref[0, 0, :, :, 320:384] = jnp.zeros((4, 96, 64), bf16)
    out_ref[0, 0, :, :, 384:512] = out_grad[:, :128].astype(bf16).reshape(4, 96, 128)
    last = jnp.concatenate([out_grad[:, 128:], rest[:, 64:]], axis=1)
    out_ref[0, 0, :, :, 512:] = last.astype(bf16).reshape(4, 96, 128)


def weight_grads(info, normed_all, mixed_grad, heads, rest, gain, branch_blocks):
    step = lambda r, zh, info: zh * 2 + jnp.bitwise_xor(info[3], r)
    fixed = lambda *shape: pl.BlockSpec(shape, lambda r, zh, info: (0,) * len(shape))
    return pl.pallas_call(
        weight_grad_kernel,
        grid_spec=pltpu.PrefetchScalarGridSpec(
            num_scalar_prefetch=1,
            grid=(2, 2),
            in_specs=[
                pl.BlockSpec((SPAN, 384), lambda r, zh, info: (0, step(r, zh, info))),
                fixed(SPAN, QW + 2 * HD),
                fixed(QW, SPAN),
                pl.BlockSpec((384, 128), lambda r, zh, info: (step(r, zh, info), 0)),
                pl.BlockSpec((1, 384), lambda r, zh, info: (0, step(r, zh, info))),
            ]
            + [pl.BlockSpec((TOK, 384), lambda r, zh, info: (0, step(r, zh, info)))] * GROUP,
            out_specs=pl.BlockSpec((1, 1, 4, 96, WIDE), lambda r, zh, info: (r, zh, 0, 0, 0)),
        ),
        out_shape=jax.ShapeDtypeStruct((2, 2, 4, 96, WIDE), bf16),
        compiler_params=pltpu.CompilerParams(vmem_limit_bytes=VMEM_LIMIT),
        cost_estimate=NO_COST,
        name="weight_grads",
    )(info, normed_all, mixed_grad, heads, rest, gain, *branch_blocks)


def token_grad_kernel(tail_ref, token_ref, hidden_ref, *refs):
    parts = refs[:4]
    out_ref = refs[4]
    normed_grad = total_of([part[...] for part in parts])
    rows = token_ref[...].astype(f32)
    gain = tail_ref[GAIN_AT : GAIN_AT + 1, :]
    out_ref[...] = hidden_ref[...] + norm_back(rows, rms_scale(rows), gain, normed_grad)


def token_grads(tail, tokens, hidden_grad, parts):
    return pl.pallas_call(
        token_grad_kernel,
        out_shape=jax.ShapeDtypeStruct((TOK, D), f32),
        in_specs=vmem_specs(7),
        out_specs=vmem_specs(1)[0],
        compiler_params=pltpu.CompilerParams(vmem_limit_bytes=VMEM_LIMIT),
        cost_estimate=NO_COST,
        name="token_grads",
    )(tail, tokens, hidden_grad, *parts)


def small_update_kernel(owned_ref, *refs):
    ins, outs, sums = refs[:12], refs[12:24], refs[24:]
    in_sum, out_sum = sums
    shared = jnp.zeros((12, 128), f32)
    for u in range(GROUP):
        grad = owned_ref[u].astype(f32)
        in_sum[:, u * QW : (u + 1) * QW] = grad[:, :QW]
        in_sum[:, 1536 + u * HD : 1536 + (u + 1) * HD] = grad[:, QW : QW + HD]
        in_sum[:, 2048 + u * HD : 2048 + (u + 1) * HD] = grad[:, QW + HD : QW + 2 * HD]
        out_sum[:, u * QW : (u + 1) * QW] = grad[:, 384 : 384 + QW]
        shared = shared + grad[:, 512:]
    square = jnp.concatenate([shared, jnp.zeros((116, 128), f32)], axis=0).T
    grads = (in_sum[...], out_sum[...], shared[:, ROUTER_AT : ROUTER_AT + EXPERTS], square[GAIN_AT : GAIN_AT + 2, :12])
    rates = (rate_project_in, rate_project_out, rate_router, rate_gains)
    for at in range(4):
        state = [ref[...] for ref in ins[at * 3 : at * 3 + 3]]
        for ref, new in zip(outs[at * 3 : at * 3 + 3], adam_update(*state, grads[at], rates[at])):
            ref[...] = new


def small_updates(owned, states):
    return pl.pallas_call(
        small_update_kernel,
        out_shape=tuple(jax.ShapeDtypeStruct(state.shape, f32) for state in states),
        in_specs=vmem_specs(13),
        out_specs=tuple(vmem_specs(12)),
        scratch_shapes=[pltpu.VMEM((12, 2560), f32), pltpu.VMEM((12, D), f32)],
        compiler_params=pltpu.CompilerParams(vmem_limit_bytes=VMEM_LIMIT),
        cost_estimate=NO_COST,
        name="small_updates",
    )(owned, *states)


def pick_rows(ranks):
    return ranks == lax.broadcasted_iota(jnp.int32, (CAP, TOK), 0)


def expert_kernel(info_ref, rank_ref, hit_ref, tail_ref, *refs):
    xs = refs[:GROUP]
    c_ref, w_ref, grad_ref, act_ref, both_ref, scale_ref, weighted_ref, gate_ref, rows, slots = refs[GROUP:]
    number = pl.program_id(0)

    @pl.when(number == 0)
    def _():
        router = tail_ref[...].astype(bf16)
        lane = lax.broadcasted_iota(jnp.int32, (CAP, 128), 1)
        for at in range(GROUP):
            span = slice(at * CAP, (at + 1) * CAP)
            logits = jnp.where(hit_ref[at] > 0.0, dot(xs[at][...], router, ((1,), (1,))), -jnp.inf)
            raised = jnp.exp(logits - jnp.max(logits, axis=1, keepdims=True))
            gates = raised / jnp.sum(raised, axis=1, keepdims=True)
            if at == 0:
                gate_ref[...] = gates
            high = gates.astype(bf16)
            low = (gates - high.astype(f32)).astype(bf16)
            hits = [pick_rows(rank_ref[e, at : at + 1, :]) for e in range(LOCAL_E)]
            onehot = jnp.concatenate(hits, axis=0).astype(f32).astype(bf16)
            x_rows = dot(onehot, xs[at][...], ((1,), (0,))).astype(bf16)
            cots = c_ref[jnp.bitwise_xor(info_ref[4], at // 2), at % 2, :, :D]
            c_rows = dot(onehot, cots, ((1,), (0,))) * residual_scale
            slot_gates = dot(onehot, high, ((1,), (0,))) + dot(onehot, low, ((1,), (0,)))
            for e in range(LOCAL_E):
                cut = slice(e * CAP, (e + 1) * CAP)
                rows[e, span] = x_rows[cut]
                mine = lane == ROUTER_AT + info_ref[2] * LOCAL_E + e
                scale = jnp.sum(jnp.where(mine, slot_gates[cut], 0.0), axis=1, keepdims=True)
                scale_ref[e, span] = jnp.broadcast_to(scale, (CAP, 128))
                slots[e, span] = (c_rows[cut] * scale).astype(bf16)

    up = w_ref[:, 0, :, : 2 * F].reshape(D, 2 * F)
    down = w_ref[:, 0, :, 2 * F :].reshape(D, F)
    both = dot(rows[number], up, ((1,), (0,)))
    gate = both[:, :F]
    linear = both[:, F:]
    sigmoid = 1.0 / (1.0 + jnp.exp(-gate))
    silu = gate * sigmoid
    activated = (silu * linear).astype(bf16)
    act_ref[0] = activated
    slope = sigmoid * (1.0 + gate * (1.0 - sigmoid))
    act_grad = dot(slots[number], down, ((1,), (0,)))
    weighted = jnp.sum(activated.astype(f32) * act_grad, axis=1, keepdims=True)
    weighted_ref[0] = jnp.broadcast_to(weighted, (SLOTS, 128))
    both_ref[0, :, :F] = (act_grad * linear * slope).astype(bf16)
    both_ref[0, :, F:] = (act_grad * silu).astype(bf16)
    for at in range(4):
        cols = slice(at * 384, (at + 1) * 384)
        up_grad = dot(rows[number, :, cols], both_ref[0], ((0,), (0,)))
        grad_ref[at * 4 : at * 4 + 4, 0, :, : 2 * F] = up_grad.astype(bf16).reshape(4, 96, 2 * F)
        down_grad = dot(slots[number, :, cols], act_ref[0], ((0,), (0,)))
        grad_ref[at * 4 : at * 4 + 4, 0, :, 2 * F :] = down_grad.astype(bf16).reshape(4, 96, F)


def whole(*shape):
    return pl.BlockSpec(shape, lambda e: (0,) * len(shape), pipeline_mode=pl.Buffered(1))


def per_expert(rows, columns):
    return pl.BlockSpec((1, rows, columns), lambda e: (e, 0, 0))


def expert_pass(info, ranks, hits, tail, rows, cots, weights):
    return pl.pallas_call(
        expert_kernel,
        grid=(LOCAL_E,),
        out_shape=(
            jax.ShapeDtypeStruct((16, LOCAL_E, 96, 3 * F), bf16),
            jax.ShapeDtypeStruct((LOCAL_E, SLOTS, F), bf16),
            jax.ShapeDtypeStruct((LOCAL_E, SLOTS, 2 * F), bf16),
            jax.ShapeDtypeStruct((LOCAL_E, SLOTS, 128), f32),
            jax.ShapeDtypeStruct((LOCAL_E, SLOTS, 128), f32),
            jax.ShapeDtypeStruct((TOK, 128), f32),
        ),
        in_specs=[SCALARS]
        + [whole(LOCAL_E, GROUP, TOK), whole(GROUP, TOK, 128), whole(128, D)]
        + [whole(TOK, D)] * GROUP
        + [whole(4, 2, TOK, D + EXTRA)]
        + [pl.BlockSpec((16, 1, 96, 3 * F), lambda e: (0, e, 0, 0))],
        out_specs=(
            pl.BlockSpec((16, 1, 96, 3 * F), lambda e: (0, e, 0, 0)),
            per_expert(SLOTS, F),
            per_expert(SLOTS, 2 * F),
            whole(LOCAL_E, SLOTS, 128),
            per_expert(SLOTS, 128),
            whole(TOK, 128),
        ),
        scratch_shapes=[pltpu.VMEM((LOCAL_E, SLOTS, D), bf16), pltpu.VMEM((LOCAL_E, SLOTS, D), bf16)],
        compiler_params=pltpu.CompilerParams(vmem_limit_bytes=VMEM_LIMIT),
        cost_estimate=NO_COST,
        name="experts",
    )(info, ranks, hits, tail, *rows, cots, weights)


def combine_blocks(rank_ref, held, outs):
    for at in range(GROUP):
        onehot = jnp.concatenate([pick_rows(rank_ref[e, at : at + 1, :]) for e in range(LOCAL_E)], axis=0)
        onehot = onehot.astype(f32).astype(bf16)
        outs[at][...] = dot(onehot, held[at], ((0,), (0,))).astype(bf16)


def input_grad_kernel(first_ref, rank_ref, both_ref, weighted_ref, w_ref, *refs):
    outs = refs[:GROUP]
    held = refs[GROUP]
    number = pl.program_id(0)
    up = w_ref[:, 0].reshape(D, 2 * F)
    back = dot(both_ref[0], up, ((1,), (1,))).astype(bf16)
    high = weighted_ref[0].astype(bf16).astype(f32)
    low = weighted_ref[0] - high
    lane = lax.broadcasted_iota(jnp.int32, (SLOTS, EXTRA), 1)
    mine = first_ref[0] + number
    tail = (jnp.where(lane == mine, high, 0.0) + jnp.where(lane == mine + EXPERTS, low, 0.0)).astype(bf16)
    for at in range(GROUP):
        span = slice(at * CAP, (at + 1) * CAP)
        place = pl.ds(pl.multiple_of(number * CAP, CAP), CAP)
        held[at, place, :D] = back[span]
        held[at, place, D:] = tail[span]

    @pl.when(number == LOCAL_E - 1)
    def _():
        combine_blocks(rank_ref, held, outs)


def expert_input_grads(first, ranks, both, weighted, weights):
    return pl.pallas_call(
        input_grad_kernel,
        grid=(LOCAL_E,),
        out_shape=(jax.ShapeDtypeStruct((TOK, D + EXTRA), bf16),) * GROUP,
        in_specs=[
            pl.BlockSpec(memory_space=pltpu.SMEM),
            whole(LOCAL_E, GROUP, TOK),
            per_expert(SLOTS, 2 * F),
            per_expert(SLOTS, 128),
            pl.BlockSpec((16, 1, 96, 2 * F), lambda e: (0, e, 0, 0)),
        ],
        out_specs=(whole(TOK, D + EXTRA),) * GROUP,
        scratch_shapes=[pltpu.VMEM((GROUP, LOCAL_E * CAP, D + EXTRA), bf16)],
        compiler_params=pltpu.CompilerParams(vmem_limit_bytes=VMEM_LIMIT),
        cost_estimate=NO_COST,
        name="input_grads",
    )(first, ranks, both, weighted, weights)


def mixture_kernel(info_ref, rank_ref, act_ref, scale_ref, w_ref, out_ref, held):
    number = pl.program_id(0)
    down = w_ref[:, 0].reshape(D, F)
    produced = dot(act_ref[0], down, ((1,), (1,))).astype(bf16).astype(f32)
    produced = (produced * scale_ref[0, :, 0:1]).astype(bf16)
    for at in range(GROUP):
        place = pl.ds(pl.multiple_of(number * CAP, CAP), CAP)
        held[at, place] = produced[at * CAP : (at + 1) * CAP]

    @pl.when(number == LOCAL_E - 1)
    def _():
        combine_blocks(rank_ref, held, [out_ref.at[jnp.bitwise_xor(info_ref[4], at // 2), at % 2] for at in range(GROUP)])


def expert_mixture(info, ranks, activated, scales, weights):
    return pl.pallas_call(
        mixture_kernel,
        grid=(LOCAL_E,),
        out_shape=jax.ShapeDtypeStruct((4, 2, TOK, D), bf16),
        in_specs=[
            SCALARS,
            whole(LOCAL_E, GROUP, TOK),
            per_expert(SLOTS, F),
            per_expert(SLOTS, 128),
            pl.BlockSpec((16, 1, 96, F), lambda e: (0, e, 0, 2)),
        ],
        out_specs=whole(4, 2, TOK, D),
        scratch_shapes=[pltpu.VMEM((GROUP, LOCAL_E * CAP, D), bf16)],
        compiler_params=pltpu.CompilerParams(vmem_limit_bytes=VMEM_LIMIT),
        cost_estimate=NO_COST,
        name="mixture",
    )(info, ranks, activated, scales, weights)


def shards(
    tokens, cotangent, routes, project_in, project_out, router_weight, norm_gains, expert_up, expert_down,
    project_in_first, project_in_second, project_out_first, project_out_second,
    router_weight_first, router_weight_second, norm_gains_first, norm_gains_second,
    expert_up_first, expert_up_second, expert_down_first, expert_down_second,
):
    block = lax.axis_index("blk")
    x_at = lax.axis_index("x")
    ulys = x_at * 2 + lax.axis_index("zl")

    experts_own = jnp.concatenate(
        [expert_up.astype(bf16), jnp.swapaxes(expert_down.astype(bf16), 1, 2)], axis=2
    )
    token_pair = jnp.stack([tokens, trade(tokens, "zl", 1)])
    token_pairs = [token_pair] + [trade(token_pair, "x", mask) for mask in (1, 2, 3)]

    core = lax.axis_index("co")
    info = jnp.stack([block, x_at // 2, ulys, core, x_at]).astype(jnp.int32)
    in_own = project_in.astype(bf16)
    shared = jnp.concatenate([router_weight.astype(bf16), norm_gains.astype(bf16).T], axis=1)
    shared = jnp.pad(shared, ((0, 0), (0, 22)))
    cut = lambda v: jnp.swapaxes(v.reshape(12, GROUP, -1), 0, 1)
    payload = jnp.concatenate(
        [
            cut(in_own[:, :1536]),
            cut(in_own[:, 1536:2048]),
            cut(in_own[:, 2048:]),
            jnp.zeros((GROUP, 12, 64), bf16),
            cut(project_out.astype(bf16).T),
            jnp.broadcast_to(shared[None], (GROUP, 12, 64)),
        ],
        axis=2,
    )
    near_rows = a2a(payload, ULYS).reshape(96, WIDE)
    carried = jnp.concatenate(
        [cotangent, jnp.pad(routes.astype(bf16), ((0, 0), (0, EXTRA - TOPK)))], axis=1
    )
    carried_partner = trade(after(carried, token_pair), "zl", 1)
    near_mine = a2a(jnp.broadcast_to(near_rows[None], (8, 96, WIDE)), ("zh", "blk"))
    near_other = trade(near_mine, "co", 1)
    experts_own = lax.optimization_barrier(
        (experts_own.reshape(LOCAL_E * 96, 3 * F), near_mine, carried_partner, *token_pairs)
    )[0]
    experts_full = lax.all_gather(experts_own, DPBLK, axis=0, tiled=True).reshape(16, LOCAL_E, 96, 3 * F)

    at_of = jnp.arange(SPAN, dtype=jnp.int32) // TOK
    within = ((ulys & 3) ^ (at_of & 3)) * TOK + jnp.arange(SPAN, dtype=jnp.int32) % TOK
    chunk_of = 2 * block + ((at_of // 4) ^ (x_at // 2))
    position = (chunk_of * CHUNK + within).astype(f32)
    frequency = rope_base ** (-jnp.arange(HALF, dtype=f32) * 2.0 / HD)
    angles = frequency[:, None] * position[None, :]
    cosine = jnp.cos(angles)
    sine = jnp.sin(angles)
    near, tail, normed_all, q_t, kv_t = project(info, near_mine, near_other, cosine, sine, token_pairs)
    router_t = tail[ROUTER_AT : ROUTER_AT + EXPERTS]
    gain_attn = tail[GAIN_AT]
    gain_ffn = tail[GAIN_AT + 1]
    kvs = [kv_t] + [trade(kv_t, "blk", mask) for mask in (1, 2, 3)]
    carried_pair = jnp.stack([carried, after(carried_partner, q_t)])
    carried_all = a2a(jnp.broadcast_to(carried_pair[None], (4, 2, TOK, D + EXTRA)), "x")
    mask_pos = within[:CHUNK]
    heads_t, heads_low, logs, *branch_parts = attend(info, mask_pos, q_t, near, kvs)
    branch = total_of(collect(branch_parts, carried_all))

    x_own = tokens.astype(f32)
    hidden = x_own + residual_scale * branch
    scale_ffn = rms_scale(hidden)
    normed_ffn = (hidden * scale_ffn * gain_ffn).astype(bf16)
    ffn_blocks = spread(normed_ffn, trade(normed_ffn, "zl", 1))

    lane_ids = jnp.arange(128, dtype=jnp.int32) - ROUTER_AT
    route_all = jnp.take(carried_all[..., D : D + TOPK], x_at ^ jnp.arange(4), axis=0)
    route_all = route_all.reshape(GROUP, TOK, TOPK).astype(jnp.int32)
    hits_all = jnp.any(route_all[..., None] == lane_ids, axis=2)
    first = (ulys * LOCAL_E).astype(jnp.int32)
    hits_local = lax.dynamic_slice_in_dim(hits_all, first + ROUTER_AT, LOCAL_E, axis=2)
    earlier = jnp.tril(jnp.ones((TOK, TOK), bf16), -1)
    ranks = jnp.einsum("rt,stj->jsr", earlier, hits_local.astype(bf16), preferred_element_type=f32)
    ranks = jnp.where(jnp.transpose(hits_local, (2, 0, 1)), ranks.astype(jnp.int32), -1)
    expert_grad, activated, both_grad, slot_gates, weighted, gates_own = expert_pass(
        info, ranks, hits_all.astype(f32), tail, ffn_blocks, carried_all, experts_full
    )
    gates_own = gates_own[:, ROUTER_AT : ROUTER_AT + EXPERTS]
    expert_sum = lax.psum_scatter(
        expert_grad.reshape(16 * LOCAL_E * 96, 3 * F), DPBLK, scatter_dimension=0, tiled=True
    ).reshape(LOCAL_E, 96, 3 * F)
    ffn_sums = expert_input_grads(first.reshape(1), ranks, both_grad, weighted, experts_full)
    mixture_sums = expert_mixture(info, after(ranks, ffn_sums[0]), activated, slot_gates, experts_full)
    returned = total_of(collect(ffn_sums, mixture_sums))

    upstream = cotangent.astype(f32)
    weighted = returned[:, D : D + EXPERTS] + returned[:, D + EXPERTS : D + 2 * EXPERTS]
    logit_grad = weighted - gates_own * jnp.sum(weighted, axis=1, keepdims=True)
    ffn_grad = returned[:, :D] + jnp.dot(logit_grad, router_t, precision=lax.Precision.HIGHEST)
    router_grad = dot(normed_ffn, logit_grad.astype(bf16), ((0,), (0,)))
    gain_ffn_grad = jnp.sum(ffn_grad * hidden * scale_ffn, axis=0)
    hidden_grad = upstream + norm_back(hidden, scale_ffn, gain_ffn, ffn_grad)
    branch_grad = (residual_scale * hidden_grad).astype(bf16)
    branch_blocks = spread(branch_grad, trade(branch_grad, "zl", 1))

    rest = jnp.concatenate([jnp.zeros((D, ROUTER_AT), f32), router_grad, jnp.zeros((D, 1), f32), gain_ffn_grad[:, None]], axis=1)
    rest = jnp.pad(rest, ((0, 0), (0, 128 - GAIN_AT - 2)))
    branch_blocks = list(lax.optimization_barrier((*branch_blocks, rest))[:GROUP])
    dq_t, *dkv = attend_back(info, mask_pos, q_t, near, kvs, heads_t, logs, branch_blocks)
    kv_parts = [dkv[0]] + [trade(dkv[mask], "blk", mask) for mask in (1, 2, 3)]
    mixture_parts = a2a(lax.optimization_barrier((mixture_sums, *branch_blocks))[0], "x")
    mixture_pair = jnp.sum(after(mixture_parts, dq_t).astype(f32), axis=0)
    mixture_other = trade(mixture_pair[1].astype(bf16), "zl", 1)
    kv_parts[0] = after(kv_parts[0], mixture_pair)

    *normed_parts, mixed_grad, gain_attn_grad = turn_back(near, tail, cosine, sine, dq_t, kv_parts, token_pairs)
    layer_out = hidden + residual_scale * (mixture_pair[0] + mixture_other.astype(f32))
    normed_all, layer_out = lax.optimization_barrier((normed_all, layer_out))
    grads = weight_grads(info, normed_all, mixed_grad, heads_low, rest, gain_attn_grad, branch_blocks)
    both_cores = grads[0].astype(f32) + trade(grads[1], "co", 1).astype(f32)
    row_parts = a2a(both_cores.astype(bf16).reshape(8, 96, WIDE), ("zh", "blk"))
    tokens_grad = token_grads(tail, tokens, hidden_grad, collect(normed_parts, both_cores, row_parts))

    row_sum = jnp.sum(row_parts.astype(f32), axis=0).astype(bf16)
    up_sum = expert_sum[:, :, : 2 * F].astype(f32)
    down_sum = jnp.swapaxes(expert_sum[:, :, 2 * F :], 1, 2).astype(f32)
    up_state = adam_update(expert_up, expert_up_first, expert_up_second, up_sum, rate_expert_up)
    down_state = adam_update(expert_down, expert_down_first, expert_down_second, down_sum, rate_expert_down)
    row_sum, *expert_state = lax.optimization_barrier((row_sum, *up_state, *down_state))
    owned = a2a(row_sum.reshape(GROUP, 12, WIDE), ULYS)
    small_state = small_updates(
        owned,
        (
            project_in, project_in_first, project_in_second,
            project_out.T, project_out_first.T, project_out_second.T,
            router_weight, router_weight_first, router_weight_second,
            norm_gains, norm_gains_first, norm_gains_second,
        ),
    )
    out_state = [state.T for state in small_state[3:6]]
    return (layer_out, tokens_grad, *small_state[:3], *out_state, *small_state[6:], *expert_state)


def solution(mesh):
    fine = Mesh(mesh.devices.reshape(2, 2, 4, 4, 2), ALL)
    rows = P(ALL, None)
    cols = P(None, ALL)
    up = P(ULYS, DPBLK, None)
    down = P(ULYS, None, DPBLK)
    in_specs = (rows,) * 4 + (cols, rows, cols, up, down)
    in_specs += (rows,) * 2 + (cols,) * 2 + (rows,) * 2 + (cols,) * 2 + (up,) * 2 + (down,) * 2
    out_specs = (rows,) * 5 + (cols,) * 3 + (rows,) * 3 + (cols,) * 3 + (up,) * 3 + (down,) * 3
    return jax.shard_map(shards, mesh=fine, in_specs=in_specs, out_specs=out_specs, check_vma=False)
```

time: 726 us -> 555 us (0.76)
  waiting for transfers between devices: 307 us -> 260 us
  local copies, waits for them, and re-layouts: 60.4 us -> 17.6 us
  blocking collectives: 38.2 us -> 10.6 us
  starting transfers between devices: 109 us -> 85.3 us
  other arithmetic: 58 us -> 35.8 us
  matrix products: 24.9 us -> 3.23 us
  Pallas kernels: 101 us -> 117 us
    all_to_all x15 -> x5, waiting for transfers between devices: 249 us -> 29 us  [a2a(): return lax.all_to_all(value, axes, split_axis=0, concat_axis=0, tiled=True)]
    ppermute x15 -> x49, waiting for transfers between devices: 58.2 us -> 208 us  [trade(): lax.ppermute(value, axis, [(i, i ^ mask) for i in range(2 if axis in ('zl...]
    all_to_all x15 -> x5, starting transfers between devices: 89.9 us -> 23.2 us  [a2a(): return lax.all_to_all(value, axes, split_axis=0, concat_axis=0, tiled=True)]
    ppermute x15 -> x49, starting transfers between devices: 19.1 us -> 62.1 us  [trade(): lax.ppermute(value, axis, [(i, i ^ mask) for i in range(2 if axis in ('zl...]
    all_to_all x1, blocking collectives: 38.2 us -> 10.6 us  [a2a(): return lax.all_to_all(value, axes, split_axis=0, concat_axis=0, tiled=True)]
    pallas_call x1 -> x6, Pallas kernels: 18.4 us -> 44.9 us  [the longest x1 16.3 us: expert_input_grads(): pl.pallas_call(input_grad_kernel, grid=(LOCAL_E,), out_shape=(jax.ShapeDt...]
    all_gather x1, waiting for transfers between devices: 0.01 us -> 22.9 us  [shards(): lax.all_gather(experts_own, DPBLK, axis=0, tiled=True)]
    dot_general x9 -> x1, matrix products: 21.5 us -> 0.36 us  [dot(): lax.dot_general(a, b, ((dims[0], dims[1]), ((), ())), preferred_element_t...]
  transfers between devices with their start and end apart: 32 -> 56, of which waited for: 20 -> 34; matrix products, arithmetic and copies ran while one was open for 16% -> 9% of each run, Pallas kernels for 7% -> 14%
where the time goes in v2:
time: 555 us; the launch traced here: 545 us
  waiting for transfers between devices  260 us (47%)
  Pallas kernels  117 us (21%)
  starting transfers between devices  85.3 us (15%)
  other arithmetic  35.8 us (6%)
  local copies, waits for them, and re-layouts  17.6 us (3%)
  between operations  15.3 us (3%)
  blocking collectives  10.6 us (2%)
    ppermute x49, waiting for transfers between devices, trade(): lax.ppermute(value, axis, [(i, i ^ mask) for i in range(2 if axis in ('zl...  208 us
    ppermute x49, starting transfers between devices, trade(): lax.ppermute(value, axis, [(i, i ^ mask) for i in range(2 if axis in ('zl...  62.1 us
    pallas_call x1, Pallas kernels, expert_pass(): pl.pallas_call(expert_kernel, grid=(LOCAL_E,), out_shape=(jax.ShapeDtypeS...  37.4 us
    all_to_all x5, waiting for transfers between devices, a2a(): return lax.all_to_all(value, axes, split_axis=0, concat_axis=0, tiled=True)  29 us
    all_to_all x5, starting transfers between devices, a2a(): return lax.all_to_all(value, axes, split_axis=0, concat_axis=0, tiled=True)  23.2 us
    all_gather x1, waiting for transfers between devices, shards(): lax.all_gather(experts_own, DPBLK, axis=0, tiled=True)  22.9 us
    pallas_call x1, Pallas kernels, expert_input_grads(): pl.pallas_call(input_grad_kernel, grid=(LOCAL_E,), out_shape=(jax.ShapeDt...  16.3 us
    pallas_call x1, Pallas kernels, attend_back(): pl.pallas_call(attend_back_kernel, out_shape=(jax.ShapeDtypeStruct((3, HD...  12.9 us
  transfers between devices with their start and end apart: 56, of which 34 were waited for; matrix products, arithmetic and copies ran while one was open for 9% of the time, Pallas kernels for 14%

profile of v2, /device:TPU:0, one launch (start us, length us, event | category | flops | bytes accessed | tf_op | source)
XLA Modules:
  0.0 545.2 jit_solution(15202733017780041889)
XLA Ops:
  13.3 10.6 %all_to_all.30 = bf16[8,12,640]{2,1,0:T(8,128)(2,1)S(1)} all-to-all(bf16[8,12,640]{2,1,0:T(8,128)(2,1)S(1)} %concatenate.16), channel_id=1, replica_groups=mesh['zh'=2,'co'=2,'blk'=4,'x'=4,'zl'=2] {'x','zl'}, dimensions={0} | all-to-all | bytes 245760 | tf_op jit(solution)/shard_map/all_to_all | solution.py:84
  25.0 7.6 %all-to-all-start.1 = ((bf16[8,96,640]{2,1,0:T(8,128)(2,1)}), bf16[8,96,640]{2,1,0:T(8,128)(2,1)}, u32[]{:S(2)}, u32[]{:S(2)}) async-start(bf16[8,96,640]{2,1,0:T(8,128)(2,1)} %broadcast_in_dim.74), calls=%async_computation.1 | async-start | bytes 1966080 | tf_op jit(solution)/shard_map/all_to_all | solution.py:84
  41.2 12.2 %collective-permute-done.11 = bf16[128,1664]{1,0:T(8,128)(2,1)S(1)} collective-permute-done((bf16[128,1664]{1,0:T(8,128)(2,1)S(1)}, bf16[128,1664]{1,0:T(8,128)(2,1)S(1)}, u32[]{:S(2)}, u32[]{:S(2)}) %collective-permute-start.11) | collective-permute-done | bytes 426016 | tf_op jit(solution)/shard_map/ppermute | solution.py:88
  53.4 14.4 %collective-permute-done.3.refs_2_ = bf16[2,128,1536]{2,1,0:T(8,128)(2,1)} collective-permute-done((bf16[2,128,1536]{2,1,0:T(8,128)(2,1)S(1)}, bf16[2,128,1536]{2,1,0:T(8,128)(2,1)}, u32[]{:S(2)}, u32[]{:S(2)}) %collective-permute-start.3) | collective-permute-done | bytes 786464 | tf_op jit(solution)/shard_map/ppermute | solution.py:88
  74.2 6.3 %project.1 = (bf16[16,96,640]{2,1,0:T(8,128)(2,1)}, f32[128,1536]{1,0:T(8,128)}, bf16[1024,1536]{1,0:T(8,128)(2,1)}, bf16[3,64,1024]{2,1,0:T(8,128)(2,1)}, bf16[128,1024]{1,0:T(8,128)(2,1)}) custom-call(s32[5]{0:T(128)} %stack.41.info_ref, bf16[8,96,640]{2,1,0:T(8,128)(2,1)} %all-to-all-done.1.mine_ref, bf16[8,96,640]{2,1,0:T(8,128)(2,1)} %copy-done.23, ...), custom_call_target="tpu_custom_call" | custom-call | tf_op jit(solution)/shard_map/project/pallas_call | solution.py:171
  92.0 9.5 %collective-permute-done.5.kv1 = bf16[128,1024]{1,0:T(8,128)(2,1)} collective-permute-done((bf16[128,1024]{1,0:T(8,128)(2,1)}, bf16[128,1024]{1,0:T(8,128)(2,1)}, u32[]{:S(2)}, u32[]{:S(2)}) %collective-permute-start.5) | collective-permute-done | bytes 262176 | tf_op jit(solution)/shard_map/ppermute | solution.py:88
  101.5 13.3 %collective-permute-done.6.kv2 = bf16[128,1024]{1,0:T(8,128)(2,1)} collective-permute-done((bf16[128,1024]{1,0:T(8,128)(2,1)}, bf16[128,1024]{1,0:T(8,128)(2,1)}, u32[]{:S(2)}, u32[]{:S(2)}) %collective-permute-start.6) | collective-permute-done | bytes 262176 | tf_op jit(solution)/shard_map/ppermute | solution.py:88
  114.8 9.9 %attend.1 = (f32[3,64,1024]{2,1,0:T(8,128)}, bf16[192,1024]{1,0:T(8,128)(2,1)}, f32[3,1,1024]{2,1,0:T(1,128)}, bf16[128,1536]{1,0:T(8,128)(2,1)}, bf16[128,1536]...) custom-call(s32[5]{0:T(128)} %stack.41.info_ref, ...), custom_call_target="tpu_custom_call" | custom-call | tf_op jit(solution)/shard_map/attend/pallas_call | solution.py:264
  129.8 8.5 %collective-permute-done.9 = bf16[128,1536]{1,0:T(8,128)(2,1)S(1)} collective-permute-done((bf16[128,1536]{1,0:T(8,128)(2,1)}, bf16[128,1536]{1,0:T(8,128)(2,1)S(1)}, u32[]{:S(2)}, u32[]{:S(2)}) %collective-permute-start.9) | collective-permute-done | bytes 393248 | tf_op jit(solution)/shard_map/ppermute | solution.py:88
  146.8 7.8 %collective-permute-done.13 = bf16[128,1536]{1,0:T(8,128)(2,1)S(1)} collective-permute-done((bf16[128,1536]{1,0:T(8,128)(2,1)S(1)}, bf16[128,1536]{1,0:T(8,128)(2,1)S(1)}, u32[]{:S(2)}, u32[]{:S(2)}) %collective-permute-start.13) | collective-permute-done | bytes 393248 | tf_op jit(solution)/shard_map/ppermute | solution.py:88
  157.3 17.8 %collective-permute-done.15 = bf16[128,1536]{1,0:T(8,128)(2,1)S(1)} collective-permute-done((bf16[128,1536]{1,0:T(8,128)(2,1)S(1)}, bf16[128,1536]{1,0:T(8,128)(2,1)S(1)}, u32[]{:S(2)}, u32[]{:S(2)}) %collective-permute-start.15) | collective-permute-done | bytes 393248 | tf_op jit(solution)/shard_map/ppermute | solution.py:88
  183.2 12.7 %collective-permute-done.16.refs_1_ = bf16[128,1536]{1,0:T(8,128)(2,1)S(1)} collective-permute-done((bf16[128,1536]{1,0:T(8,128)(2,1)S(1)}, bf16[128,1536]{1,0:T(8,128)(2,1)S(1)}, u32[]{:S(2)}, u32[]{:S(2)}) %collective-permute-start.16) | collective-permute-done | bytes 393248 | tf_op jit(solution)/shard_map/ppermute | solution.py:88
  207.7 4.7 collective-permute-done.20.refs_5_
  215.4 22.9 %all-gather.2.cloned.1.call-done = bf16[7680,1536]{1,0:T(8,128)(2,1)} async-done(((bf16[480,1536]{1,0:T(8,128)(2,1)}), bf16[7680,1536]{1,0:T(8,128)(2,1)}) %all-gather.2.cloned.1.call-update) | async-done | bytes 23592976 | tf_op jit(solution)/shard_map/all_gather | solution.py:727
  238.3 37.4 %experts.1 = (bf16[16,5,96,1536]{3,2,1,0:T(8,128)(2,1)}, bf16[5,384,512]{2,1,0:T(8,128)(2,1)}, bf16[5,384,1024]{2,1,0:T(8,128)(2,1)}, f32[5,384,128]{2,1,0:T(8,1...) custom-call(s32[5]{0:T(128)} %stack.41.info_ref, s32[5,8,128]{2,1,0:T(8,128)} %fusion.3.rank_ref, ...), custom_call_target="tpu_custom_call" | custom-call | tf_op jit(solution)/shard_map/experts/pallas_call | solution.py:570
  275.7 16.3 %input_grads.1 = (bf16[128,1664]{1,0:T(8,128)(2,1)}, bf16[128,1664]{1,0:T(8,128)(2,1)}, bf16[128,1664]{1,0:T(8,128)(2,1)}, bf16[128,1664]{1,0:T(8,128)(2,1)}, bf...) custom-call(s32[1]{0:T(128)} %bitcast.22.first_ref, ...), custom_call_target="tpu_custom_call" | custom-call | tf_op jit(solution)/shard_map/input_grads/pallas_call | solution.py:631
  296.7 11.9 %mixture.1 = bf16[4,2,128,1536]{3,2,1,0:T(8,128)(2,1)} custom-call(s32[5]{0:T(128)} %stack.41.info_ref, s32[5,8,128]{2,1,0:T(8,128)} %fusion.3.rank_ref, bf16[5,384,512]{2,1,0:T(8,128)(2,1)} %get-tuple-element.130.act_ref, f32[5,384,128]{2,1,0:T(8,128)} %get-tuple-element.131.scale_ref, bf16[16,5,96,1536]{3,2,1,0:T(8,128)(2,1)} %bitcast.84), custom_call_target="tpu_custom_call" | custom-call | tf_op jit(solution)/shard_map/mixture/pallas_call | solution.py:665
  315.1 9.8 %collective-permute-done.27 = bf16[128,1664]{1,0:T(8,128)(2,1)S(1)} collective-permute-done((bf16[128,1664]{1,0:T(8,128)(2,1)S(1)}, bf16[128,1664]{1,0:T(8,128)(2,1)S(1)}, u32[]{:S(2)}, u32[]{:S(2)}) %collective-permute-start.27) | collective-permute-done | bytes 426016 | tf_op jit(solution)/shard_map/ppermute | solution.py:88
  325.2 21.1 %collective-permute-done.29 = bf16[128,1664]{1,0:T(8,128)(2,1)S(1)} collective-permute-done((bf16[128,1664]{1,0:T(8,128)(2,1)S(1)}, bf16[128,1664]{1,0:T(8,128)(2,1)S(1)}, u32[]{:S(2)}, u32[]{:S(2)}) %collective-permute-start.29) | collective-permute-done | bytes 426016 | tf_op jit(solution)/shard_map/ppermute | solution.py:88
  355.5 5.0 collective-permute-done.30.refs_1_
  373.8 5.2 collective-permute-done.32.refs_3_
  379.0 6.4 %collective-permute-done.34.refs_5_ = bf16[128,1536]{1,0:T(8,128)(2,1)S(1)} collective-permute-done((bf16[128,1536]{1,0:T(8,128)(2,1)S(1)}, bf16[128,1536]{1,0:T(8,128)(2,1)S(1)}, u32[]{:S(2)}, u32[]{:S(2)}) %collective-permute-start.34) | collective-permute-done | bytes 393248 | tf_op jit(solution)/shard_map/ppermute | solution.py:88
  388.1 4.9 all-to-all-start.3
  393.0 12.9 %attend_back.1 = (bf16[3,64,1024]{2,1,0:T(8,128)(2,1)}, bf16[1024,128]{1,0:T(8,128)(2,1)}, bf16[1024,128]{1,0:T(8,128)(2,1)}, bf16[1024,128]{1,0:T(8,128)(2,1)}, bf16[1024,128]{1,0:T(8,128)(2,1)}) custom-call(s32[5]{0:T(128)} %stack.41.info_ref, s32[1,512]{1,0:T(1,128)} %bitcast.97, s32[512,1]{1,0:T(8,128)} %copy.62.pos_col, ...), custom_call_target="tpu_custom_call" | custom-call | tf_op jit(solution)/shard_map/attend_back/pallas_call | solution.py:340
  405.9 22.6 %all-to-all-done.3 = bf16[4,2,128,1536]{3,2,1,0:T(8,128)(2,1)} async-done(((bf16[4,2,128,1536]{3,2,1,0:T(8,128)(2,1)}), bf16[4,2,128,1536]{3,2,1,0:T(8,128)(2,1)}, u32[]{:S(2)}, u32[]{:S(2)}) %all-to-all-start.3) | async-done | bytes 3145760 | tf_op jit(solution)/shard_map/all_to_all | solution.py:84
  436.3 8.3 %collective-permute-done.38.kv1 = bf16[1024,128]{1,0:T(8,128)(2,1)S(1)} collective-permute-done((bf16[1024,128]{1,0:T(8,128)(2,1)S(1)}, bf16[1024,128]{1,0:T(8,128)(2,1)S(1)}, u32[]{:S(2)}, u32[]{:S(2)}) %collective-permute-start.38) | collective-permute-done | bytes 262176 | tf_op jit(solution)/shard_map/ppermute | solution.py:88
  444.6 10.2 %collective-permute-done.39.kv2 = bf16[1024,128]{1,0:T(8,128)(2,1)S(1)} collective-permute-done((bf16[1024,128]{1,0:T(8,128)(2,1)S(1)}, bf16[1024,128]{1,0:T(8,128)(2,1)S(1)}, u32[]{:S(2)}, u32[]{:S(2)}) %collective-permute-start.39) | collective-permute-done | bytes 262176 | tf_op jit(solution)/shard_map/ppermute | solution.py:88
  456.2 7.8 %turn_back.1 = (bf16[128,1536]{1,0:T(8,128)(2,1)}, bf16[128,1536]{1,0:T(8,128)(2,1)}, bf16[128,1536]{1,0:T(8,128)(2,1)}, bf16[128,1536]{1,0:T(8,128)(2,1)}, bf16...) custom-call(bf16[16,96,640]{2,1,0:T(8,128)(2,1)} %get-tuple-element., ...), custom_call_target="tpu_custom_call" | custom-call | tf_op jit(solution)/shard_map/turn_back/pallas_call | solution.py:392
  465.0 8.7 %weight_grads.1 = bf16[2,2,4,96,640]{4,3,2,1,0:T(8,128)(2,1)} custom-call(s32[5]{0:T(128)} %stack.41.info_ref, bf16[1024,1536]{1,0:T(8,128)(2,1)} %get-tuple-element.166.normed_ref, bf16[1024,320]{1,0:T(8,128)(2,1)} %get-tuple-element.167.mixed_ref, bf16[192,1024]{1,0:T(8,128)(2,1)} %get-tuple-element.168.heads_ref, f32[1536,128]{1,0:T(8,128)} %pad.14.rest_ref, ...), custom_call_target="tpu_custom_call" | custom-call | tf_op jit(solution)/shard_map/weight_grads/pallas_call | solution.py:426
  480.7 7.8 %collective-permute-done.42 = bf16[128,1536]{1,0:T(8,128)(2,1)S(1)} collective-permute-done((bf16[128,1536]{1,0:T(8,128)(2,1)S(1)}, bf16[128,1536]{1,0:T(8,128)(2,1)S(1)}, u32[]{:S(2)}, u32[]{:S(2)}) %collective-permute-start.42) | collective-permute-done | bytes 393248 | tf_op jit(solution)/shard_map/ppermute | solution.py:88
  499.1 7.6 %collective-permute-done.46 = bf16[128,1536]{1,0:T(8,128)(2,1)} collective-permute-done((bf16[128,1536]{1,0:T(8,128)(2,1)S(1)}, bf16[128,1536]{1,0:T(8,128)(2,1)}, u32[]{:S(2)}, u32[]{:S(2)}) %collective-permute-start.46) | collective-permute-done | bytes 393248 | tf_op jit(solution)/shard_map/ppermute | solution.py:88
  514.7 6.3 %multiply_subtract_fusion = (f32[5,96,1024]{2,1,0:T(8,128)}, f32[5,96,1024]{2,1,0:T(8,128)}, f32[5,96,1024]{2,1,0:T(8,128)}) fusion(f32[5,96,1024]{2,1,0:T(8,128)S(1)} %copy-done.2, bf16[5,96,1536]{2,1,0:T(8,128)(2,1)} %bitcast.88, f32[5,96,1024]{2,1,0:T(8,128)} %param.38, f32[5,96,1024]{2,1,0:T(8,128)} %param.39), kind=kLoop, calls=%fused_computation.8 | loop fusion | flops 7864320 | bytes 12779520 | tf_op jit(solution)/shard_map/sub | solution.py:77
  (277 shorter events, 161.6 us)
Async XLA Ops:
  7.2 25.5 %collective-permute-start.1 = (bf16[128,1536]{1,0:T(8,128)(2,1)}, bf16[128,1536]{1,0:T(8,128)(2,1)S(1)}, u32[]{:S(2)}, u32[]{:S(2)}) collective-permute-start(bf16[128,1536]{1,0:T(8,128)(2,1)} %token_ref.1), channel_id=1, source_target_pairs={{0,1},{1,0},{2,3},{3,2},{4,5},{5,4},{6,7},{7,6},{8,9},{9,8},{10,11... | collective-permute-start | bytes 1179656 | tf_op jit(solution)/shard_map/ppermute | solution.py:88
  25.0 28.4 %all-to-all-start.1 = ((bf16[8,96,640]{2,1,0:T(8,128)(2,1)}), bf16[8,96,640]{2,1,0:T(8,128)(2,1)}, u32[]{:S(2)}, u32[]{:S(2)}) async-start(bf16[8,96,640]{2,1,0:T(8,128)(2,1)} %broadcast_in_dim.74), calls=%async_computation.1 | async-start | bytes 1966080 | tf_op jit(solution)/shard_map/all_to_all | solution.py:84
  32.6 205.7 %all-gather.2.cloned.1.call-start = ((), (), s32[]{:S(2)}) async-start(), calls=%async_computation.7 | async-start | bytes 25067520 | tf_op jit(solution)/shard_map/all_gather | solution.py:727
  32.8 20.6 %collective-permute-start.2 = (bf16[2,128,1536]{2,1,0:T(8,128)(2,1)S(1)}, bf16[2,128,1536]{2,1,0:T(8,128)(2,1)S(1)}, u32[]{:S(2)}, u32[]{:S(2)}) collective-permute-start(bf16[2,128,1536]{2,1,0:T(8,128)(2,1)S(1)} %pad_maximum_fusion.2.refs_0_), channel_id=1, source_target_pairs={{0,2},{2,0},{4,6},{6,4},{1,3},{3,1},{5,7},{7,5},{8,10},{10,8},{12,... | collective-permute-start | bytes 2359304 | tf_op jit(solution)/shard_map/ppermute | solution.py:88
  33.3 34.5 %collective-permute-start.3 = (bf16[2,128,1536]{2,1,0:T(8,128)(2,1)S(1)}, bf16[2,128,1536]{2,1,0:T(8,128)(2,1)}, u32[]{:S(2)}, u32[]{:S(2)}) collective-permute-start(bf16[2,128,1536]{2,1,0:T(8,128)(2,1)S(1)} %pad_maximum_fusion.2.refs_0_), channel_id=1, source_target_pairs={{0,4},{2,6},{4,0},{6,2},{1,5},{3,7},{5,1},{7,3},{8,12},{10,14},{12... | collective-permute-start | bytes 2359304 | tf_op jit(solution)/shard_map/ppermute | solution.py:88
  35.4 35.0 %collective-permute-start.4 = (bf16[2,128,1536]{2,1,0:T(8,128)(2,1)S(1)}, bf16[2,128,1536]{2,1,0:T(8,128)(2,1)}, u32[]{:S(2)}, u32[]{:S(2)}) collective-permute-start(bf16[2,128,1536]{2,1,0:T(8,128)(2,1)S(1)} %pad_maximum_fusion.2.refs_0_), channel_id=1, source_target_pairs={{0,6},{2,4},{4,2},{6,0},{1,7},{3,5},{5,3},{7,1},{8,14},{10,12},{12... | collective-permute-start | bytes 2359304 | tf_op jit(solution)/shard_map/ppermute | solution.py:88
  82.6 57.5 %all-to-all-start.2 = ((bf16[4,2,128,1664]{3,2,1,0:T(8,128)(2,1)}), bf16[4,2,128,1664]{3,2,1,0:T(8,128)(2,1)S(1)}, u32[]{:S(2)}, u32[]{:S(2)}) async-start(bf16[4,2,128,1664]{3,2,1,0:T(8,128)(2,1)} %broadcast_in_dim.77), calls=%async_computation.2 | async-start | bytes 6815744 | tf_op jit(solution)/shard_map/all_to_all | solution.py:84
  86.3 428.3 %reduce-scatter.2.cloned.1.call-start = ((), (), s32[]{:S(2)}) async-start(), calls=%async_computation.8 | async-start | bytes 25067520 | tf_op jit(solution)/shard_map/reduce_scatter | solution.py:767
  88.1 26.7 %collective-permute-start.6 = (bf16[128,1024]{1,0:T(8,128)(2,1)}, bf16[128,1024]{1,0:T(8,128)(2,1)}, u32[]{:S(2)}, u32[]{:S(2)}) collective-permute-start(bf16[128,1024]{1,0:T(8,128)(2,1)} %get-tuple-element.111.kv0), channel_id=1, source_target_pairs={{0,16},{8,24},{16,0},{24,8},{1,17},{9,25},{17,1},{25,9},{2,18},{10... | collective-permute-start | bytes 786440 | tf_op jit(solution)/shard_map/ppermute | solution.py:88
  90.8 24.0 %collective-permute-start.7 = (bf16[128,1024]{1,0:T(8,128)(2,1)}, bf16[128,1024]{1,0:T(8,128)(2,1)}, u32[]{:S(2)}, u32[]{:S(2)}) collective-permute-start(bf16[128,1024]{1,0:T(8,128)(2,1)} %get-tuple-element.111.kv0), channel_id=1, source_target_pairs={{0,24},{8,16},{16,8},{24,0},{1,25},{9,17},{17,9},{25,1},{2,26},{10... | collective-permute-start | bytes 786440 | tf_op jit(solution)/shard_map/ppermute | solution.py:88
  128.0 18.8 %collective-permute-start.14 = (bf16[128,1536]{1,0:T(8,128)(2,1)}, bf16[128,1536]{1,0:T(8,128)(2,1)}, u32[]{:S(2)}, u32[]{:S(2)}) collective-permute-start(bf16[128,1536]{1,0:T(8,128)(2,1)} %get-tuple-element.123), channel_id=1, source_target_pairs={{0,6},{2,4},{4,2},{6,0},{1,7},{3,5},{5,3},{7,1},{8,14},{10,12},{12... | collective-permute-start | bytes 1179656 | tf_op jit(solution)/shard_map/ppermute | solution.py:88
  129.1 28.1 %collective-permute-start.8 = (bf16[128,1536]{1,0:T(8,128)(2,1)}, bf16[128,1536]{1,0:T(8,128)(2,1)}, u32[]{:S(2)}, u32[]{:S(2)}) collective-permute-start(bf16[128,1536]{1,0:T(8,128)(2,1)} %get-tuple-element.113), channel_id=1, source_target_pairs={{0,2},{2,0},{4,6},{6,4},{1,3},{3,1},{5,7},{7,5},{8,10},{10,8},{12,... | collective-permute-start | bytes 1179656 | tf_op jit(solution)/shard_map/ppermute | solution.py:88
  155.7 19.4 %collective-permute-start.15 = (bf16[128,1536]{1,0:T(8,128)(2,1)S(1)}, bf16[128,1536]{1,0:T(8,128)(2,1)S(1)}, u32[]{:S(2)}, u32[]{:S(2)}) collective-permute-start(bf16[128,1536]{1,0:T(8,128)(2,1)S(1)} %add_convert_fusion.6), channel_id=1, source_target_pairs={{0,1},{1,0},{2,3},{3,2},{4,5},{5,4},{6,7},{7,6},{8,9},{9,8},{10,11... | collective-permute-start | bytes 1179656 | tf_op jit(solution)/shard_map/ppermute | solution.py:88
  176.7 19.2 %collective-permute-start.16 = (bf16[128,1536]{1,0:T(8,128)(2,1)S(1)}, bf16[128,1536]{1,0:T(8,128)(2,1)S(1)}, u32[]{:S(2)}, u32[]{:S(2)}) collective-permute-start(bf16[128,1536]{1,0:T(8,128)(2,1)S(1)} %multiply_convert_fusion.1.refs_0_), channel_id=1, source_target_pairs={{0,1},{1,0},{2,3},{3,2},{4,5},{5,4},{6,7},{7,6},{8,9},{9,8},{10,11... | collective-permute-start | bytes 1179656 | tf_op jit(solution)/shard_map/ppermute | solution.py:88
  177.5 20.6 %collective-permute-start.17 = (bf16[128,1536]{1,0:T(8,128)(2,1)S(1)}, bf16[128,1536]{1,0:T(8,128)(2,1)S(1)}, u32[]{:S(2)}, u32[]{:S(2)}) collective-permute-start(bf16[128,1536]{1,0:T(8,128)(2,1)S(1)} %multiply_convert_fusion.1.refs_0_), channel_id=1, source_target_pairs={{0,2},{2,0},{4,6},{6,4},{1,3},{3,1},{5,7},{7,5},{8,10},{10,8},{12,... | collective-permute-start | bytes 1179656 | tf_op jit(solution)/shard_map/ppermute | solution.py:88
  178.7 26.0 %collective-permute-start.19 = (bf16[128,1536]{1,0:T(8,128)(2,1)S(1)}, bf16[128,1536]{1,0:T(8,128)(2,1)S(1)}, u32[]{:S(2)}, u32[]{:S(2)}) collective-permute-start(bf16[128,1536]{1,0:T(8,128)(2,1)S(1)} %multiply_convert_fusion.1.refs_0_), channel_id=1, source_target_pairs={{0,4},{2,6},{4,0},{6,2},{1,5},{3,7},{5,1},{7,3},{8,12},{10,14},{12... | collective-permute-start | bytes 1179656 | tf_op jit(solution)/shard_map/ppermute | solution.py:88
  180.6 24.2 %collective-permute-start.21 = (bf16[128,1536]{1,0:T(8,128)(2,1)S(1)}, bf16[128,1536]{1,0:T(8,128)(2,1)S(1)}, u32[]{:S(2)}, u32[]{:S(2)}) collective-permute-start(bf16[128,1536]{1,0:T(8,128)(2,1)S(1)} %multiply_convert_fusion.1.refs_0_), channel_id=1, source_target_pairs={{0,6},{2,4},{4,2},{6,0},{1,7},{3,5},{5,3},{7,1},{8,14},{10,12},{12... | collective-permute-start | bytes 1179656 | tf_op jit(solution)/shard_map/ppermute | solution.py:88
  294.7 20.4 %collective-permute-start.28 = (bf16[128,1664]{1,0:T(8,128)(2,1)}, bf16[128,1664]{1,0:T(8,128)(2,1)S(1)}, u32[]{:S(2)}, u32[]{:S(2)}) collective-permute-start(bf16[128,1664]{1,0:T(8,128)(2,1)} %get-tuple-element.140), channel_id=1, source_target_pairs={{0,6},{2,4},{4,2},{6,0},{1,7},{3,5},{5,3},{7,1},{8,14},{10,12},{12... | collective-permute-start | bytes 1277960 | tf_op jit(solution)/shard_map/ppermute | solution.py:88
  296.1 29.1 %collective-permute-start.23 = (bf16[128,1664]{1,0:T(8,128)(2,1)}, bf16[128,1664]{1,0:T(8,128)(2,1)S(1)}, u32[]{:S(2)}, u32[]{:S(2)}) collective-permute-start(bf16[128,1664]{1,0:T(8,128)(2,1)} %get-tuple-element.132), channel_id=1, source_target_pairs={{0,2},{2,0},{4,6},{6,4},{1,3},{3,1},{5,7},{7,5},{8,10},{10,8},{12,... | collective-permute-start | bytes 1277960 | tf_op jit(solution)/shard_map/ppermute | solution.py:88
  325.1 21.2 %collective-permute-start.29 = (bf16[128,1664]{1,0:T(8,128)(2,1)S(1)}, bf16[128,1664]{1,0:T(8,128)(2,1)S(1)}, u32[]{:S(2)}, u32[]{:S(2)}) collective-permute-start(bf16[128,1664]{1,0:T(8,128)(2,1)S(1)} %add_convert_fusion), channel_id=1, source_target_pairs={{0,1},{1,0},{2,3},{3,2},{4,5},{5,4},{6,7},{7,6},{8,9},{9,8},{10,11... | collective-permute-start | bytes 1277960 | tf_op jit(solution)/shard_map/ppermute | solution.py:88
  350.6 20.2 %collective-permute-start.33 = (bf16[128,1536]{1,0:T(8,128)(2,1)S(1)}, bf16[128,1536]{1,0:T(8,128)(2,1)S(1)}, u32[]{:S(2)}, u32[]{:S(2)}) collective-permute-start(bf16[128,1536]{1,0:T(8,128)(2,1)S(1)} %get-tuple-element.142.refs_0_), channel_id=1, source_target_pairs={{0,4},{2,6},{4,0},{6,2},{1,5},{3,7},{5,1},{7,3},{8,12},{10,14},{12... | collective-permute-start | bytes 1179656 | tf_op jit(solution)/shard_map/ppermute | solution.py:88
  352.4 21.4 %collective-permute-start.35 = (bf16[128,1536]{1,0:T(8,128)(2,1)S(1)}, bf16[128,1536]{1,0:T(8,128)(2,1)S(1)}, u32[]{:S(2)}, u32[]{:S(2)}) collective-permute-start(bf16[128,1536]{1,0:T(8,128)(2,1)S(1)} %get-tuple-element.142.refs_0_), channel_id=1, source_target_pairs={{0,6},{2,4},{4,2},{6,0},{1,7},{3,5},{5,3},{7,1},{8,14},{10,12},{12... | collective-permute-start | bytes 1179656 | tf_op jit(solution)/shard_map/ppermute | solution.py:88
  361.4 24.0 %collective-permute-start.34 = (bf16[128,1536]{1,0:T(8,128)(2,1)S(1)}, bf16[128,1536]{1,0:T(8,128)(2,1)S(1)}, u32[]{:S(2)}, u32[]{:S(2)}) collective-permute-start(bf16[128,1536]{1,0:T(8,128)(2,1)S(1)} %collective-permute-done.30.refs_1_), channel_id=1, source_target_pairs={{0,4},{2,6},{4,0},{6,2},{1,5},{3,7},{5,1},{7,3},{8,12},{10,14},{12... | collective-permute-start | bytes 1179656 | tf_op jit(solution)/shard_map/ppermute | solution.py:88
  362.1 26.0 %collective-permute-start.36 = (bf16[128,1536]{1,0:T(8,128)(2,1)S(1)}, bf16[128,1536]{1,0:T(8,128)(2,1)}, u32[]{:S(2)}, u32[]{:S(2)}) collective-permute-start(bf16[128,1536]{1,0:T(8,128)(2,1)S(1)} %collective-permute-done.30.refs_1_), channel_id=1, source_target_pairs={{0,6},{2,4},{4,2},{6,0},{1,7},{3,5},{5,3},{7,1},{8,14},{10,12},{12... | collective-permute-start | bytes 1179656 | tf_op jit(solution)/shard_map/ppermute | solution.py:88
  388.1 40.4 %all-to-all-start.3 = ((bf16[4,2,128,1536]{3,2,1,0:T(8,128)(2,1)}), bf16[4,2,128,1536]{3,2,1,0:T(8,128)(2,1)}, u32[]{:S(2)}, u32[]{:S(2)}) async-start(bf16[4,2,128,1536]{3,2,1,0:T(8,128)(2,1)} %mixture.1), calls=%async_computation.3 | async-start | bytes 6291456 | tf_op jit(solution)/shard_map/all_to_all | solution.py:84
  431.2 32.8 %collective-permute-start.37 = (bf16[128,1536]{1,0:T(8,128)(2,1)S(1)}, bf16[128,1536]{1,0:T(8,128)(2,1)S(1)}, u32[]{:S(2)}, u32[]{:S(2)}) collective-permute-start(bf16[128,1536]{1,0:T(8,128)(2,1)S(1)} %fusion.11), channel_id=1, source_target_pairs={{0,1},{1,0},{2,3},{3,2},{4,5},{5,4},{6,7},{7,6},{8,9},{9,8},{10,11... | collective-permute-start | bytes 1179656 | tf_op jit(solution)/shard_map/ppermute | solution.py:88
  431.4 23.4 %collective-permute-start.39 = (bf16[1024,128]{1,0:T(8,128)(2,1)S(1)}, bf16[1024,128]{1,0:T(8,128)(2,1)S(1)}, u32[]{:S(2)}, u32[]{:S(2)}) collective-permute-start(bf16[1024,128]{1,0:T(8,128)(2,1)S(1)} %copy-done.48), channel_id=1, source_target_pairs={{0,16},{8,24},{16,0},{24,8},{1,17},{9,25},{17,1},{25,9},{2,18},{10... | collective-permute-start | bytes 786440 | tf_op jit(solution)/shard_map/ppermute | solution.py:88
  434.8 20.0 %collective-permute-start.40 = (bf16[1024,128]{1,0:T(8,128)(2,1)S(1)}, bf16[1024,128]{1,0:T(8,128)(2,1)S(1)}, u32[]{:S(2)}, u32[]{:S(2)}) collective-permute-start(bf16[1024,128]{1,0:T(8,128)(2,1)S(1)} %copy-done.47), channel_id=1, source_target_pairs={{0,24},{8,16},{16,8},{24,0},{1,25},{9,17},{17,9},{25,1},{2,26},{10... | collective-permute-start | bytes 786440 | tf_op jit(solution)/shard_map/ppermute | solution.py:88
  478.8 49.5 %collective-permute-start.41 = (bf16[128,1536]{1,0:T(8,128)(2,1)}, bf16[128,1536]{1,0:T(8,128)(2,1)S(1)}, u32[]{:S(2)}, u32[]{:S(2)}) collective-permute-start(bf16[128,1536]{1,0:T(8,128)(2,1)} %get-tuple-element.162), channel_id=1, source_target_pairs={{0,2},{2,0},{4,6},{6,4},{1,3},{3,1},{5,7},{7,5},{8,10},{10,8},{12,... | collective-permute-start | bytes 1179656 | tf_op jit(solution)/shard_map/ppermute | solution.py:88
  480.6 30.2 %collective-permute-start.47 = (bf16[128,1536]{1,0:T(8,128)(2,1)}, bf16[128,1536]{1,0:T(8,128)(2,1)}, u32[]{:S(2)}, u32[]{:S(2)}) collective-permute-start(bf16[128,1536]{1,0:T(8,128)(2,1)} %get-tuple-element.175), channel_id=1, source_target_pairs={{0,6},{2,4},{4,2},{6,0},{1,7},{3,5},{5,3},{7,1},{8,14},{10,12},{12... | collective-permute-start | bytes 1179656 | tf_op jit(solution)/shard_map/ppermute | solution.py:88
  491.8 19.0 %all-to-all-start.4 = ((bf16[8,96,640]{2,1,0:T(8,128)(2,1)}), bf16[8,96,640]{2,1,0:T(8,128)(2,1)S(1)}, u32[]{:S(2)}, u32[]{:S(2)}) async-start(bf16[8,96,640]{2,1,0:T(8,128)(2,1)} %bitcast.30), calls=%async_computation.4 | async-start | bytes 1966080 | tf_op jit(solution)/shard_map/all_to_all | solution.py:84
  497.9 30.4 %collective-permute-start.45 = (bf16[128,1536]{1,0:T(8,128)(2,1)}, bf16[128,1536]{1,0:T(8,128)(2,1)}, u32[]{:S(2)}, u32[]{:S(2)}) collective-permute-start(bf16[128,1536]{1,0:T(8,128)(2,1)} %add_convert_fusion.5), channel_id=1, source_target_pairs={{0,6},{2,4},{4,2},{6,0},{1,7},{3,5},{5,3},{7,1},{8,14},{10,12},{12... | collective-permute-start | bytes 1179656 | tf_op jit(solution)/shard_map/ppermute | solution.py:88
  (75 other events, 1047.0 us)
Sparse Core Ops, SparseCore 0:
  70.5 167.7 all-gather.1
  275.8 195.6 reduce-scatter.1

commit v3 on v2

--- a/solution.py
+++ b/solution.py
@@ -88,6 +88,11 @@
     return lax.ppermute(value, axis, [(i, i ^ mask) for i in range(2 if axis in ("zl", "co", "zh") else 4)])
 
 
+def causal_trade(value, mask, up):
+    pairs = [(i, i ^ mask) for i in range(4) if (i < i ^ mask) == up]
+    return lax.ppermute(value, "blk", pairs)
+
+
 def after(value, *others):
     return lax.optimization_barrier((value,) + others)[0]
 
@@ -106,12 +111,13 @@
     to3 = trade(blocks[5], "x", 3)
     to1 = trade(blocks[4], "x", 1)
     got3_1 = trade(blocks[7], "x", 3)
-    got1_0 = trade(blocks[2], "x", 1)
     if gate is not None:
         to3, to1, _ = lax.optimization_barrier((to3, to1, gate))
     send1 = (blocks[3].astype(f32) + to3.astype(f32)).astype(bf16)
+    got1_1 = trade(send1, "x", 1)
     send3 = (blocks[6].astype(f32) + to1.astype(f32)).astype(bf16)
-    got1_1 = trade(send1, "x", 1)
+    keep1, send3, got3_1 = lax.optimization_barrier((blocks[2], send3, got3_1))
+    got1_0 = trade(keep1, "x", 1)
     got3_0 = trade(send3, "x", 3)
     if last is not None:
         got1_1 = after(got1_1, last)
@@ -719,11 +725,10 @@
         [cotangent, jnp.pad(routes.astype(bf16), ((0, 0), (0, EXTRA - TOPK)))], axis=1
     )
     carried_partner = trade(after(carried, token_pair), "zl", 1)
+    near_rows = after(near_rows, token_pair)
     near_mine = a2a(jnp.broadcast_to(near_rows[None], (8, 96, WIDE)), ("zh", "blk"))
-    near_other = trade(near_mine, "co", 1)
-    experts_own = lax.optimization_barrier(
-        (experts_own.reshape(LOCAL_E * 96, 3 * F), near_mine, carried_partner, *token_pairs)
-    )[0]
+    near_other = trade(lax.optimization_barrier((near_mine, carried_partner, *token_pairs))[0], "co", 1)
+    experts_own = experts_own.reshape(LOCAL_E * 96, 3 * F)
     experts_full = lax.all_gather(experts_own, DPBLK, axis=0, tiled=True).reshape(16, LOCAL_E, 96, 3 * F)
 
     at_of = jnp.arange(SPAN, dtype=jnp.int32) // TOK
@@ -738,7 +743,7 @@
     router_t = tail[ROUTER_AT : ROUTER_AT + EXPERTS]
     gain_attn = tail[GAIN_AT]
     gain_ffn = tail[GAIN_AT + 1]
-    kvs = [kv_t] + [trade(kv_t, "blk", mask) for mask in (1, 2, 3)]
+    kvs = [kv_t] + [causal_trade(kv_t, mask, True) for mask in (1, 2, 3)]
     carried_pair = jnp.stack([carried, after(carried_partner, q_t)])
     carried_all = a2a(jnp.broadcast_to(carried_pair[None], (4, 2, TOK, D + EXTRA)), "x")
     mask_pos = within[:CHUNK]
@@ -785,7 +790,7 @@
     rest = jnp.pad(rest, ((0, 0), (0, 128 - GAIN_AT - 2)))
     branch_blocks = list(lax.optimization_barrier((*branch_blocks, rest))[:GROUP])
     dq_t, *dkv = attend_back(info, mask_pos, q_t, near, kvs, heads_t, logs, branch_blocks)
-    kv_parts = [dkv[0]] + [trade(dkv[mask], "blk", mask) for mask in (1, 2, 3)]
+    kv_parts = [dkv[0]] + [causal_trade(dkv[mask], mask, False) for mask in (1, 2, 3)]
     mixture_parts = a2a(lax.optimization_barrier((mixture_sums, *branch_blocks))[0], "x")
     mixture_pair = jnp.sum(after(mixture_parts, dq_t).astype(f32), axis=0)
     mixture_other = trade(mixture_pair[1].astype(bf16), "zl", 1)

time: 555 us -> 499 us (0.90)
  waiting for transfers between devices: 260 us -> 198 us
  starting transfers between devices: 85.3 us -> 94.9 us
    ppermute x49 -> x43, waiting for transfers between devices: 208 us -> 141 us  [trade(): lax.ppermute(value, axis, [(i, i ^ mask) for i in range(2 if axis in ('zl...]
    ppermute x0 -> x6, waiting for transfers between devices: none -> 38.1 us  [causal_trade(): return lax.ppermute(value, 'blk', pairs)]
    all_gather x1, waiting for transfers between devices: 22.9 us -> 0.01 us  [shards(): lax.all_gather(experts_own, DPBLK, axis=0, tiled=True)]
    ppermute x0 -> x6, starting transfers between devices: none -> 15.7 us  [causal_trade(): return lax.ppermute(value, 'blk', pairs)]
    all_to_all x5, waiting for transfers between devices: 29 us -> 19.1 us  [a2a(): return lax.all_to_all(value, axes, split_axis=0, concat_axis=0, tiled=True)]
    ppermute x49 -> x43, starting transfers between devices: 62.1 us -> 54.4 us  [trade(): lax.ppermute(value, axis, [(i, i ^ mask) for i in range(2 if axis in ('zl...]
  transfers between devices with their start and end apart: 56 -> 56, of which waited for: 34 -> 39; matrix products, arithmetic and copies ran while one was open for 9% -> 9% of each run, Pallas kernels for 14% -> 16%
where the time goes in v3:
time: 499 us; the launch traced here: 490 us
  waiting for transfers between devices  198 us (40%)
  Pallas kernels  116 us (23%)
  starting transfers between devices  94.9 us (19%)
  other arithmetic  36 us (7%)
  local copies, waits for them, and re-layouts  15.3 us (3%)
  between operations  15.3 us (3%)
  blocking collectives  10.6 us (2%)
    ppermute x43, waiting for transfers between devices, trade(): lax.ppermute(value, axis, [(i, i ^ mask) for i in range(2 if axis in ('zl...  141 us
    ppermute x43, starting transfers between devices, trade(): lax.ppermute(value, axis, [(i, i ^ mask) for i in range(2 if axis in ('zl...  54.4 us
    ppermute x6, waiting for transfers between devices, causal_trade(): return lax.ppermute(value, 'blk', pairs)  38.1 us
    pallas_call x1, Pallas kernels, expert_pass(): pl.pallas_call(expert_kernel, grid=(LOCAL_E,), out_shape=(jax.ShapeDtypeS...  37.4 us
    all_to_all x5, starting transfers between devices, a2a(): return lax.all_to_all(value, axes, split_axis=0, concat_axis=0, tiled=True)  24.7 us
    all_to_all x5, waiting for transfers between devices, a2a(): return lax.all_to_all(value, axes, split_axis=0, concat_axis=0, tiled=True)  19.1 us
    ppermute x6, starting transfers between devices, causal_trade(): return lax.ppermute(value, 'blk', pairs)  15.7 us
    pallas_call x1, Pallas kernels, expert_input_grads(): pl.pallas_call(input_grad_kernel, grid=(LOCAL_E,), out_shape=(jax.ShapeDt...  14.3 us
  transfers between devices with their start and end apart: 56, of which 39 were waited for; matrix products, arithmetic and copies ran while one was open for 9% of the time, Pallas kernels for 16%

profile of v3, /device:TPU:0, one launch (start us, length us, event | category | flops | bytes accessed | tf_op | source)
XLA Modules:
  0.0 489.7 jit_solution(6124954428289496617)
XLA Ops:
  14.5 10.6 %all_to_all.30 = bf16[8,12,640]{2,1,0:T(8,128)(2,1)S(1)} all-to-all(bf16[8,12,640]{2,1,0:T(8,128)(2,1)S(1)} %concatenate.16), channel_id=1, replica_groups=mesh['zh'=2,'co'=2,'blk'=4,'x'=4,'zl'=2] {'x','zl'}, dimensions={0} | all-to-all | bytes 245760 | tf_op jit(solution)/shard_map/all_to_all | solution.py:84
  26.4 7.5 %all-to-all-start.1 = ((bf16[8,96,640]{2,1,0:T(8,128)(2,1)}), bf16[8,96,640]{2,1,0:T(8,128)(2,1)S(1)}, u32[]{:S(2)}, u32[]{:S(2)}) async-start(bf16[8,96,640]{2,1,0:T(8,128)(2,1)} %broadcast_in_dim.72), calls=%async_computation.1 | async-start | bytes 1966080 | tf_op jit(solution)/shard_map/all_to_all | solution.py:84
  41.0 22.7 %collective-permute-done.1 = bf16[128,1664]{1,0:T(8,128)(2,1)S(1)} collective-permute-done((bf16[128,1664]{1,0:T(8,128)(2,1)S(1)}, bf16[128,1664]{1,0:T(8,128)(2,1)S(1)}, u32[]{:S(2)}, u32[]{:S(2)}) %collective-permute-start.1) | collective-permute-done | bytes 426016 | tf_op jit(solution)/shard_map/ppermute | solution.py:88
  63.7 6.5 %collective-permute-done.3.refs_2_ = bf16[2,128,1536]{2,1,0:T(8,128)(2,1)S(1)} collective-permute-done((bf16[2,128,1536]{2,1,0:T(8,128)(2,1)S(1)}, bf16[2,128,1536]{2,1,0:T(8,128)(2,1)S(1)}, u32[]{:S(2)}, u32[]{:S(2)}) %collective-permute-start.3) | collective-permute-done | bytes 786464 | tf_op jit(solution)/shard_map/ppermute | solution.py:88
  75.6 7.0 %project.1 = (bf16[16,96,640]{2,1,0:T(8,128)(2,1)}, f32[128,1536]{1,0:T(8,128)}, bf16[1024,1536]{1,0:T(8,128)(2,1)}, bf16[3,64,1024]{2,1,0:T(8,128)(2,1)}, bf16[128,1024]{1,0:T(8,128)(2,1)}) custom-call(s32[5]{0:T(128)} %stack.41.info_ref, bf16[8,96,640]{2,1,0:T(8,128)(2,1)} %copy-done.5, bf16[8,96,640]{2,1,0:T(8,128)(2,1)} %collective-permute-done.5.other_ref, ...), custom_call_target="tpu_custom_call" | custom-call | tf_op jit(solution)/shard_map/project/pallas_call | solution.py:177
  93.2 5.4 %collective-permute-start.7 = (bf16[128,1024]{1,0:T(8,128)(2,1)}, bf16[128,1024]{1,0:T(8,128)(2,1)}, u32[]{:S(2)}, u32[]{:S(2)}) collective-permute-start(bf16[128,1024]{1,0:T(8,128)(2,1)} %get-tuple-element.124.kv0), channel_id=1, source_target_pairs={{0,16},{8,24},{1,17},{9,25},{2,18},{10,26},{3,19},{11,27},{4,20},{... | collective-permute-start | bytes 786440 | tf_op jit(solution)/shard_map/ppermute | solution.py:93
  103.2 8.2 %collective-permute-done.7.kv2 = bf16[128,1024]{1,0:T(8,128)(2,1)} collective-permute-done((bf16[128,1024]{1,0:T(8,128)(2,1)}, bf16[128,1024]{1,0:T(8,128)(2,1)}, u32[]{:S(2)}, u32[]{:S(2)}) %collective-permute-start.7) | collective-permute-done | bytes 262176 | tf_op jit(solution)/shard_map/ppermute | solution.py:93
  112.6 9.9 %attend.1 = (f32[3,64,1024]{2,1,0:T(8,128)}, bf16[192,1024]{1,0:T(8,128)(2,1)}, f32[3,1,1024]{2,1,0:T(1,128)}, bf16[128,1536]{1,0:T(8,128)(2,1)}, bf16[128,1536]...) custom-call(s32[5]{0:T(128)} %stack.41.info_ref, ...), custom_call_target="tpu_custom_call" | custom-call | tf_op jit(solution)/shard_map/attend/pallas_call | solution.py:270
  126.6 11.6 %collective-permute-done.9 = bf16[128,1536]{1,0:T(8,128)(2,1)S(1)} collective-permute-done((bf16[128,1536]{1,0:T(8,128)(2,1)}, bf16[128,1536]{1,0:T(8,128)(2,1)S(1)}, u32[]{:S(2)}, u32[]{:S(2)}) %collective-permute-start.9) | collective-permute-done | bytes 393248 | tf_op jit(solution)/shard_map/ppermute | solution.py:88
  147.9 5.2 %collective-permute-done.14 = bf16[128,1536]{1,0:T(8,128)(2,1)S(1)} collective-permute-done((bf16[128,1536]{1,0:T(8,128)(2,1)S(1)}, bf16[128,1536]{1,0:T(8,128)(2,1)S(1)}, u32[]{:S(2)}, u32[]{:S(2)}) %collective-permute-start.14) | collective-permute-done | bytes 393248 | tf_op jit(solution)/shard_map/ppermute | solution.py:88
  186.8 4.3 collective-permute-done.21.refs_6_
  194.9 5.1 %collective-permute-done.20.refs_5_ = bf16[128,1536]{1,0:T(8,128)(2,1)} collective-permute-done((bf16[128,1536]{1,0:T(8,128)(2,1)S(1)}, bf16[128,1536]{1,0:T(8,128)(2,1)}, u32[]{:S(2)}, u32[]{:S(2)}) %collective-permute-start.20) | collective-permute-done | bytes 393248 | tf_op jit(solution)/shard_map/ppermute | solution.py:88
  203.7 37.4 %experts.1 = (bf16[16,5,96,1536]{3,2,1,0:T(8,128)(2,1)}, bf16[5,384,512]{2,1,0:T(8,128)(2,1)}, bf16[5,384,1024]{2,1,0:T(8,128)(2,1)}, f32[5,384,128]{2,1,0:T(8,1...) custom-call(s32[5]{0:T(128)} %stack.41.info_ref, s32[5,8,128]{2,1,0:T(8,128)} %fusion.3.rank_ref, ...), custom_call_target="tpu_custom_call" | custom-call | tf_op jit(solution)/shard_map/experts/pallas_call | solution.py:576
  241.1 14.3 %input_grads.1 = (bf16[128,1664]{1,0:T(8,128)(2,1)}, bf16[128,1664]{1,0:T(8,128)(2,1)}, bf16[128,1664]{1,0:T(8,128)(2,1)}, bf16[128,1664]{1,0:T(8,128)(2,1)}, bf...) custom-call(s32[1]{0:T(128)} %bitcast.22.first_ref, ...), custom_call_target="tpu_custom_call" | custom-call | tf_op jit(solution)/shard_map/input_grads/pallas_call | solution.py:637
  258.6 12.3 %mixture.1 = bf16[4,2,128,1536]{3,2,1,0:T(8,128)(2,1)} custom-call(s32[5]{0:T(128)} %stack.41.info_ref, s32[5,8,128]{2,1,0:T(8,128)} %fusion.3.rank_ref, bf16[5,384,512]{2,1,0:T(8,128)(2,1)} %get-tuple-element.144.act_ref, f32[5,384,128]{2,1,0:T(8,128)} %get-tuple-element.145.scale_ref, bf16[16,5,96,1536]{3,2,1,0:T(8,128)(2,1)} %bitcast.84), custom_call_target="tpu_custom_call" | custom-call | tf_op jit(solution)/shard_map/mixture/pallas_call | solution.py:671
  277.3 6.2 %collective-permute-done.28 = bf16[128,1664]{1,0:T(8,128)(2,1)S(1)} collective-permute-done((bf16[128,1664]{1,0:T(8,128)(2,1)S(1)}, bf16[128,1664]{1,0:T(8,128)(2,1)S(1)}, u32[]{:S(2)}, u32[]{:S(2)}) %collective-permute-start.28) | collective-permute-done | bytes 426016 | tf_op jit(solution)/shard_map/ppermute | solution.py:88
  284.5 4.5 collective-permute-done.26
  302.6 9.3 %collective-permute-done.30.refs_1_ = bf16[128,1536]{1,0:T(8,128)(2,1)S(1)} collective-permute-done((bf16[128,1536]{1,0:T(8,128)(2,1)S(1)}, bf16[128,1536]{1,0:T(8,128)(2,1)S(1)}, u32[]{:S(2)}, u32[]{:S(2)}) %collective-permute-start.30) | collective-permute-done | bytes 393248 | tf_op jit(solution)/shard_map/ppermute | solution.py:88
  321.5 5.8 %collective-permute-done.34.refs_5_ = bf16[128,1536]{1,0:T(8,128)(2,1)S(1)} collective-permute-done((bf16[128,1536]{1,0:T(8,128)(2,1)S(1)}, bf16[128,1536]{1,0:T(8,128)(2,1)S(1)}, u32[]{:S(2)}, u32[]{:S(2)}) %collective-permute-start.34) | collective-permute-done | bytes 393248 | tf_op jit(solution)/shard_map/ppermute | solution.py:88
  328.1 5.2 %collective-permute-done.36.refs_7_ = bf16[128,1536]{1,0:T(8,128)(2,1)} collective-permute-done((bf16[128,1536]{1,0:T(8,128)(2,1)S(1)}, bf16[128,1536]{1,0:T(8,128)(2,1)}, u32[]{:S(2)}, u32[]{:S(2)}) %collective-permute-start.36) | collective-permute-done | bytes 393248 | tf_op jit(solution)/shard_map/ppermute | solution.py:88
  333.4 4.9 all-to-all-start.3
  338.3 13.0 %attend_back.1 = (bf16[3,64,1024]{2,1,0:T(8,128)(2,1)}, bf16[1024,128]{1,0:T(8,128)(2,1)}, bf16[1024,128]{1,0:T(8,128)(2,1)}, bf16[1024,128]{1,0:T(8,128)(2,1)}, bf16[1024,128]{1,0:T(8,128)(2,1)}) custom-call(s32[5]{0:T(128)} %stack.41.info_ref, s32[1,512]{1,0:T(1,128)} %bitcast.97, s32[512,1]{1,0:T(8,128)} %copy.63.pos_col, ...), custom_call_target="tpu_custom_call" | custom-call | tf_op jit(solution)/shard_map/attend_back/pallas_call | solution.py:346
  351.2 13.1 %all-to-all-done.3 = bf16[4,2,128,1536]{3,2,1,0:T(8,128)(2,1)} async-done(((bf16[4,2,128,1536]{3,2,1,0:T(8,128)(2,1)}), bf16[4,2,128,1536]{3,2,1,0:T(8,128)(2,1)}, u32[]{:S(2)}, u32[]{:S(2)}) %all-to-all-start.3) | async-done | bytes 3145760 | tf_op jit(solution)/shard_map/all_to_all | solution.py:84
  375.3 8.1 %collective-permute-done.39.kv2 = bf16[1024,128]{1,0:T(8,128)(2,1)S(1)} collective-permute-done((bf16[1024,128]{1,0:T(8,128)(2,1)S(1)}, bf16[1024,128]{1,0:T(8,128)(2,1)S(1)}, u32[]{:S(2)}, u32[]{:S(2)}) %collective-permute-start.39) | collective-permute-done | bytes 262176 | tf_op jit(solution)/shard_map/ppermute | solution.py:93
  383.4 14.7 %collective-permute-done.40.kv3 = bf16[1024,128]{1,0:T(8,128)(2,1)S(1)} collective-permute-done((bf16[1024,128]{1,0:T(8,128)(2,1)S(1)}, bf16[1024,128]{1,0:T(8,128)(2,1)S(1)}, u32[]{:S(2)}, u32[]{:S(2)}) %collective-permute-start.40) | collective-permute-done | bytes 262176 | tf_op jit(solution)/shard_map/ppermute | solution.py:93
  398.9 7.7 %turn_back.1 = (bf16[128,1536]{1,0:T(8,128)(2,1)}, bf16[128,1536]{1,0:T(8,128)(2,1)}, bf16[128,1536]{1,0:T(8,128)(2,1)}, bf16[128,1536]{1,0:T(8,128)(2,1)}, bf16...) custom-call(bf16[16,96,640]{2,1,0:T(8,128)(2,1)} %get-tuple-element., ...), custom_call_target="tpu_custom_call" | custom-call | tf_op jit(solution)/shard_map/turn_back/pallas_call | solution.py:398
  407.6 8.7 %weight_grads.1 = bf16[2,2,4,96,640]{4,3,2,1,0:T(8,128)(2,1)} custom-call(s32[5]{0:T(128)} %stack.41.info_ref, bf16[1024,1536]{1,0:T(8,128)(2,1)} %get-tuple-element.183.normed_ref, bf16[1024,320]{1,0:T(8,128)(2,1)} %get-tuple-element.184.mixed_ref, bf16[192,1024]{1,0:T(8,128)(2,1)} %get-tuple-element.185.heads_ref, f32[1536,128]{1,0:T(8,128)} %pad.14.rest_ref, ...), custom_call_target="tpu_custom_call" | custom-call | tf_op jit(solution)/shard_map/weight_grads/pallas_call | solution.py:432
  422.3 9.3 %collective-permute-done.41 = bf16[128,1536]{1,0:T(8,128)(2,1)S(1)} collective-permute-done((bf16[128,1536]{1,0:T(8,128)(2,1)S(1)}, bf16[128,1536]{1,0:T(8,128)(2,1)S(1)}, u32[]{:S(2)}, u32[]{:S(2)}) %collective-permute-start.41) | collective-permute-done | bytes 393248 | tf_op jit(solution)/shard_map/ppermute | solution.py:88
  434.0 4.3 all-to-all-start.4
  444.2 6.4 %collective-permute-done.47 = bf16[128,1536]{1,0:T(8,128)(2,1)} collective-permute-done((bf16[128,1536]{1,0:T(8,128)(2,1)S(1)}, bf16[128,1536]{1,0:T(8,128)(2,1)}, u32[]{:S(2)}, u32[]{:S(2)}) %collective-permute-start.47) | collective-permute-done | bytes 393248 | tf_op jit(solution)/shard_map/ppermute | solution.py:88
  458.2 6.3 %multiply_subtract_fusion = (f32[5,96,1024]{2,1,0:T(8,128)}, f32[5,96,1024]{2,1,0:T(8,128)}, f32[5,96,1024]{2,1,0:T(8,128)}) fusion(f32[5,96,1024]{2,1,0:T(8,128)S(1)} %copy-done.1, bf16[5,96,1536]{2,1,0:T(8,128)(2,1)} %bitcast.88, f32[5,96,1024]{2,1,0:T(8,128)} %param.38, f32[5,96,1024]{2,1,0:T(8,128)} %param.39), kind=kLoop, calls=%fused_computation.8 | loop fusion | flops 7864320 | bytes 12779520 | tf_op jit(solution)/shard_map/sub | solution.py:77
  468.4 4.3 all-to-all-start.5
  (291 shorter events, 174.5 us)
Async XLA Ops:
  7.2 196.5 %all-gather.2.cloned.1.call-start = ((), (), s32[]{:S(2)}) async-start(), calls=%async_computation.7 | async-start | bytes 25067520 | tf_op jit(solution)/shard_map/all_gather | solution.py:732
  26.4 46.5 %all-to-all-start.1 = ((bf16[8,96,640]{2,1,0:T(8,128)(2,1)}), bf16[8,96,640]{2,1,0:T(8,128)(2,1)S(1)}, u32[]{:S(2)}, u32[]{:S(2)}) async-start(bf16[8,96,640]{2,1,0:T(8,128)(2,1)} %broadcast_in_dim.72), calls=%async_computation.1 | async-start | bytes 1966080 | tf_op jit(solution)/shard_map/all_to_all | solution.py:84
  33.8 29.8 %collective-permute-start.2 = (bf16[2,128,1536]{2,1,0:T(8,128)(2,1)S(1)}, bf16[2,128,1536]{2,1,0:T(8,128)(2,1)S(1)}, u32[]{:S(2)}, u32[]{:S(2)}) collective-permute-start(bf16[2,128,1536]{2,1,0:T(8,128)(2,1)S(1)} %pad_maximum_fusion.2.refs_0_), channel_id=1, source_target_pairs={{0,2},{2,0},{4,6},{6,4},{1,3},{3,1},{5,7},{7,5},{8,10},{10,8},{12,... | collective-permute-start | bytes 2359304 | tf_op jit(solution)/shard_map/ppermute | solution.py:88
  34.8 35.4 %collective-permute-start.3 = (bf16[2,128,1536]{2,1,0:T(8,128)(2,1)S(1)}, bf16[2,128,1536]{2,1,0:T(8,128)(2,1)S(1)}, u32[]{:S(2)}, u32[]{:S(2)}) collective-permute-start(bf16[2,128,1536]{2,1,0:T(8,128)(2,1)S(1)} %pad_maximum_fusion.2.refs_0_), channel_id=1, source_target_pairs={{0,4},{2,6},{4,0},{6,2},{1,5},{3,7},{5,1},{7,3},{8,12},{10,14},{12... | collective-permute-start | bytes 2359304 | tf_op jit(solution)/shard_map/ppermute | solution.py:88
  37.5 35.3 %collective-permute-start.4 = (bf16[2,128,1536]{2,1,0:T(8,128)(2,1)S(1)}, bf16[2,128,1536]{2,1,0:T(8,128)(2,1)}, u32[]{:S(2)}, u32[]{:S(2)}) collective-permute-start(bf16[2,128,1536]{2,1,0:T(8,128)(2,1)S(1)} %pad_maximum_fusion.2.refs_0_), channel_id=1, source_target_pairs={{0,6},{2,4},{4,2},{6,0},{1,7},{3,5},{5,3},{7,1},{8,14},{10,12},{12... | collective-permute-start | bytes 2359304 | tf_op jit(solution)/shard_map/ppermute | solution.py:88
  40.5 23.2 %collective-permute-start.1 = (bf16[128,1664]{1,0:T(8,128)(2,1)S(1)}, bf16[128,1664]{1,0:T(8,128)(2,1)S(1)}, u32[]{:S(2)}, u32[]{:S(2)}) collective-permute-start(bf16[128,1664]{1,0:T(8,128)(2,1)S(1)} %get-tuple-element.119), channel_id=1, source_target_pairs={{0,1},{1,0},{2,3},{3,2},{4,5},{5,4},{6,7},{7,6},{8,9},{9,8},{10,11... | collective-permute-start | bytes 1277960 | tf_op jit(solution)/shard_map/ppermute | solution.py:88
  85.2 53.8 %all-to-all-start.2 = ((bf16[4,2,128,1664]{3,2,1,0:T(8,128)(2,1)}), bf16[4,2,128,1664]{3,2,1,0:T(8,128)(2,1)S(1)}, u32[]{:S(2)}, u32[]{:S(2)}) async-start(bf16[4,2,128,1664]{3,2,1,0:T(8,128)(2,1)} %broadcast_in_dim.75), calls=%async_computation.2 | async-start | bytes 6815744 | tf_op jit(solution)/shard_map/all_to_all | solution.py:84
  88.9 369.2 %reduce-scatter.2.cloned.1.call-start = ((), (), s32[]{:S(2)}) async-start(), calls=%async_computation.8 | async-start | bytes 25067520 | tf_op jit(solution)/shard_map/reduce_scatter | solution.py:772
  93.2 18.3 %collective-permute-start.7 = (bf16[128,1024]{1,0:T(8,128)(2,1)}, bf16[128,1024]{1,0:T(8,128)(2,1)}, u32[]{:S(2)}, u32[]{:S(2)}) collective-permute-start(bf16[128,1024]{1,0:T(8,128)(2,1)} %get-tuple-element.124.kv0), channel_id=1, source_target_pairs={{0,16},{8,24},{1,17},{9,25},{2,18},{10,26},{3,19},{11,27},{4,20},{... | collective-permute-start | bytes 786440 | tf_op jit(solution)/shard_map/ppermute | solution.py:93
  122.5 15.7 %collective-permute-start.9 = (bf16[128,1536]{1,0:T(8,128)(2,1)}, bf16[128,1536]{1,0:T(8,128)(2,1)S(1)}, u32[]{:S(2)}, u32[]{:S(2)}) collective-permute-start(bf16[128,1536]{1,0:T(8,128)(2,1)} %get-tuple-element.128), channel_id=1, source_target_pairs={{0,6},{2,4},{4,2},{6,0},{1,7},{3,5},{5,3},{7,1},{8,14},{10,12},{12... | collective-permute-start | bytes 1179656 | tf_op jit(solution)/shard_map/ppermute | solution.py:88
  125.5 21.2 %collective-permute-start.11 = (bf16[128,1536]{1,0:T(8,128)(2,1)}, bf16[128,1536]{1,0:T(8,128)(2,1)}, u32[]{:S(2)}, u32[]{:S(2)}) collective-permute-start(bf16[128,1536]{1,0:T(8,128)(2,1)} %get-tuple-element.132), channel_id=1, source_target_pairs={{0,6},{2,4},{4,2},{6,0},{1,7},{3,5},{5,3},{7,1},{8,14},{10,12},{12... | collective-permute-start | bytes 1179656 | tf_op jit(solution)/shard_map/ppermute | solution.py:88
  167.3 19.5 %collective-permute-start.19 = (bf16[128,1536]{1,0:T(8,128)(2,1)S(1)}, bf16[128,1536]{1,0:T(8,128)(2,1)S(1)}, u32[]{:S(2)}, u32[]{:S(2)}) collective-permute-start(bf16[128,1536]{1,0:T(8,128)(2,1)S(1)} %multiply_convert_fusion.1.refs_0_), channel_id=1, source_target_pairs={{0,4},{2,6},{4,0},{6,2},{1,5},{3,7},{5,1},{7,3},{8,12},{10,14},{12... | collective-permute-start | bytes 1179656 | tf_op jit(solution)/shard_map/ppermute | solution.py:88
  169.4 21.7 %collective-permute-start.21 = (bf16[128,1536]{1,0:T(8,128)(2,1)S(1)}, bf16[128,1536]{1,0:T(8,128)(2,1)S(1)}, u32[]{:S(2)}, u32[]{:S(2)}) collective-permute-start(bf16[128,1536]{1,0:T(8,128)(2,1)S(1)} %multiply_convert_fusion.1.refs_0_), channel_id=1, source_target_pairs={{0,6},{2,4},{4,2},{6,0},{1,7},{3,5},{5,3},{7,1},{8,14},{10,12},{12... | collective-permute-start | bytes 1179656 | tf_op jit(solution)/shard_map/ppermute | solution.py:88
  173.0 21.9 %collective-permute-start.18 = (bf16[128,1536]{1,0:T(8,128)(2,1)S(1)}, bf16[128,1536]{1,0:T(8,128)(2,1)}, u32[]{:S(2)}, u32[]{:S(2)}) collective-permute-start(bf16[128,1536]{1,0:T(8,128)(2,1)S(1)} %collective-permute-done.16.refs_1_), channel_id=1, source_target_pairs={{0,2},{2,0},{4,6},{6,4},{1,3},{3,1},{5,7},{7,5},{8,10},{10,8},{12,... | collective-permute-start | bytes 1179656 | tf_op jit(solution)/shard_map/ppermute | solution.py:88
  173.4 26.7 %collective-permute-start.20 = (bf16[128,1536]{1,0:T(8,128)(2,1)S(1)}, bf16[128,1536]{1,0:T(8,128)(2,1)}, u32[]{:S(2)}, u32[]{:S(2)}) collective-permute-start(bf16[128,1536]{1,0:T(8,128)(2,1)S(1)} %collective-permute-done.16.refs_1_), channel_id=1, source_target_pairs={{0,4},{2,6},{4,0},{6,2},{1,5},{3,7},{5,1},{7,3},{8,12},{10,14},{12... | collective-permute-start | bytes 1179656 | tf_op jit(solution)/shard_map/ppermute | solution.py:88
  177.9 25.8 %collective-permute-start.22 = (bf16[128,1536]{1,0:T(8,128)(2,1)S(1)}, bf16[128,1536]{1,0:T(8,128)(2,1)}, u32[]{:S(2)}, u32[]{:S(2)}) collective-permute-start(bf16[128,1536]{1,0:T(8,128)(2,1)S(1)} %collective-permute-done.16.refs_1_), channel_id=1, source_target_pairs={{0,6},{2,4},{4,2},{6,0},{1,7},{3,5},{5,3},{7,1},{8,14},{10,12},{12... | collective-permute-start | bytes 1179656 | tf_op jit(solution)/shard_map/ppermute | solution.py:88
  255.4 15.6 %collective-permute-start.23 = (bf16[128,1664]{1,0:T(8,128)(2,1)}, bf16[128,1664]{1,0:T(8,128)(2,1)S(1)}, u32[]{:S(2)}, u32[]{:S(2)}) collective-permute-start(bf16[128,1664]{1,0:T(8,128)(2,1)} %get-tuple-element.148), channel_id=1, source_target_pairs={{0,6},{2,4},{4,2},{6,0},{1,7},{3,5},{5,3},{7,1},{8,14},{10,12},{12... | collective-permute-start | bytes 1277960 | tf_op jit(solution)/shard_map/ppermute | solution.py:88
  257.6 17.4 %collective-permute-start.25 = (bf16[128,1664]{1,0:T(8,128)(2,1)}, bf16[128,1664]{1,0:T(8,128)(2,1)S(1)}, u32[]{:S(2)}, u32[]{:S(2)}) collective-permute-start(bf16[128,1664]{1,0:T(8,128)(2,1)} %get-tuple-element.151), channel_id=1, source_target_pairs={{0,6},{2,4},{4,2},{6,0},{1,7},{3,5},{5,3},{7,1},{8,14},{10,12},{12... | collective-permute-start | bytes 1277960 | tf_op jit(solution)/shard_map/ppermute | solution.py:88
  295.7 16.2 %collective-permute-start.30 = (bf16[128,1536]{1,0:T(8,128)(2,1)S(1)}, bf16[128,1536]{1,0:T(8,128)(2,1)S(1)}, u32[]{:S(2)}, u32[]{:S(2)}) collective-permute-start(bf16[128,1536]{1,0:T(8,128)(2,1)S(1)} %get-tuple-element.159.refs_0_), channel_id=1, source_target_pairs={{0,1},{1,0},{2,3},{3,2},{4,5},{5,4},{6,7},{7,6},{8,9},{9,8},{10,11... | collective-permute-start | bytes 1179656 | tf_op jit(solution)/shard_map/ppermute | solution.py:88
  295.7 21.6 %collective-permute-start.31 = (bf16[128,1536]{1,0:T(8,128)(2,1)S(1)}, bf16[128,1536]{1,0:T(8,128)(2,1)S(1)}, u32[]{:S(2)}, u32[]{:S(2)}) collective-permute-start(bf16[128,1536]{1,0:T(8,128)(2,1)S(1)} %get-tuple-element.159.refs_0_), channel_id=1, source_target_pairs={{0,2},{2,0},{4,6},{6,4},{1,3},{3,1},{5,7},{7,5},{8,10},{10,8},{12,... | collective-permute-start | bytes 1179656 | tf_op jit(solution)/shard_map/ppermute | solution.py:88
  299.3 20.2 %collective-permute-start.33 = (bf16[128,1536]{1,0:T(8,128)(2,1)S(1)}, bf16[128,1536]{1,0:T(8,128)(2,1)S(1)}, u32[]{:S(2)}, u32[]{:S(2)}) collective-permute-start(bf16[128,1536]{1,0:T(8,128)(2,1)S(1)} %get-tuple-element.159.refs_0_), channel_id=1, source_target_pairs={{0,4},{2,6},{4,0},{6,2},{1,5},{3,7},{5,1},{7,3},{8,12},{10,14},{12... | collective-permute-start | bytes 1179656 | tf_op jit(solution)/shard_map/ppermute | solution.py:88
  301.2 19.1 %collective-permute-start.35 = (bf16[128,1536]{1,0:T(8,128)(2,1)S(1)}, bf16[128,1536]{1,0:T(8,128)(2,1)S(1)}, u32[]{:S(2)}, u32[]{:S(2)}) collective-permute-start(bf16[128,1536]{1,0:T(8,128)(2,1)S(1)} %get-tuple-element.159.refs_0_), channel_id=1, source_target_pairs={{0,6},{2,4},{4,2},{6,0},{1,7},{3,5},{5,3},{7,1},{8,14},{10,12},{12... | collective-permute-start | bytes 1179656 | tf_op jit(solution)/shard_map/ppermute | solution.py:88
  317.3 16.1 %collective-permute-start.36 = (bf16[128,1536]{1,0:T(8,128)(2,1)S(1)}, bf16[128,1536]{1,0:T(8,128)(2,1)}, u32[]{:S(2)}, u32[]{:S(2)}) collective-permute-start(bf16[128,1536]{1,0:T(8,128)(2,1)S(1)} %collective-permute-done.30.refs_1_), channel_id=1, source_target_pairs={{0,6},{2,4},{4,2},{6,0},{1,7},{3,5},{5,3},{7,1},{8,14},{10,12},{12... | collective-permute-start | bytes 1179656 | tf_op jit(solution)/shard_map/ppermute | solution.py:88
  333.4 30.9 %all-to-all-start.3 = ((bf16[4,2,128,1536]{3,2,1,0:T(8,128)(2,1)}), bf16[4,2,128,1536]{3,2,1,0:T(8,128)(2,1)}, u32[]{:S(2)}, u32[]{:S(2)}) async-start(bf16[4,2,128,1536]{3,2,1,0:T(8,128)(2,1)} %mixture.1), calls=%async_computation.3 | async-start | bytes 6291456 | tf_op jit(solution)/shard_map/all_to_all | solution.py:84
  366.9 39.7 %collective-permute-start.37 = (bf16[128,1536]{1,0:T(8,128)(2,1)S(1)}, bf16[128,1536]{1,0:T(8,128)(2,1)S(1)}, u32[]{:S(2)}, u32[]{:S(2)}) collective-permute-start(bf16[128,1536]{1,0:T(8,128)(2,1)S(1)} %fusion.11), channel_id=1, source_target_pairs={{0,1},{1,0},{2,3},{3,2},{4,5},{5,4},{6,7},{7,6},{8,9},{9,8},{10,11... | collective-permute-start | bytes 1179656 | tf_op jit(solution)/shard_map/ppermute | solution.py:88
  369.7 28.5 %collective-permute-start.40 = (bf16[1024,128]{1,0:T(8,128)(2,1)S(1)}, bf16[1024,128]{1,0:T(8,128)(2,1)S(1)}, u32[]{:S(2)}, u32[]{:S(2)}) collective-permute-start(bf16[1024,128]{1,0:T(8,128)(2,1)S(1)} %copy-done.54), channel_id=1, source_target_pairs={{16,8},{24,0},{17,9},{25,1},{18,10},{26,2},{19,11},{27,3},{20,12},... | collective-permute-start | bytes 786440 | tf_op jit(solution)/shard_map/ppermute | solution.py:93
  417.7 15.1 %collective-permute-start.43 = (bf16[2,4,96,640]{3,2,1,0:T(8,128)(2,1)S(1)}, bf16[2,4,96,640]{3,2,1,0:T(8,128)(2,1)S(1)}, u32[]{:S(2)}, u32[]{:S(2)}) collective-permute-start(bf16[2,4,96,640]{3,2,1,0:T(8,128)(2,1)S(1)} %slice_bitcast_fusion), channel_id=1, source_target_pairs={{0,32},{32,0},{1,33},{33,1},{2,34},{34,2},{3,35},{35,3},{4,36},{36... | collective-permute-start | bytes 2949128 | tf_op jit(solution)/shard_map/ppermute | solution.py:88
  421.5 19.3 %collective-permute-start.44 = (bf16[128,1536]{1,0:T(8,128)(2,1)}, bf16[128,1536]{1,0:T(8,128)(2,1)}, u32[]{:S(2)}, u32[]{:S(2)}) collective-permute-start(bf16[128,1536]{1,0:T(8,128)(2,1)} %get-tuple-element.188), channel_id=1, source_target_pairs={{0,6},{2,4},{4,2},{6,0},{1,7},{3,5},{5,3},{7,1},{8,14},{10,12},{12... | collective-permute-start | bytes 1179656 | tf_op jit(solution)/shard_map/ppermute | solution.py:88
  434.0 20.3 %all-to-all-start.4 = ((bf16[8,96,640]{2,1,0:T(8,128)(2,1)}), bf16[8,96,640]{2,1,0:T(8,128)(2,1)S(1)}, u32[]{:S(2)}, u32[]{:S(2)}) async-start(bf16[8,96,640]{2,1,0:T(8,128)(2,1)} %bitcast.30), calls=%async_computation.4 | async-start | bytes 1966080 | tf_op jit(solution)/shard_map/all_to_all | solution.py:84
  440.8 31.8 %collective-permute-start.45 = (bf16[128,1536]{1,0:T(8,128)(2,1)}, bf16[128,1536]{1,0:T(8,128)(2,1)S(1)}, u32[]{:S(2)}, u32[]{:S(2)}) collective-permute-start(bf16[128,1536]{1,0:T(8,128)(2,1)} %get-tuple-element.189), channel_id=1, source_target_pairs={{0,2},{2,0},{4,6},{6,4},{1,3},{3,1},{5,7},{7,5},{8,10},{10,8},{12,... | collective-permute-start | bytes 1179656 | tf_op jit(solution)/shard_map/ppermute | solution.py:88
  442.4 30.3 %collective-permute-start.46 = (bf16[128,1536]{1,0:T(8,128)(2,1)}, bf16[128,1536]{1,0:T(8,128)(2,1)}, u32[]{:S(2)}, u32[]{:S(2)}) collective-permute-start(bf16[128,1536]{1,0:T(8,128)(2,1)} %add_convert_fusion.5), channel_id=1, source_target_pairs={{0,6},{2,4},{4,2},{6,0},{1,7},{3,5},{5,3},{7,1},{8,14},{10,12},{12... | collective-permute-start | bytes 1179656 | tf_op jit(solution)/shard_map/ppermute | solution.py:88
  456.4 16.3 %collective-permute-start.48 = (bf16[128,1536]{1,0:T(8,128)(2,1)}, bf16[128,1536]{1,0:T(8,128)(2,1)}, u32[]{:S(2)}, u32[]{:S(2)}) collective-permute-start(bf16[128,1536]{1,0:T(8,128)(2,1)} %add_convert_fusion.3), channel_id=1, source_target_pairs={{0,1},{1,0},{2,3},{3,2},{4,5},{5,4},{6,7},{7,6},{8,9},{9,8},{10,11... | collective-permute-start | bytes 1179656 | tf_op jit(solution)/shard_map/ppermute | solution.py:88
  (82 other events, 888.3 us)
Sparse Core Ops, SparseCore 0:
  11.6 161.2 all-gather.1
  241.2 212.1 reduce-scatter.1

commit v4 on v3

--- a/solution.py
+++ b/solution.py
@@ -410,7 +410,7 @@
 
 def weight_grad_kernel(info_ref, normed_ref, mixed_ref, heads_ref, rest_ref, gain_ref, *refs):
     branches = refs[:GROUP]
-    out_ref = refs[GROUP]
+    keep_ref, give_ref = refs[GROUP:]
     in_grad = dot(normed_ref[...], mixed_ref[...], ((0,), (0,)))
     out_grad = jnp.zeros((384, QW), f32)
     for at in range(GROUP):
@@ -419,11 +419,21 @@
     lane = lax.broadcasted_iota(jnp.int32, (384, 128), 1)
     column = jnp.broadcast_to(gain_ref[...], (128, 384)).T
     rest = jnp.where(lane == GAIN_AT, column, rest_ref[...])
-    out_ref[0, 0, :, :, :320] = in_grad.astype(bf16).reshape(4, 96, 320)
-    out_ref[0, 0, :, :, 320:384] = jnp.zeros((4, 96, 64), bf16)
-    out_ref[0, 0, :, :, 384:512] = out_grad[:, :128].astype(bf16).reshape(4, 96, 128)
     last = jnp.concatenate([out_grad[:, 128:], rest[:, 64:]], axis=1)
-    out_ref[0, 0, :, :, 512:] = last.astype(bf16).reshape(4, 96, 128)
+
+    def write(out_ref):
+        out_ref[0, :, :, :320] = in_grad.astype(bf16).reshape(4, 96, 320)
+        out_ref[0, :, :, 320:384] = jnp.zeros((4, 96, 64), bf16)
+        out_ref[0, :, :, 384:512] = out_grad[:, :128].astype(bf16).reshape(4, 96, 128)
+        out_ref[0, :, :, 512:] = last.astype(bf16).reshape(4, 96, 128)
+
+    @pl.when(pl.program_id(0) == 0)
+    def _():
+        write(keep_ref)
+
+    @pl.when(pl.program_id(0) == 1)
+    def _():
+        write(give_ref)
 
 
 def weight_grads(info, normed_all, mixed_grad, heads, rest, gain, branch_blocks):
@@ -442,9 +452,12 @@
                 pl.BlockSpec((1, 384), lambda r, zh, info: (0, step(r, zh, info))),
             ]
             + [pl.BlockSpec((TOK, 384), lambda r, zh, info: (0, step(r, zh, info)))] * GROUP,
-            out_specs=pl.BlockSpec((1, 1, 4, 96, WIDE), lambda r, zh, info: (r, zh, 0, 0, 0)),
+            out_specs=(
+                pl.BlockSpec((1, 4, 96, WIDE), lambda r, zh, info: (jnp.maximum(r, zh), 0, 0, 0)),
+                pl.BlockSpec((1, 4, 96, WIDE), lambda r, zh, info: (r * zh, 0, 0, 0)),
+            ),
         ),
-        out_shape=jax.ShapeDtypeStruct((2, 2, 4, 96, WIDE), bf16),
+        out_shape=(jax.ShapeDtypeStruct((2, 4, 96, WIDE), bf16),) * 2,
         compiler_params=pltpu.CompilerParams(vmem_limit_bytes=VMEM_LIMIT),
         cost_estimate=NO_COST,
         name="weight_grads",
@@ -799,18 +812,18 @@
     *normed_parts, mixed_grad, gain_attn_grad = turn_back(near, tail, cosine, sine, dq_t, kv_parts, token_pairs)
     layer_out = hidden + residual_scale * (mixture_pair[0] + mixture_other.astype(f32))
     normed_all, layer_out = lax.optimization_barrier((normed_all, layer_out))
-    grads = weight_grads(info, normed_all, mixed_grad, heads_low, rest, gain_attn_grad, branch_blocks)
-    both_cores = grads[0].astype(f32) + trade(grads[1], "co", 1).astype(f32)
+    keep, give = weight_grads(info, normed_all, mixed_grad, heads_low, rest, gain_attn_grad, branch_blocks)
+    both_cores = keep.astype(f32) + trade(give, "co", 1).astype(f32)
     row_parts = a2a(both_cores.astype(bf16).reshape(8, 96, WIDE), ("zh", "blk"))
-    tokens_grad = token_grads(tail, tokens, hidden_grad, collect(normed_parts, both_cores, row_parts))
+    tokens_grad = token_grads(tail, tokens, hidden_grad, collect(normed_parts, None, row_parts))
 
     row_sum = jnp.sum(row_parts.astype(f32), axis=0).astype(bf16)
     up_sum = expert_sum[:, :, : 2 * F].astype(f32)
     down_sum = jnp.swapaxes(expert_sum[:, :, 2 * F :], 1, 2).astype(f32)
     up_state = adam_update(expert_up, expert_up_first, expert_up_second, up_sum, rate_expert_up)
     down_state = adam_update(expert_down, expert_down_first, expert_down_second, down_sum, rate_expert_down)
-    row_sum, *expert_state = lax.optimization_barrier((row_sum, *up_state, *down_state))
     owned = a2a(row_sum.reshape(GROUP, 12, WIDE), ULYS)
+    owned, *expert_state = lax.optimization_barrier((owned, *up_state, *down_state))
     small_state = small_updates(
         owned,
         (

time: 499 us -> 500 us (level)
  the two profiles are of different devices: /device:TPU:0 before, /device:TPU:12 now
where the time goes in v4:
time: 500 us; the launch traced here: 491 us
  waiting for transfers between devices  164 us (33%)
  Pallas kernels  127 us (25%)
  starting transfers between devices  121 us (24%)
  other arithmetic  36.1 us (7%)
  between operations  15.3 us (3%)
  local copies, waits for them, and re-layouts  14 us (3%)
  blocking collectives  9.98 us (2%)
    ppermute x43, waiting for transfers between devices, trade(): lax.ppermute(value, axis, [(i, i ^ mask) for i in range(2 if axis in ('zl...  111 us
    ppermute x43, starting transfers between devices, trade(): lax.ppermute(value, axis, [(i, i ^ mask) for i in range(2 if axis in ('zl...  63 us
    ppermute x6, waiting for transfers between devices, causal_trade(): return lax.ppermute(value, 'blk', pairs)  41.3 us
    pallas_call x1, Pallas kernels, expert_pass(): pl.pallas_call(expert_kernel, grid=(LOCAL_E,), out_shape=(jax.ShapeDtypeS...  37.4 us
    all_to_all x5, starting transfers between devices, a2a(): return lax.all_to_all(value, axes, split_axis=0, concat_axis=0, tiled=True)  32.7 us
    ppermute x6, starting transfers between devices, causal_trade(): return lax.ppermute(value, 'blk', pairs)  25 us
    pallas_call x1, Pallas kernels, attend_back(): pl.pallas_call(attend_back_kernel, out_shape=(jax.ShapeDtypeStruct((3, HD...  21.7 us
    pallas_call x1, Pallas kernels, expert_input_grads(): pl.pallas_call(input_grad_kernel, grid=(LOCAL_E,), out_shape=(jax.ShapeDt...  14.3 us
  transfers between devices with their start and end apart: 56, of which 34 were waited for; matrix products, arithmetic and copies ran while one was open for 9% of the time, Pallas kernels for 18%

profile of v4, /device:TPU:12, one launch (start us, length us, event | category | flops | bytes accessed | tf_op | source)
XLA Modules:
  0.0 490.9 jit_solution(6727837667506095409)
XLA Ops:
  14.4 10.0 %all_to_all.30 = bf16[8,12,640]{2,1,0:T(8,128)(2,1)S(1)} all-to-all(bf16[8,12,640]{2,1,0:T(8,128)(2,1)S(1)} %concatenate.16), channel_id=1, replica_groups=mesh['zh'=2,'co'=2,'blk'=4,'x'=4,'zl'=2] {'x','zl'}, dimensions={0} | all-to-all | bytes 245760 | tf_op jit(solution)/shard_map/all_to_all | solution.py:84
  25.6 8.1 %all-to-all-start.1 = ((bf16[8,96,640]{2,1,0:T(8,128)(2,1)}), bf16[8,96,640]{2,1,0:T(8,128)(2,1)S(1)}, u32[]{:S(2)}, u32[]{:S(2)}) async-start(bf16[8,96,640]{2,1,0:T(8,128)(2,1)} %broadcast_in_dim.72), calls=%async_computation.1 | async-start | bytes 1966080 | tf_op jit(solution)/shard_map/all_to_all | solution.py:84
  40.1 23.3 %collective-permute-done.1 = bf16[128,1664]{1,0:T(8,128)(2,1)S(1)} collective-permute-done((bf16[128,1664]{1,0:T(8,128)(2,1)S(1)}, bf16[128,1664]{1,0:T(8,128)(2,1)S(1)}, u32[]{:S(2)}, u32[]{:S(2)}) %collective-permute-start.1) | collective-permute-done | bytes 426016 | tf_op jit(solution)/shard_map/ppermute | solution.py:88
  63.5 4.4 collective-permute-done.3.refs_2_
  72.2 6.3 %project.1 = (bf16[16,96,640]{2,1,0:T(8,128)(2,1)}, f32[128,1536]{1,0:T(8,128)}, bf16[1024,1536]{1,0:T(8,128)(2,1)}, bf16[3,64,1024]{2,1,0:T(8,128)(2,1)}, bf16[128,1024]{1,0:T(8,128)(2,1)}) custom-call(s32[5]{0:T(128)} %stack.41.info_ref, bf16[8,96,640]{2,1,0:T(8,128)(2,1)} %copy-done.4, bf16[8,96,640]{2,1,0:T(8,128)(2,1)} %collective-permute-done.5.other_ref, ...), custom_call_target="tpu_custom_call" | custom-call | tf_op jit(solution)/shard_map/project/pallas_call | solution.py:177
  80.6 8.7 %all-to-all-start.2 = ((bf16[4,2,128,1664]{3,2,1,0:T(8,128)(2,1)}), bf16[4,2,128,1664]{3,2,1,0:T(8,128)(2,1)S(1)}, u32[]{:S(2)}, u32[]{:S(2)}) async-start(bf16[4,2,128,1664]{3,2,1,0:T(8,128)(2,1)} %broadcast_in_dim.75), calls=%async_computation.2 | async-start | bytes 6815744 | tf_op jit(solution)/shard_map/all_to_all | solution.py:84
  90.6 4.8 collective-permute-start.7
  99.4 5.3 %collective-permute-done.6.kv1 = bf16[128,1024]{1,0:T(8,128)(2,1)} collective-permute-done((bf16[128,1024]{1,0:T(8,128)(2,1)}, bf16[128,1024]{1,0:T(8,128)(2,1)}, u32[]{:S(2)}, u32[]{:S(2)}) %collective-permute-start.6) | collective-permute-done | bytes 262176 | tf_op jit(solution)/shard_map/ppermute | solution.py:93
  104.6 8.3 %collective-permute-done.8.kv3 = bf16[128,1024]{1,0:T(8,128)(2,1)} collective-permute-done((bf16[128,1024]{1,0:T(8,128)(2,1)}, bf16[128,1024]{1,0:T(8,128)(2,1)}, u32[]{:S(2)}, u32[]{:S(2)}) %collective-permute-start.8) | collective-permute-done | bytes 262176 | tf_op jit(solution)/shard_map/ppermute | solution.py:93
  113.0 14.1 %attend.1 = (f32[3,64,1024]{2,1,0:T(8,128)}, bf16[192,1024]{1,0:T(8,128)(2,1)}, f32[3,1,1024]{2,1,0:T(1,128)}, bf16[128,1536]{1,0:T(8,128)(2,1)}, bf16[128,1536]...) custom-call(s32[5]{0:T(128)} %stack.41.info_ref, ...), custom_call_target="tpu_custom_call" | custom-call | tf_op jit(solution)/shard_map/attend/pallas_call | solution.py:270
  130.8 8.5 %collective-permute-done.9 = bf16[128,1536]{1,0:T(8,128)(2,1)S(1)} collective-permute-done((bf16[128,1536]{1,0:T(8,128)(2,1)}, bf16[128,1536]{1,0:T(8,128)(2,1)S(1)}, u32[]{:S(2)}, u32[]{:S(2)}) %collective-permute-start.9) | collective-permute-done | bytes 393248 | tf_op jit(solution)/shard_map/ppermute | solution.py:88
  148.4 4.8 collective-permute-done.14
  158.7 7.0 %collective-permute-done.15 = bf16[128,1536]{1,0:T(8,128)(2,1)S(1)} collective-permute-done((bf16[128,1536]{1,0:T(8,128)(2,1)S(1)}, bf16[128,1536]{1,0:T(8,128)(2,1)S(1)}, u32[]{:S(2)}, u32[]{:S(2)}) %collective-permute-start.15) | collective-permute-done | bytes 393248 | tf_op jit(solution)/shard_map/ppermute | solution.py:88
  177.0 4.2 collective-permute-done.17.refs_2_
  197.3 37.4 %experts.1 = (bf16[16,5,96,1536]{3,2,1,0:T(8,128)(2,1)}, bf16[5,384,512]{2,1,0:T(8,128)(2,1)}, bf16[5,384,1024]{2,1,0:T(8,128)(2,1)}, f32[5,384,128]{2,1,0:T(8,1...) custom-call(s32[5]{0:T(128)} %stack.41.info_ref, s32[5,8,128]{2,1,0:T(8,128)} %fusion.3.rank_ref, ...), custom_call_target="tpu_custom_call" | custom-call | tf_op jit(solution)/shard_map/experts/pallas_call | solution.py:589
  234.7 14.3 %input_grads.1 = (bf16[128,1664]{1,0:T(8,128)(2,1)}, bf16[128,1664]{1,0:T(8,128)(2,1)}, bf16[128,1664]{1,0:T(8,128)(2,1)}, bf16[128,1664]{1,0:T(8,128)(2,1)}, bf...) custom-call(s32[1]{0:T(128)} %bitcast.22.first_ref, ...), custom_call_target="tpu_custom_call" | custom-call | tf_op jit(solution)/shard_map/input_grads/pallas_call | solution.py:650
  250.3 4.2 collective-permute-start.24
  254.4 11.1 %mixture.1 = bf16[4,2,128,1536]{3,2,1,0:T(8,128)(2,1)} custom-call(s32[5]{0:T(128)} %stack.41.info_ref, s32[5,8,128]{2,1,0:T(8,128)} %fusion.3.rank_ref, bf16[5,384,512]{2,1,0:T(8,128)(2,1)} %get-tuple-element.144.act_ref, f32[5,384,128]{2,1,0:T(8,128)} %get-tuple-element.145.scale_ref, bf16[16,5,96,1536]{3,2,1,0:T(8,128)(2,1)} %bitcast.75), custom_call_target="tpu_custom_call" | custom-call | tf_op jit(solution)/shard_map/mixture/pallas_call | solution.py:684
  279.4 5.4 %collective-permute-done.29 = bf16[128,1664]{1,0:T(8,128)(2,1)S(1)} collective-permute-done((bf16[128,1664]{1,0:T(8,128)(2,1)S(1)}, bf16[128,1664]{1,0:T(8,128)(2,1)S(1)}, u32[]{:S(2)}, u32[]{:S(2)}) %collective-permute-start.29) | collective-permute-done | bytes 426016 | tf_op jit(solution)/shard_map/ppermute | solution.py:88
  297.2 4.0 collective-permute-start.34
  308.1 13.0 %collective-permute-done.34.refs_5_ = bf16[128,1536]{1,0:T(8,128)(2,1)S(1)} collective-permute-done((bf16[128,1536]{1,0:T(8,128)(2,1)S(1)}, bf16[128,1536]{1,0:T(8,128)(2,1)S(1)}, u32[]{:S(2)}, u32[]{:S(2)}) %collective-permute-start.34) | collective-permute-done | bytes 393248 | tf_op jit(solution)/shard_map/ppermute | solution.py:88
  321.8 5.0 %all-to-all-start.3 = ((bf16[4,2,128,1536]{3,2,1,0:T(8,128)(2,1)}), bf16[4,2,128,1536]{3,2,1,0:T(8,128)(2,1)}, u32[]{:S(2)}, u32[]{:S(2)}) async-start(bf16[4,2,128,1536]{3,2,1,0:T(8,128)(2,1)} %mixture.1), calls=%async_computation.3 | async-start | bytes 6291456 | tf_op jit(solution)/shard_map/all_to_all | solution.py:84
  326.8 21.7 %attend_back.1 = (bf16[3,64,1024]{2,1,0:T(8,128)(2,1)}, bf16[1024,128]{1,0:T(8,128)(2,1)}, bf16[1024,128]{1,0:T(8,128)(2,1)}, bf16[1024,128]{1,0:T(8,128)(2,1)}, bf16[1024,128]{1,0:T(8,128)(2,1)}) custom-call(s32[5]{0:T(128)} %stack.41.info_ref, s32[1,512]{1,0:T(1,128)} %bitcast.88, s32[512,1]{1,0:T(8,128)} %copy.63.pos_col, ...), custom_call_target="tpu_custom_call" | custom-call | tf_op jit(solution)/shard_map/attend_back/pallas_call | solution.py:346
  353.8 13.0 %collective-permute-start.38 = (bf16[1024,128]{1,0:T(8,128)(2,1)S(1)}, bf16[1024,128]{1,0:T(8,128)(2,1)S(1)}, u32[]{:S(2)}, u32[]{:S(2)}) collective-permute-start(bf16[1024,128]{1,0:T(8,128)(2,1)S(1)} %copy-done.56), channel_id=1, source_target_pairs={{8,0},{24,16},{9,1},{25,17},{10,2},{26,18},{11,3},{27,19},{12,4},{... | collective-permute-start | bytes 786440 | tf_op jit(solution)/shard_map/ppermute | solution.py:93
  370.6 26.7 %collective-permute-done.39.kv2 = bf16[1024,128]{1,0:T(8,128)(2,1)S(1)} collective-permute-done((bf16[1024,128]{1,0:T(8,128)(2,1)S(1)}, bf16[1024,128]{1,0:T(8,128)(2,1)S(1)}, u32[]{:S(2)}, u32[]{:S(2)}) %collective-permute-start.39) | collective-permute-done | bytes 262176 | tf_op jit(solution)/shard_map/ppermute | solution.py:93
  398.8 7.7 %turn_back.1 = (bf16[128,1536]{1,0:T(8,128)(2,1)}, bf16[128,1536]{1,0:T(8,128)(2,1)}, bf16[128,1536]{1,0:T(8,128)(2,1)}, bf16[128,1536]{1,0:T(8,128)(2,1)}, bf16...) custom-call(bf16[16,96,640]{2,1,0:T(8,128)(2,1)} %get-tuple-element., ...), custom_call_target="tpu_custom_call" | custom-call | tf_op jit(solution)/shard_map/turn_back/pallas_call | solution.py:398
  407.5 8.9 %weight_grads.1 = (bf16[2,4,96,640]{3,2,1,0:T(8,128)(2,1)}, bf16[2,4,96,640]{3,2,1,0:T(8,128)(2,1)}) custom-call(s32[5]{0:T(128)} %stack.41.info_ref, bf16[1024,1536]{1,0:T(8,128)(2,1)} %get-tuple-element.188.normed_ref, bf16[1024,320]{1,0:T(8,128)(2,1)} %get-tuple-element.189.mixed_ref, bf16[192,1024]{1,0:T(8,128)(2,1)} %get-tuple-element.190.heads_ref, ...), custom_call_target="tpu_custom_call" | custom-call | tf_op jit(solution)/shard_map/weight_grads/pallas_call | solution.py:442
  423.3 5.5 %all-to-all-start.4 = ((bf16[8,96,640]{2,1,0:T(8,128)(2,1)}), bf16[8,96,640]{2,1,0:T(8,128)(2,1)S(1)}, u32[]{:S(2)}, u32[]{:S(2)}) async-start(bf16[8,96,640]{2,1,0:T(8,128)(2,1)} %bitcast.28), calls=%async_computation.4 | async-start | bytes 1966080 | tf_op jit(solution)/shard_map/all_to_all | solution.py:84
  442.4 11.0 %all-to-all-done.4 = bf16[8,96,640]{2,1,0:T(8,128)(2,1)S(1)} async-done(((bf16[8,96,640]{2,1,0:T(8,128)(2,1)}), bf16[8,96,640]{2,1,0:T(8,128)(2,1)S(1)}, u32[]{:S(2)}, u32[]{:S(2)}) %all-to-all-start.4) | async-done | bytes 983072 | tf_op jit(solution)/shard_map/all_to_all | solution.py:84
  456.3 5.3 %all-to-all-start.5 = ((bf16[8,12,640]{2,1,0:T(8,128)(2,1)}), bf16[8,12,640]{2,1,0:T(8,128)(2,1)S(1)}, u32[]{:S(2)}, u32[]{:S(2)}) async-start(bf16[8,12,640]{2,1,0:T(8,128)(2,1)} %reshape.194), calls=%async_computation.5 | async-start | bytes 327680 | tf_op jit(solution)/shard_map/all_to_all | solution.py:84
  461.7 4.8 collective-permute-done.48.refs_3_
  470.9 6.3 %multiply_subtract_fusion = (f32[5,96,1024]{2,1,0:T(8,128)}, f32[5,96,1024]{2,1,0:T(8,128)}, f32[5,96,1024]{2,1,0:T(8,128)}) fusion(f32[5,96,1024]{2,1,0:T(8,128)S(1)} %copy-done.1, bf16[5,96,1536]{2,1,0:T(8,128)(2,1)} %bitcast.79, f32[5,96,1024]{2,1,0:T(8,128)} %param.38, f32[5,96,1024]{2,1,0:T(8,128)} %param.39), kind=kLoop, calls=%fused_computation.7 | loop fusion | flops 7864320 | bytes 12779520 | tf_op jit(solution)/shard_map/sub | solution.py:77
  (290 shorter events, 152.6 us)
Async XLA Ops:
  7.2 190.0 %all-gather.2.cloned.1.call-start = ((), (), s32[]{:S(2)}) async-start(), calls=%async_computation.7 | async-start | bytes 25067520 | tf_op jit(solution)/shard_map/all_gather | solution.py:745
  25.6 43.8 %all-to-all-start.1 = ((bf16[8,96,640]{2,1,0:T(8,128)(2,1)}), bf16[8,96,640]{2,1,0:T(8,128)(2,1)S(1)}, u32[]{:S(2)}, u32[]{:S(2)}) async-start(bf16[8,96,640]{2,1,0:T(8,128)(2,1)} %broadcast_in_dim.72), calls=%async_computation.1 | async-start | bytes 1966080 | tf_op jit(solution)/shard_map/all_to_all | solution.py:84
  33.7 29.8 %collective-permute-start.2 = (bf16[2,128,1536]{2,1,0:T(8,128)(2,1)S(1)}, bf16[2,128,1536]{2,1,0:T(8,128)(2,1)S(1)}, u32[]{:S(2)}, u32[]{:S(2)}) collective-permute-start(bf16[2,128,1536]{2,1,0:T(8,128)(2,1)S(1)} %pad_maximum_fusion.2.refs_0_), channel_id=1, source_target_pairs={{0,2},{2,0},{4,6},{6,4},{1,3},{3,1},{5,7},{7,5},{8,10},{10,8},{12,... | collective-permute-start | bytes 2359304 | tf_op jit(solution)/shard_map/ppermute | solution.py:88
  34.9 33.0 %collective-permute-start.3 = (bf16[2,128,1536]{2,1,0:T(8,128)(2,1)S(1)}, bf16[2,128,1536]{2,1,0:T(8,128)(2,1)S(1)}, u32[]{:S(2)}, u32[]{:S(2)}) collective-permute-start(bf16[2,128,1536]{2,1,0:T(8,128)(2,1)S(1)} %pad_maximum_fusion.2.refs_0_), channel_id=1, source_target_pairs={{0,4},{2,6},{4,0},{6,2},{1,5},{3,7},{5,1},{7,3},{8,12},{10,14},{12... | collective-permute-start | bytes 2359304 | tf_op jit(solution)/shard_map/ppermute | solution.py:88
  35.7 33.8 %collective-permute-start.4 = (bf16[2,128,1536]{2,1,0:T(8,128)(2,1)S(1)}, bf16[2,128,1536]{2,1,0:T(8,128)(2,1)}, u32[]{:S(2)}, u32[]{:S(2)}) collective-permute-start(bf16[2,128,1536]{2,1,0:T(8,128)(2,1)S(1)} %pad_maximum_fusion.2.refs_0_), channel_id=1, source_target_pairs={{0,6},{2,4},{4,2},{6,0},{1,7},{3,5},{5,3},{7,1},{8,14},{10,12},{12... | collective-permute-start | bytes 2359304 | tf_op jit(solution)/shard_map/ppermute | solution.py:88
  39.1 24.4 %collective-permute-start.1 = (bf16[128,1664]{1,0:T(8,128)(2,1)S(1)}, bf16[128,1664]{1,0:T(8,128)(2,1)S(1)}, u32[]{:S(2)}, u32[]{:S(2)}) collective-permute-start(bf16[128,1664]{1,0:T(8,128)(2,1)S(1)} %get-tuple-element.119), channel_id=1, source_target_pairs={{0,1},{1,0},{2,3},{3,2},{4,5},{5,4},{6,7},{7,6},{8,9},{9,8},{10,11... | collective-permute-start | bytes 1277960 | tf_op jit(solution)/shard_map/ppermute | solution.py:88
  80.6 59.5 %all-to-all-start.2 = ((bf16[4,2,128,1664]{3,2,1,0:T(8,128)(2,1)}), bf16[4,2,128,1664]{3,2,1,0:T(8,128)(2,1)S(1)}, u32[]{:S(2)}, u32[]{:S(2)}) async-start(bf16[4,2,128,1664]{3,2,1,0:T(8,128)(2,1)} %broadcast_in_dim.75), calls=%async_computation.2 | async-start | bytes 6815744 | tf_op jit(solution)/shard_map/all_to_all | solution.py:84
  89.3 381.6 %reduce-scatter.2.cloned.1.call-start = ((), (), s32[]{:S(2)}) async-start(), calls=%async_computation.8 | async-start | bytes 25067520 | tf_op jit(solution)/shard_map/reduce_scatter | solution.py:785
  89.3 15.3 %collective-permute-start.6 = (bf16[128,1024]{1,0:T(8,128)(2,1)}, bf16[128,1024]{1,0:T(8,128)(2,1)}, u32[]{:S(2)}, u32[]{:S(2)}) collective-permute-start(bf16[128,1024]{1,0:T(8,128)(2,1)} %get-tuple-element.124.kv0), channel_id=1, source_target_pairs={{0,8},{16,24},{1,9},{17,25},{2,10},{18,26},{3,11},{19,27},{4,12},{... | collective-permute-start | bytes 786440 | tf_op jit(solution)/shard_map/ppermute | solution.py:93
  95.3 17.6 %collective-permute-start.8 = (bf16[128,1024]{1,0:T(8,128)(2,1)}, bf16[128,1024]{1,0:T(8,128)(2,1)}, u32[]{:S(2)}, u32[]{:S(2)}) collective-permute-start(bf16[128,1024]{1,0:T(8,128)(2,1)} %get-tuple-element.124.kv0), channel_id=1, source_target_pairs={{0,24},{8,16},{1,25},{9,17},{2,26},{10,18},{3,27},{11,19},{4,28},{... | collective-permute-start | bytes 786440 | tf_op jit(solution)/shard_map/ppermute | solution.py:93
  128.3 17.4 %collective-permute-start.11 = (bf16[128,1536]{1,0:T(8,128)(2,1)}, bf16[128,1536]{1,0:T(8,128)(2,1)}, u32[]{:S(2)}, u32[]{:S(2)}) collective-permute-start(bf16[128,1536]{1,0:T(8,128)(2,1)} %get-tuple-element.132), channel_id=1, source_target_pairs={{0,6},{2,4},{4,2},{6,0},{1,7},{3,5},{5,3},{7,1},{8,14},{10,12},{12... | collective-permute-start | bytes 1179656 | tf_op jit(solution)/shard_map/ppermute | solution.py:88
  172.1 14.4 %collective-permute-start.19 = (bf16[128,1536]{1,0:T(8,128)(2,1)S(1)}, bf16[128,1536]{1,0:T(8,128)(2,1)S(1)}, u32[]{:S(2)}, u32[]{:S(2)}) collective-permute-start(bf16[128,1536]{1,0:T(8,128)(2,1)S(1)} %multiply_convert_fusion.1.refs_0_), channel_id=1, source_target_pairs={{0,4},{2,6},{4,0},{6,2},{1,5},{3,7},{5,1},{7,3},{8,12},{10,14},{12... | collective-permute-start | bytes 1179656 | tf_op jit(solution)/shard_map/ppermute | solution.py:88
  172.2 16.5 %collective-permute-start.21 = (bf16[128,1536]{1,0:T(8,128)(2,1)S(1)}, bf16[128,1536]{1,0:T(8,128)(2,1)S(1)}, u32[]{:S(2)}, u32[]{:S(2)}) collective-permute-start(bf16[128,1536]{1,0:T(8,128)(2,1)S(1)} %multiply_convert_fusion.1.refs_0_), channel_id=1, source_target_pairs={{0,6},{2,4},{4,2},{6,0},{1,7},{3,5},{5,3},{7,1},{8,14},{10,12},{12... | collective-permute-start | bytes 1179656 | tf_op jit(solution)/shard_map/ppermute | solution.py:88
  174.6 16.5 %collective-permute-start.18 = (bf16[128,1536]{1,0:T(8,128)(2,1)S(1)}, bf16[128,1536]{1,0:T(8,128)(2,1)}, u32[]{:S(2)}, u32[]{:S(2)}) collective-permute-start(bf16[128,1536]{1,0:T(8,128)(2,1)S(1)} %collective-permute-done.16.refs_1_), channel_id=1, source_target_pairs={{0,2},{2,0},{4,6},{6,4},{1,3},{3,1},{5,7},{7,5},{8,10},{10,8},{12,... | collective-permute-start | bytes 1179656 | tf_op jit(solution)/shard_map/ppermute | solution.py:88
  176.9 18.1 %collective-permute-start.20 = (bf16[128,1536]{1,0:T(8,128)(2,1)S(1)}, bf16[128,1536]{1,0:T(8,128)(2,1)}, u32[]{:S(2)}, u32[]{:S(2)}) collective-permute-start(bf16[128,1536]{1,0:T(8,128)(2,1)S(1)} %collective-permute-done.16.refs_1_), channel_id=1, source_target_pairs={{0,4},{2,6},{4,0},{6,2},{1,5},{3,7},{5,1},{7,3},{8,12},{10,14},{12... | collective-permute-start | bytes 1179656 | tf_op jit(solution)/shard_map/ppermute | solution.py:88
  181.2 16.0 %collective-permute-start.22 = (bf16[128,1536]{1,0:T(8,128)(2,1)S(1)}, bf16[128,1536]{1,0:T(8,128)(2,1)}, u32[]{:S(2)}, u32[]{:S(2)}) collective-permute-start(bf16[128,1536]{1,0:T(8,128)(2,1)S(1)} %collective-permute-done.16.refs_1_), channel_id=1, source_target_pairs={{0,6},{2,4},{4,2},{6,0},{1,7},{3,5},{5,3},{7,1},{8,14},{10,12},{12... | collective-permute-start | bytes 1179656 | tf_op jit(solution)/shard_map/ppermute | solution.py:88
  248.9 16.6 %collective-permute-start.23 = (bf16[128,1664]{1,0:T(8,128)(2,1)}, bf16[128,1664]{1,0:T(8,128)(2,1)S(1)}, u32[]{:S(2)}, u32[]{:S(2)}) collective-permute-start(bf16[128,1664]{1,0:T(8,128)(2,1)} %get-tuple-element.148), channel_id=1, source_target_pairs={{0,6},{2,4},{4,2},{6,0},{1,7},{3,5},{5,3},{7,1},{8,14},{10,12},{12... | collective-permute-start | bytes 1277960 | tf_op jit(solution)/shard_map/ppermute | solution.py:88
  250.3 15.3 %collective-permute-start.24 = (bf16[128,1664]{1,0:T(8,128)(2,1)}, bf16[128,1664]{1,0:T(8,128)(2,1)S(1)}, u32[]{:S(2)}, u32[]{:S(2)}) collective-permute-start(bf16[128,1664]{1,0:T(8,128)(2,1)} %get-tuple-element.149), channel_id=1, source_target_pairs={{0,2},{2,0},{4,6},{6,4},{1,3},{3,1},{5,7},{7,5},{8,10},{10,8},{12,... | collective-permute-start | bytes 1277960 | tf_op jit(solution)/shard_map/ppermute | solution.py:88
  290.3 16.0 %collective-permute-start.33 = (bf16[128,1536]{1,0:T(8,128)(2,1)S(1)}, bf16[128,1536]{1,0:T(8,128)(2,1)S(1)}, u32[]{:S(2)}, u32[]{:S(2)}) collective-permute-start(bf16[128,1536]{1,0:T(8,128)(2,1)S(1)} %get-tuple-element.159.refs_0_), channel_id=1, source_target_pairs={{0,4},{2,6},{4,0},{6,2},{1,5},{3,7},{5,1},{7,3},{8,12},{10,14},{12... | collective-permute-start | bytes 1179656 | tf_op jit(solution)/shard_map/ppermute | solution.py:88
  297.2 23.8 %collective-permute-start.34 = (bf16[128,1536]{1,0:T(8,128)(2,1)S(1)}, bf16[128,1536]{1,0:T(8,128)(2,1)S(1)}, u32[]{:S(2)}, u32[]{:S(2)}) collective-permute-start(bf16[128,1536]{1,0:T(8,128)(2,1)S(1)} %collective-permute-done.30.refs_1_), channel_id=1, source_target_pairs={{0,4},{2,6},{4,0},{6,2},{1,5},{3,7},{5,1},{7,3},{8,12},{10,14},{12... | collective-permute-start | bytes 1179656 | tf_op jit(solution)/shard_map/ppermute | solution.py:88
  301.2 20.6 %collective-permute-start.36 = (bf16[128,1536]{1,0:T(8,128)(2,1)S(1)}, bf16[128,1536]{1,0:T(8,128)(2,1)}, u32[]{:S(2)}, u32[]{:S(2)}) collective-permute-start(bf16[128,1536]{1,0:T(8,128)(2,1)S(1)} %collective-permute-done.30.refs_1_), channel_id=1, source_target_pairs={{0,6},{2,4},{4,2},{6,0},{1,7},{3,5},{5,3},{7,1},{8,14},{10,12},{12... | collective-permute-start | bytes 1179656 | tf_op jit(solution)/shard_map/ppermute | solution.py:88
  321.8 27.7 %all-to-all-start.3 = ((bf16[4,2,128,1536]{3,2,1,0:T(8,128)(2,1)}), bf16[4,2,128,1536]{3,2,1,0:T(8,128)(2,1)}, u32[]{:S(2)}, u32[]{:S(2)}) async-start(bf16[4,2,128,1536]{3,2,1,0:T(8,128)(2,1)} %mixture.1), calls=%async_computation.3 | async-start | bytes 6291456 | tf_op jit(solution)/shard_map/all_to_all | solution.py:84
  352.1 54.4 %collective-permute-start.37 = (bf16[128,1536]{1,0:T(8,128)(2,1)S(1)}, bf16[128,1536]{1,0:T(8,128)(2,1)S(1)}, u32[]{:S(2)}, u32[]{:S(2)}) collective-permute-start(bf16[128,1536]{1,0:T(8,128)(2,1)S(1)} %fusion.11), channel_id=1, source_target_pairs={{0,1},{1,0},{2,3},{3,2},{4,5},{5,4},{6,7},{7,6},{8,9},{9,8},{10,11... | collective-permute-start | bytes 1179656 | tf_op jit(solution)/shard_map/ppermute | solution.py:88
  353.8 16.8 %collective-permute-start.38 = (bf16[1024,128]{1,0:T(8,128)(2,1)S(1)}, bf16[1024,128]{1,0:T(8,128)(2,1)S(1)}, u32[]{:S(2)}, u32[]{:S(2)}) collective-permute-start(bf16[1024,128]{1,0:T(8,128)(2,1)S(1)} %copy-done.56), channel_id=1, source_target_pairs={{8,0},{24,16},{9,1},{25,17},{10,2},{26,18},{11,3},{27,19},{12,4},{... | collective-permute-start | bytes 786440 | tf_op jit(solution)/shard_map/ppermute | solution.py:93
  366.8 30.6 %collective-permute-start.39 = (bf16[1024,128]{1,0:T(8,128)(2,1)S(1)}, bf16[1024,128]{1,0:T(8,128)(2,1)S(1)}, u32[]{:S(2)}, u32[]{:S(2)}) collective-permute-start(bf16[1024,128]{1,0:T(8,128)(2,1)S(1)} %copy-done.55), channel_id=1, source_target_pairs={{16,0},{24,8},{17,1},{25,9},{18,2},{26,10},{19,3},{27,11},{20,4},{... | collective-permute-start | bytes 786440 | tf_op jit(solution)/shard_map/ppermute | solution.py:93
  368.1 29.3 %collective-permute-start.40 = (bf16[1024,128]{1,0:T(8,128)(2,1)S(1)}, bf16[1024,128]{1,0:T(8,128)(2,1)S(1)}, u32[]{:S(2)}, u32[]{:S(2)}) collective-permute-start(bf16[1024,128]{1,0:T(8,128)(2,1)S(1)} %copy-done.54), channel_id=1, source_target_pairs={{16,8},{24,0},{17,9},{25,1},{18,10},{26,2},{19,11},{27,3},{20,12},... | collective-permute-start | bytes 786440 | tf_op jit(solution)/shard_map/ppermute | solution.py:93
  417.3 15.5 %collective-permute-start.41 = (bf16[128,1536]{1,0:T(8,128)(2,1)}, bf16[128,1536]{1,0:T(8,128)(2,1)S(1)}, u32[]{:S(2)}, u32[]{:S(2)}) collective-permute-start(bf16[128,1536]{1,0:T(8,128)(2,1)} %get-tuple-element.181), channel_id=1, source_target_pairs={{0,2},{2,0},{4,6},{6,4},{1,3},{3,1},{5,7},{7,5},{8,10},{10,8},{12,... | collective-permute-start | bytes 1179656 | tf_op jit(solution)/shard_map/ppermute | solution.py:88
  418.3 18.4 %collective-permute-start.42 = (bf16[128,1536]{1,0:T(8,128)(2,1)}, bf16[128,1536]{1,0:T(8,128)(2,1)S(1)}, u32[]{:S(2)}, u32[]{:S(2)}) collective-permute-start(bf16[128,1536]{1,0:T(8,128)(2,1)} %get-tuple-element.182), channel_id=1, source_target_pairs={{0,6},{2,4},{4,2},{6,0},{1,7},{3,5},{5,3},{7,1},{8,14},{10,12},{12... | collective-permute-start | bytes 1179656 | tf_op jit(solution)/shard_map/ppermute | solution.py:88
  423.3 30.1 %all-to-all-start.4 = ((bf16[8,96,640]{2,1,0:T(8,128)(2,1)}), bf16[8,96,640]{2,1,0:T(8,128)(2,1)S(1)}, u32[]{:S(2)}, u32[]{:S(2)}) async-start(bf16[8,96,640]{2,1,0:T(8,128)(2,1)} %bitcast.28), calls=%async_computation.4 | async-start | bytes 1966080 | tf_op jit(solution)/shard_map/all_to_all | solution.py:84
  436.7 25.0 %collective-permute-start.43 = (bf16[128,1536]{1,0:T(8,128)(2,1)}, bf16[128,1536]{1,0:T(8,128)(2,1)S(1)}, u32[]{:S(2)}, u32[]{:S(2)}) collective-permute-start(bf16[128,1536]{1,0:T(8,128)(2,1)} %get-tuple-element.183), channel_id=1, source_target_pairs={{0,2},{2,0},{4,6},{6,4},{1,3},{3,1},{5,7},{7,5},{8,10},{10,8},{12,... | collective-permute-start | bytes 1179656 | tf_op jit(solution)/shard_map/ppermute | solution.py:88
  439.5 22.2 %collective-permute-start.44 = (bf16[128,1536]{1,0:T(8,128)(2,1)}, bf16[128,1536]{1,0:T(8,128)(2,1)S(1)}, u32[]{:S(2)}, u32[]{:S(2)}) collective-permute-start(bf16[128,1536]{1,0:T(8,128)(2,1)} %add_convert_fusion.6), channel_id=1, source_target_pairs={{0,6},{2,4},{4,2},{6,0},{1,7},{3,5},{5,3},{7,1},{8,14},{10,12},{12... | collective-permute-start | bytes 1179656 | tf_op jit(solution)/shard_map/ppermute | solution.py:88
  456.3 24.1 %all-to-all-start.5 = ((bf16[8,12,640]{2,1,0:T(8,128)(2,1)}), bf16[8,12,640]{2,1,0:T(8,128)(2,1)S(1)}, u32[]{:S(2)}, u32[]{:S(2)}) async-start(bf16[8,12,640]{2,1,0:T(8,128)(2,1)} %reshape.194), calls=%async_computation.5 | async-start | bytes 327680 | tf_op jit(solution)/shard_map/all_to_all | solution.py:84
  (82 other events, 830.5 us)
Sparse Core Ops, SparseCore 0:
  11.6 159.6 all-gather.1
  234.8 217.3 reduce-scatter.1
